TPU v7x, 128 devices: a whole 4x4x4 slice. The times are simulated.
128 devices in a mesh: section: 2 (over core), dp: 16 (over y, x), expert: 4 (over z).
Axes of the slice: x: 4, y: 4, z: 4, core: 2. Of those that a mesh axis runs over, the one named last changes fastest.
Arguments:
- inputs: bfloat16 [2, 1024, 3072], P(None, 'dp'), may hold values from -6 to 6
- cotangent: bfloat16 [2, 1024, 3072], P(None, 'dp'), may hold values from -1.5 to 1.5
- gain: bfloat16 [2, 3072], P('section'), may hold values from 0.099609375 to 1.8984375
- w_up: bfloat16 [2, 16, 5376, 3072], P('section', 'dp', 'expert'), may hold values from -0.109375 to 0.109375
- w_down: bfloat16 [2, 16, 5376, 3072], P('section', 'dp', 'expert'), may hold values from -0.078125 to 0.078125
- expert_ids: int32 [2, 2, 1024, 6], P('section', None, 'dp'), may hold values from 0 to 15, all different within a row; in each aligned block of 64 rows (0 to 63, 64 to 127, ..., all dimensions but the last counted through in order) at most 25 rows name the same one
- expert_counts: int32 [2, 2, 1024], P('section', None, 'dp'), may hold values from 5 to 6
- combine_fixed: int32 [2, 2, 1024, 6], P('section', None, 'dp'), may hold values from 1024 to 4096
Outputs:
- outputs: bfloat16 [2, 2, 1024, 3072], P('section', None, 'dp')
- input_grads: bfloat16 [2, 2, 1024, 3072], P('section', None, 'dp')
- grad_gain: float32 [2, 3072], P('section', 'dp')
Inputs may be any that keep to these rules, and one draw needn't show every extreme that they name: `expert_ids`: each token's 6 slots name different experts. In the 64 tokens of one index of dp in one microbatch (aligned blocks of 64 rows), no expert is named by more than 25 slots, used or not, and in some blocks one expert is named by exactly 25. Only the first expert_counts slots of a token are used.
All inputs are finite; a program needn't handle non-finite values.
Results may differ from a plain program's by a relative error of at most 0.013.
Values may be sent and summed in bfloat16 or wider, within the bound.
No kernel may reach another device: no remote copies, remote signals or barrier semaphores. Data moves between devices by JAX's collectives and lax.ppermute only.
A program may use at most 128 MiB of HBM per device.

v0:
```python
from functools import partial

import jax
import jax.numpy as jnp
from jax import lax
from jax.sharding import PartitionSpec as P

EPSILON = 1e-05
PRECISE = lax.Precision.HIGHEST


def passed_along(x, axis, by):
    devices = lax.axis_size(axis)
    pairs = [(i, i + by) for i in range(devices) if 0 <= i + by < devices]
    return lax.ppermute(x, axis, pairs)


def slot_tables(expert_index, counts, fixed, experts, capacity):
    row_count, top_count = expert_index.shape
    is_live = jnp.arange(top_count)[None, :] < counts[:, None]
    shares = jnp.where(is_live, fixed.astype(jnp.float32), 0.0)
    weights = shares / jnp.sum(shares, axis=1, keepdims=True)
    flattened = expert_index.reshape(-1)
    onehot = (flattened[:, None] == jnp.arange(experts)[None, :]).astype(jnp.int32)
    before = jnp.cumsum(onehot, axis=0) - onehot
    position = jnp.sum(before * onehot, axis=1)
    target = flattened * capacity + position
    placing = (target[:, None] == jnp.arange(experts * capacity)[None, :]).astype(jnp.float32)
    owners = jnp.arange(row_count * top_count) // top_count
    token_hot = (owners[:, None] == jnp.arange(row_count)[None, :]).astype(jnp.float32)
    selector = jnp.dot(placing.T, token_hot, precision=PRECISE)
    slot_weights = jnp.dot(placing.T, weights.reshape(-1), precision=PRECISE)
    return (selector, slot_weights)


def pick_row(table, index):
    return lax.dynamic_index_in_dim(table, index, 0, keepdims=False)


def keep_at(stash, value, index, active):
    previous = lax.dynamic_index_in_dim(stash, index, 0, keepdims=False)
    return lax.dynamic_update_index_in_dim(stash, jnp.where(active, value, previous), index, 0)


def norm_rows(current):
    state_f = current.astype(jnp.float32)
    inverse_rms = lax.rsqrt(jnp.mean(state_f * state_f, axis=-1, keepdims=True) + EPSILON)
    return (state_f, inverse_rms)


def shards(inputs, cotangent, gain, w_up, w_down, expert_ids, expert_counts, combine_fixed):
    sections = lax.axis_size("section")
    section_now = lax.axis_index("section")
    owners = lax.axis_size("dp")
    micro_count, row_count, model_width = inputs.shape
    top_count = expert_ids.shape[3]
    capacity = min(row_count, row_count * top_count // owners + 1)
    local_rows = owners * capacity
    up_rows = w_up[0, 0]
    down_rows = w_down[0, 0]
    hidden = up_rows.shape[0]
    gain_row = gain[0].astype(jnp.float32)
    table_fn = jax.vmap(partial(slot_tables, experts=owners, capacity=capacity))
    selectors, slot_weights = table_fn(expert_ids[0], expert_counts[0], combine_fixed[0])

    def dispatch(current, selector):
        state_f, inverse_rms = norm_rows(current)
        normed = (state_f * inverse_rms * gain_row).astype(jnp.bfloat16)
        outgoing = jnp.dot(
            selector.astype(jnp.bfloat16), normed, preferred_element_type=jnp.float32
        )
        return outgoing.astype(jnp.bfloat16).reshape(owners, capacity, model_width)

    def expert_forward(slot_rows):
        pre_act = lax.dot_general(
            slot_rows, up_rows, (((1,), (1,)), ((), ())), preferred_element_type=jnp.float32
        )
        activated = jax.nn.silu(pre_act).astype(jnp.bfloat16)
        part = jnp.dot(activated, down_rows, preferred_element_type=jnp.float32).astype(
            jnp.bfloat16
        )
        return (pre_act, part)

    def forward_spare(slot_rows):
        return (
            jnp.zeros((local_rows, hidden), jnp.float32),
            jnp.zeros((local_rows, model_width), jnp.bfloat16),
        )

    def expert_backward(d_rows, pre_act):
        d_act = lax.dot_general(
            d_rows, down_rows, (((1,), (1,)), ((), ())), preferred_element_type=jnp.float32
        )
        logistic = jax.nn.sigmoid(pre_act)
        d_pre = (d_act * logistic * (1.0 + pre_act * (1.0 - logistic))).astype(jnp.bfloat16)
        return jnp.dot(d_pre, up_rows, preferred_element_type=jnp.float32).astype(jnp.bfloat16)

    def backward_spare(d_rows, pre_act):
        return jnp.zeros((local_rows, model_width), jnp.bfloat16)

    def home_rows(returned, selector):
        flat = returned.reshape(local_rows, model_width).astype(jnp.float32)
        return jnp.einsum("sr,sc->rc", selector, flat, precision=PRECISE)

    def weighted_home(returned, selector, weights):
        flat = returned.reshape(local_rows, model_width).astype(jnp.float32) * weights[:, None]
        return jnp.einsum("sr,sc->rc", selector, flat, precision=PRECISE)

    def spread_back(upstream, selector, weights):
        spread = (
            jnp.dot(selector, upstream.astype(jnp.float32), precision=PRECISE) * weights[:, None]
        )
        return spread.astype(jnp.bfloat16).reshape(owners, capacity, model_width)

    def finish(current, upstream, d_norm):
        state_f, inverse_rms = norm_rows(current)
        scaled = state_f * inverse_rms
        d_scaled = d_norm * gain_row
        d_input = inverse_rms * (
            d_scaled - scaled * jnp.mean(d_scaled * scaled, axis=-1, keepdims=True)
        )
        return (
            (upstream.astype(jnp.float32) + d_input).astype(jnp.bfloat16),
            jnp.sum(d_norm * scaled, axis=0),
        )

    def forward_front(incoming, index_now):
        active = (index_now >= 0) & (index_now < micro_count)
        clipped = jnp.clip(index_now, 0, micro_count - 1)
        current = jnp.where(section_now == 0, pick_row(inputs, clipped), incoming)
        return (active, clipped, current, dispatch(current, pick_row(selectors, clipped)))

    def backward_front(incoming, index_now):
        active = (index_now >= 0) & (index_now < micro_count)
        clipped = jnp.clip(index_now, 0, micro_count - 1)
        upstream = jnp.where(section_now == sections - 1, pick_row(cotangent, clipped), incoming)
        outgoing = spread_back(
            upstream, pick_row(selectors, clipped), pick_row(slot_weights, clipped)
        )
        return (active, clipped, upstream, outgoing)

    zeros_rows = jnp.zeros((row_count, model_width), jnp.bfloat16)
    layer_out = jnp.zeros((micro_count, row_count, model_width), jnp.bfloat16)
    layer_grad = jnp.zeros_like(layer_out)
    keep_x = jnp.zeros_like(layer_out)
    keep_pre = jnp.zeros((micro_count, local_rows, hidden), jnp.float32)
    gain_acc = jnp.zeros((model_width,), jnp.float32)

    def forward_tick(moment, state_now):
        last_out, outs_now, stash_x, stash_pre = state_now
        from_below = passed_along(last_out, "section", 1)
        active, clipped, current, outgoing = forward_front(from_below, moment - section_now)
        arrived = lax.all_to_all(outgoing, "dp", split_axis=0, concat_axis=0, tiled=True)
        pre_act, part = lax.cond(
            active, expert_forward, forward_spare, arrived.reshape(local_rows, model_width)
        )
        returned = lax.all_to_all(
            part.reshape(owners, capacity, model_width),
            "dp",
            split_axis=0,
            concat_axis=0,
            tiled=True,
        )
        mixture = lax.psum(
            weighted_home(returned, pick_row(selectors, clipped), pick_row(slot_weights, clipped)),
            "expert",
        )
        following = (current.astype(jnp.float32) + mixture).astype(jnp.bfloat16)
        return (
            following,
            keep_at(outs_now, following, clipped, active),
            keep_at(stash_x, current, clipped, active),
            keep_at(stash_pre, pre_act, clipped, active),
        )

    forward_state = (zeros_rows, layer_out, keep_x, keep_pre)
    forward_state = lax.fori_loop(0, micro_count + sections - 1, forward_tick, forward_state)
    layer_out, keep_x, keep_pre = (forward_state[1], forward_state[2], forward_state[3])

    def backward_tick(moment, state_now):
        last_grad, grads_now, gain_now = state_now
        from_above = passed_along(last_grad, "section", -1)
        active, clipped, upstream, outgoing = backward_front(
            from_above, moment - (sections - 1 - section_now)
        )
        arrived = lax.all_to_all(outgoing, "dp", split_axis=0, concat_axis=0, tiled=True)
        d_part = lax.cond(
            active,
            expert_backward,
            backward_spare,
            arrived.reshape(local_rows, model_width),
            pick_row(keep_pre, clipped),
        )
        returned = lax.all_to_all(
            d_part.reshape(owners, capacity, model_width),
            "dp",
            split_axis=0,
            concat_axis=0,
            tiled=True,
        )
        d_norm = lax.psum(home_rows(returned, pick_row(selectors, clipped)), "expert")
        preceding, gain_term = finish(pick_row(keep_x, clipped), upstream, d_norm)
        return (
            preceding,
            keep_at(grads_now, preceding, clipped, active),
            gain_now + jnp.where(active, gain_term, 0.0),
        )

    backward_state = (zeros_rows, layer_grad, gain_acc)
    backward_state = lax.fori_loop(0, micro_count + sections - 1, backward_tick, backward_state)
    layer_grad, gain_acc = (backward_state[1], backward_state[2])
    grad_gain = lax.psum_scatter(gain_acc, "dp", scatter_dimension=0, tiled=True)
    return (layer_out[None], layer_grad[None], grad_gain[None])


def solution(mesh):
    return jax.shard_map(
        shards,
        mesh=mesh,
        in_specs=(
            P(None, "dp", None),
            P(None, "dp", None),
            P("section", None),
            P("section", "dp", "expert", None),
            P("section", "dp", "expert", None),
            P("section", None, "dp", None),
            P("section", None, "dp"),
            P("section", None, "dp", None),
        ),
        out_specs=(
            P("section", None, "dp", None),
            P("section", None, "dp", None),
            P("section", "dp"),
        ),
        check_vma=False,
    )
```

profile of v0, /device:TPU:1, one launch (start us, length us, event | category | flops | bytes accessed | tf_op | source)
XLA Modules:
  0.0 1164.5 jit_solution(13343957224108623872)
XLA Ops:
  20.8 560.8 %while.41 = (s32[]{:T(128)}, bf16[64,3072]{1,0:T(8,128)(2,1)S(1)}, bf16[2,64,3072]{2,1,0:T(8,128)(2,1)}, bf16[2,64,3072]{2,1,0:T(8,128)(2,1)}, f32[2,400,1344]{2...) while((s32[]{:T(128)}, bf16[64,3072]{1,0:T(8,128)(2,1)S(1)}, ...), condition=%wide.region_9.10_spmd.clone, body=%wide.region_4.9_spmd.clone.sunk | while | flops 7718123520 | bytes 142989104 | solution.py:177
  30.8 7.3 all-to-all-start
  38.1 48.1 %all-to-all-done = bf16[16,25,3072]{2,1,0:T(8,128)(2,1)S(1)} async-done(((bf16[16,25,3072]{2,1,0:T(8,128)(2,1)}), bf16[16,25,3072]{2,1,0:T(8,128)(2,1)S(1)}, u32[]{:S(2)}, u32[]{:S(2)}) %all-to-all-start) | async-done | bytes 2457632 | tf_op jit(solution)/shard_map/while/body/eval_jaxpr/all_to_all | solution.py:153
  100.1 27.5 %all-to-all-done.1 = bf16[16,25,3072]{2,1,0:T(8,128)(2,1)S(1)} async-done(((bf16[16,25,3072]{2,1,0:T(8,128)(2,1)}), bf16[16,25,3072]{2,1,0:T(8,128)(2,1)S(1)}, u32[]{:S(2)}, u32[]{:S(2)}) %all-to-all-start.1) | async-done | bytes 2457632 | tf_op jit(solution)/shard_map/while/body/eval_jaxpr/all_to_all | solution.py:157
  146.4 55.4 %all-reduce.4.cloned.1.call-done = f32[64,3072]{1,0:T(8,128)} async-done(((f32[64,3072]{1,0:T(8,128)}), f32[64,3072]{1,0:T(8,128)}) %all-reduce.4.cloned.1.call-update) | async-done | bytes 786448 | tf_op jit(solution)/shard_map/while/body/eval_jaxpr/psum | solution.py:164
  221.3 48.1 %all-to-all-done = bf16[16,25,3072]{2,1,0:T(8,128)(2,1)S(1)} async-done(((bf16[16,25,3072]{2,1,0:T(8,128)(2,1)}), bf16[16,25,3072]{2,1,0:T(8,128)(2,1)S(1)}, u32[]{:S(2)}, u32[]{:S(2)}) %all-to-all-start) | async-done | bytes 2457632 | tf_op jit(solution)/shard_map/while/body/eval_jaxpr/all_to_all | solution.py:153
  269.4 18.5 %conditional.6 = (f32[400,1344]{1,0:T(8,128)}, bf16[400,3072]{1,0:T(8,128)(2,1)}) conditional(s32[]{:T(128)} %convert_element_type.221, () %tuple.113, (bf16[16,25,3072]{2,1,0:T(8,128)(2,1)S(1)}, bf16[1344,3072]{1,0:T(8,128)(2,1)}, bf16[1344,3072]{1,0:T(8,128)(2,1)}) %tuple.114), branch_computations={%region_6.6_spmd, %region_7.7_spmd} | conditional | flops 6609945600 | bytes 63676460 | solution.py:154
  271.3 9.6 fusion.60
  280.9 7.0 convolution_convert_fusion
  298.7 41.8 %all-to-all-done.1 = bf16[16,25,3072]{2,1,0:T(8,128)(2,1)S(1)} async-done(((bf16[16,25,3072]{2,1,0:T(8,128)(2,1)}), bf16[16,25,3072]{2,1,0:T(8,128)(2,1)S(1)}, u32[]{:S(2)}, u32[]{:S(2)}) %all-to-all-start.1) | async-done | bytes 2457632 | tf_op jit(solution)/shard_map/while/body/eval_jaxpr/all_to_all | solution.py:157
  360.9 36.8 %all-reduce.4.cloned.1.call-done = f32[64,3072]{1,0:T(8,128)} async-done(((f32[64,3072]{1,0:T(8,128)}), f32[64,3072]{1,0:T(8,128)}) %all-reduce.4.cloned.1.call-update) | async-done | bytes 786448 | tf_op jit(solution)/shard_map/while/body/eval_jaxpr/psum | solution.py:164
  417.2 48.1 %all-to-all-done = bf16[16,25,3072]{2,1,0:T(8,128)(2,1)S(1)} async-done(((bf16[16,25,3072]{2,1,0:T(8,128)(2,1)}), bf16[16,25,3072]{2,1,0:T(8,128)(2,1)S(1)}, u32[]{:S(2)}, u32[]{:S(2)}) %all-to-all-start) | async-done | bytes 2457632 | tf_op jit(solution)/shard_map/while/body/eval_jaxpr/all_to_all | solution.py:153
  465.3 18.5 %conditional.6 = (f32[400,1344]{1,0:T(8,128)}, bf16[400,3072]{1,0:T(8,128)(2,1)}) conditional(s32[]{:T(128)} %convert_element_type.221, () %tuple.113, (bf16[16,25,3072]{2,1,0:T(8,128)(2,1)S(1)}, bf16[1344,3072]{1,0:T(8,128)(2,1)}, bf16[1344,3072]{1,0:T(8,128)(2,1)}) %tuple.114), branch_computations={%region_6.6_spmd, %region_7.7_spmd} | conditional | flops 6609945600 | bytes 63676460 | solution.py:154
  467.2 9.6 fusion.60
  476.8 7.0 convolution_convert_fusion
  494.6 27.4 %all-to-all-done.1 = bf16[16,25,3072]{2,1,0:T(8,128)(2,1)S(1)} async-done(((bf16[16,25,3072]{2,1,0:T(8,128)(2,1)}), bf16[16,25,3072]{2,1,0:T(8,128)(2,1)S(1)}, u32[]{:S(2)}, u32[]{:S(2)}) %all-to-all-start.1) | async-done | bytes 2457632 | tf_op jit(solution)/shard_map/while/body/eval_jaxpr/all_to_all | solution.py:157
  542.3 37.3 %all-reduce.4.cloned.1.call-done = f32[64,3072]{1,0:T(8,128)} async-done(((f32[64,3072]{1,0:T(8,128)}), f32[64,3072]{1,0:T(8,128)}) %all-reduce.4.cloned.1.call-update) | async-done | bytes 786448 | tf_op jit(solution)/shard_map/while/body/eval_jaxpr/psum | solution.py:164
  582.6 513.1 %while.42 = (s32[]{:T(128)}, bf16[64,3072]{1,0:T(8,128)(2,1)}, bf16[2,64,3072]{2,1,0:T(8,128)(2,1)}, f32[3072]{0:T(1024)}, pred[]{:T(512)}, /*index=5*/s32[]{:T(...) while((s32[]{:T(128)}, bf16[64,3072]{1,0:T(8,128)(2,1)}, ...), condition=%wide.region_17.18_spmd.clone, body=%wide.region_10.17_spmd.clone.sunk | while | flops 8506715136 | bytes 95939080 | solution.py:210
  600.1 47.5 %all-to-all-done.2 = bf16[16,25,3072]{2,1,0:T(8,128)(2,1)S(1)} async-done(((bf16[16,25,3072]{2,1,0:T(8,128)(2,1)}), bf16[16,25,3072]{2,1,0:T(8,128)(2,1)S(1)}, u32[]{:S(2)}, u32[]{:S(2)}) %all-to-all-start.2) | async-done | bytes 2457632 | tf_op jit(solution)/shard_map/while/body/eval_jaxpr/all_to_all | solution.py:186
  647.7 16.9 %conditional.7 = (bf16[400,3072]{1,0:T(8,128)(2,1)S(1)}) conditional(s32[]{:T(128)} %convert_element_type.223, () %tuple.118, (bf16[16,25,3072]{2,1,0:T(8,128)(2,1)S(1)}, bf16[1344,3072]{1,0:T(8,128)(2,1)}, f32[2,400,1344]{2,1,0:T(8,128)}, s32[]{:T(128)}, bf16[1344,3072]{1,0:T(8,128)(2,1)}) %tuple.119), branch_computations={%region_12.12_spmd, %region_13.13_spmd} | conditional | flops 6612096000 | bytes 28598792 | solution.py:187
  649.6 15.0 %convolution_convert_fusion.1 = bf16[400,3072]{1,0:T(8,128)(2,1)S(1)} fusion(bf16[1344,3072]{1,0:T(8,128)(2,1)} %get-tuple-element.585, bf16[400,3072]{1,0:T(8,128)(2,1)} %reshape.159, bf16[1344,3072]{1,0:T(8,128)(2,1)} %get-tuple-element.582, f32[2,400,1344]{2,1,0:T(8,128)} %get-tuple-element.583, s32[]{:T(128)} %get-tuple-element.584), kind=kOutput, calls=%fused_computation.4 | convolution fusion | flops 6612096000 | bytes 23683584 | tf_op jit(solution)/shard_map/while/body/eval_jaxpr/cond/branch_1_fun/dot_general | solution.py:96
  668.2 29.9 %all_to_all.50 = bf16[16,25,3072]{2,1,0:T(8,128)(2,1)} all-to-all(bf16[16,25,3072]{2,1,0:T(8,128)(2,1)S(1)} %reshape.192), channel_id=1, replica_groups=mesh['section'=2,'dp'=16,'expert'=4] {'dp'}, dimensions={0} | all-to-all | bytes 4915200 | tf_op jit(solution)/shard_map/while/body/eval_jaxpr/all_to_all | solution.py:194
  706.0 37.0 %all-reduce.6.cloned.1.call-done = f32[64,3072]{1,0:T(8,128)} async-done(((f32[64,3072]{1,0:T(8,128)}), f32[64,3072]{1,0:T(8,128)}) %all-reduce.6.cloned.1.call-update) | async-done | bytes 786448 | tf_op jit(solution)/shard_map/while/body/eval_jaxpr/psum | solution.py:201
  766.5 47.5 %all-to-all-done.2 = bf16[16,25,3072]{2,1,0:T(8,128)(2,1)S(1)} async-done(((bf16[16,25,3072]{2,1,0:T(8,128)(2,1)}), bf16[16,25,3072]{2,1,0:T(8,128)(2,1)S(1)}, u32[]{:S(2)}, u32[]{:S(2)}) %all-to-all-start.2) | async-done | bytes 2457632 | tf_op jit(solution)/shard_map/while/body/eval_jaxpr/all_to_all | solution.py:186
  814.0 16.9 %conditional.7 = (bf16[400,3072]{1,0:T(8,128)(2,1)S(1)}) conditional(s32[]{:T(128)} %convert_element_type.223, () %tuple.118, (bf16[16,25,3072]{2,1,0:T(8,128)(2,1)S(1)}, bf16[1344,3072]{1,0:T(8,128)(2,1)}, f32[2,400,1344]{2,1,0:T(8,128)}, s32[]{:T(128)}, bf16[1344,3072]{1,0:T(8,128)(2,1)}) %tuple.119), branch_computations={%region_12.12_spmd, %region_13.13_spmd} | conditional | flops 6612096000 | bytes 28598792 | solution.py:187
  816.0 15.0 %convolution_convert_fusion.1 = bf16[400,3072]{1,0:T(8,128)(2,1)S(1)} fusion(bf16[1344,3072]{1,0:T(8,128)(2,1)} %get-tuple-element.585, bf16[400,3072]{1,0:T(8,128)(2,1)} %reshape.159, bf16[1344,3072]{1,0:T(8,128)(2,1)} %get-tuple-element.582, f32[2,400,1344]{2,1,0:T(8,128)} %get-tuple-element.583, s32[]{:T(128)} %get-tuple-element.584), kind=kOutput, calls=%fused_computation.4 | convolution fusion | flops 6612096000 | bytes 23683584 | tf_op jit(solution)/shard_map/while/body/eval_jaxpr/cond/branch_1_fun/dot_general | solution.py:96
  834.6 42.3 %all_to_all.50 = bf16[16,25,3072]{2,1,0:T(8,128)(2,1)} all-to-all(bf16[16,25,3072]{2,1,0:T(8,128)(2,1)S(1)} %reshape.192), channel_id=1, replica_groups=mesh['section'=2,'dp'=16,'expert'=4] {'dp'}, dimensions={0} | all-to-all | bytes 4915200 | tf_op jit(solution)/shard_map/while/body/eval_jaxpr/all_to_all | solution.py:194
  884.8 39.4 %all-reduce.6.cloned.1.call-done = f32[64,3072]{1,0:T(8,128)} async-done(((f32[64,3072]{1,0:T(8,128)}), f32[64,3072]{1,0:T(8,128)}) %all-reduce.6.cloned.1.call-update) | async-done | bytes 786448 | tf_op jit(solution)/shard_map/while/body/eval_jaxpr/psum | solution.py:201
  947.7 47.5 %all-to-all-done.2 = bf16[16,25,3072]{2,1,0:T(8,128)(2,1)S(1)} async-done(((bf16[16,25,3072]{2,1,0:T(8,128)(2,1)}), bf16[16,25,3072]{2,1,0:T(8,128)(2,1)S(1)}, u32[]{:S(2)}, u32[]{:S(2)}) %all-to-all-start.2) | async-done | bytes 2457632 | tf_op jit(solution)/shard_map/while/body/eval_jaxpr/all_to_all | solution.py:186
  999.1 27.3 %all_to_all.50 = bf16[16,25,3072]{2,1,0:T(8,128)(2,1)} all-to-all(bf16[16,25,3072]{2,1,0:T(8,128)(2,1)S(1)} %reshape.192), channel_id=1, replica_groups=mesh['section'=2,'dp'=16,'expert'=4] {'dp'}, dimensions={0} | all-to-all | bytes 4915200 | tf_op jit(solution)/shard_map/while/body/eval_jaxpr/all_to_all | solution.py:194
  1034.3 56.4 %all-reduce.6.cloned.1.call-done = f32[64,3072]{1,0:T(8,128)} async-done(((f32[64,3072]{1,0:T(8,128)}), f32[64,3072]{1,0:T(8,128)}) %all-reduce.6.cloned.1.call-update) | async-done | bytes 786448 | tf_op jit(solution)/shard_map/while/body/eval_jaxpr/psum | solution.py:201
  1095.7 60.1 %all-reduce = f32[3072]{0:T(1024)S(1)} all-reduce(f32[3072]{0:T(1024)} %get-tuple-element.613), channel_id=2, replica_groups=mesh['section'=2,'dp'=16,'expert'=4] {'dp'}, use_global_device_ids=true, to_apply=%region_18.19.clone | all-reduce | flops 3072 | bytes 24576
  (219 shorter events, 276.6 us)
Async XLA Ops:
  20.8 3.9 collective-permute-start
  30.8 55.4 %all-to-all-start = ((bf16[16,25,3072]{2,1,0:T(8,128)(2,1)}), bf16[16,25,3072]{2,1,0:T(8,128)(2,1)S(1)}, u32[]{:S(2)}, u32[]{:S(2)}) async-start(bf16[16,25,3072]{2,1,0:T(8,128)(2,1)} %reshape.189), calls=%async_computation | async-start | bytes 6291456 | tf_op jit(solution)/shard_map/while/body/eval_jaxpr/all_to_all | solution.py:153
  92.8 34.9 %all-to-all-start.1 = ((bf16[16,25,3072]{2,1,0:T(8,128)(2,1)}), bf16[16,25,3072]{2,1,0:T(8,128)(2,1)S(1)}, u32[]{:S(2)}, u32[]{:S(2)}) async-start(bf16[16,25,3072]{2,1,0:T(8,128)(2,1)} %reshape.190), calls=%async_computation.1 | async-start | bytes 6291456 | tf_op jit(solution)/shard_map/while/body/eval_jaxpr/all_to_all | solution.py:157
  96.9 104.9 %all-reduce.4.cloned.1.call-start = ((), (), s32[]{:S(2)}) async-start(), calls=%async_computation.4 | async-start | bytes 1572864 | tf_op jit(solution)/shard_map/while/body/eval_jaxpr/psum | solution.py:164
  144.7 57.1 %copy-start.1 = (bf16[1,64,3072]{2,1,0:T(8,128)(2,1)S(1)}, bf16[1,64,3072]{2,1,0:T(8,128)(2,1)}, u32[]{:S(2)}) copy-start(bf16[1,64,3072]{2,1,0:T(8,128)(2,1)} %constant_dynamic-slice_fusion.11) | copy-start | bytes 1179652 | tf_op jit(solution)/shard_map/while
  203.9 4.8 collective-permute-start
  214.8 54.6 %all-to-all-start = ((bf16[16,25,3072]{2,1,0:T(8,128)(2,1)}), bf16[16,25,3072]{2,1,0:T(8,128)(2,1)S(1)}, u32[]{:S(2)}, u32[]{:S(2)}) async-start(bf16[16,25,3072]{2,1,0:T(8,128)(2,1)} %reshape.189), calls=%async_computation | async-start | bytes 6291456 | tf_op jit(solution)/shard_map/while/body/eval_jaxpr/all_to_all | solution.py:153
  291.3 49.2 %all-to-all-start.1 = ((bf16[16,25,3072]{2,1,0:T(8,128)(2,1)}), bf16[16,25,3072]{2,1,0:T(8,128)(2,1)S(1)}, u32[]{:S(2)}, u32[]{:S(2)}) async-start(bf16[16,25,3072]{2,1,0:T(8,128)(2,1)} %reshape.190), calls=%async_computation.1 | async-start | bytes 6291456 | tf_op jit(solution)/shard_map/while/body/eval_jaxpr/all_to_all | solution.py:157
  295.5 102.3 %all-reduce.4.cloned.1.call-start = ((), (), s32[]{:S(2)}) async-start(), calls=%async_computation.4 | async-start | bytes 1572864 | tf_op jit(solution)/shard_map/while/body/eval_jaxpr/psum | solution.py:164
  399.8 4.8 collective-permute-start
  410.7 54.6 %all-to-all-start = ((bf16[16,25,3072]{2,1,0:T(8,128)(2,1)}), bf16[16,25,3072]{2,1,0:T(8,128)(2,1)S(1)}, u32[]{:S(2)}, u32[]{:S(2)}) async-start(bf16[16,25,3072]{2,1,0:T(8,128)(2,1)} %reshape.189), calls=%async_computation | async-start | bytes 6291456 | tf_op jit(solution)/shard_map/while/body/eval_jaxpr/all_to_all | solution.py:153
  487.1 34.8 %all-to-all-start.1 = ((bf16[16,25,3072]{2,1,0:T(8,128)(2,1)}), bf16[16,25,3072]{2,1,0:T(8,128)(2,1)S(1)}, u32[]{:S(2)}, u32[]{:S(2)}) async-start(bf16[16,25,3072]{2,1,0:T(8,128)(2,1)} %reshape.190), calls=%async_computation.1 | async-start | bytes 6291456 | tf_op jit(solution)/shard_map/while/body/eval_jaxpr/all_to_all | solution.py:157
  491.3 88.2 %all-reduce.4.cloned.1.call-start = ((), (), s32[]{:S(2)}) async-start(), calls=%async_computation.4 | async-start | bytes 1572864 | tf_op jit(solution)/shard_map/while/body/eval_jaxpr/psum | solution.py:164
  582.6 573.2 %copy-start.8 = (u32[128]{0:T(128)S(1)}, u32[128]{0:T(128)}, u32[]{:S(2)}) copy-start(u32[128]{0:T(128)} %constant.215) | copy-start | bytes 1540
  582.6 5.6 collective-permute-start.1
  593.5 54.1 %all-to-all-start.2 = ((bf16[16,25,3072]{2,1,0:T(8,128)(2,1)}), bf16[16,25,3072]{2,1,0:T(8,128)(2,1)S(1)}, u32[]{:S(2)}, u32[]{:S(2)}) async-start(bf16[16,25,3072]{2,1,0:T(8,128)(2,1)} %reshape.191), calls=%async_computation.2 | async-start | bytes 6291456 | tf_op jit(solution)/shard_map/while/body/eval_jaxpr/all_to_all | solution.py:186
  600.1 143.0 %all-reduce.6.cloned.1.call-start = ((), (), s32[]{:S(2)}) async-start(), calls=%async_computation.5 | async-start | bytes 1572864 | tf_op jit(solution)/shard_map/while/body/eval_jaxpr/psum | solution.py:201
  703.6 41.0 %copy-start.5 = (f32[3072]{0:T(1024)S(1)}, f32[3072]{0:T(1024)}, u32[]{:S(2)}) copy-start(f32[3072]{0:T(1024)} %get-tuple-element.1102) | copy-start | bytes 36868 | tf_op jit(solution)/shard_map/while
  703.6 41.0 %copy-start.2 = (bf16[2,64,3072]{2,1,0:T(8,128)(2,1)S(1)}, bf16[2,64,3072]{2,1,0:T(8,128)(2,1)}, u32[]{:S(2)}) copy-start(bf16[2,64,3072]{2,1,0:T(8,128)(2,1)} %get-tuple-element.1122) | copy-start | bytes 2359300 | tf_op jit(solution)/shard_map/while
  703.6 41.0 %copy-start.3 = (bf16[2,64,3072]{2,1,0:T(8,128)(2,1)S(1)}, bf16[2,64,3072]{2,1,0:T(8,128)(2,1)}, u32[]{:S(2)}) copy-start(bf16[2,64,3072]{2,1,0:T(8,128)(2,1)} %get-tuple-element.1101) | copy-start | bytes 2359300 | tf_op jit(solution)/shard_map/while
  749.0 5.6 collective-permute-start.1
  759.9 54.1 %all-to-all-start.2 = ((bf16[16,25,3072]{2,1,0:T(8,128)(2,1)}), bf16[16,25,3072]{2,1,0:T(8,128)(2,1)S(1)}, u32[]{:S(2)}, u32[]{:S(2)}) async-start(bf16[16,25,3072]{2,1,0:T(8,128)(2,1)} %reshape.191), calls=%async_computation.2 | async-start | bytes 6291456 | tf_op jit(solution)/shard_map/while/body/eval_jaxpr/all_to_all | solution.py:186
  766.4 157.8 %all-reduce.6.cloned.1.call-start = ((), (), s32[]{:S(2)}) async-start(), calls=%async_computation.5 | async-start | bytes 1572864 | tf_op jit(solution)/shard_map/while/body/eval_jaxpr/psum | solution.py:201
  882.4 43.4 %copy-start.5 = (f32[3072]{0:T(1024)S(1)}, f32[3072]{0:T(1024)}, u32[]{:S(2)}) copy-start(f32[3072]{0:T(1024)} %get-tuple-element.1102) | copy-start | bytes 36868 | tf_op jit(solution)/shard_map/while
  882.4 43.4 %copy-start.2 = (bf16[2,64,3072]{2,1,0:T(8,128)(2,1)S(1)}, bf16[2,64,3072]{2,1,0:T(8,128)(2,1)}, u32[]{:S(2)}) copy-start(bf16[2,64,3072]{2,1,0:T(8,128)(2,1)} %get-tuple-element.1122) | copy-start | bytes 2359300 | tf_op jit(solution)/shard_map/while
  882.4 43.4 %copy-start.3 = (bf16[2,64,3072]{2,1,0:T(8,128)(2,1)S(1)}, bf16[2,64,3072]{2,1,0:T(8,128)(2,1)}, u32[]{:S(2)}) copy-start(bf16[2,64,3072]{2,1,0:T(8,128)(2,1)} %get-tuple-element.1101) | copy-start | bytes 2359300 | tf_op jit(solution)/shard_map/while
  930.2 5.6 collective-permute-start.1
  941.1 54.1 %all-to-all-start.2 = ((bf16[16,25,3072]{2,1,0:T(8,128)(2,1)}), bf16[16,25,3072]{2,1,0:T(8,128)(2,1)S(1)}, u32[]{:S(2)}, u32[]{:S(2)}) async-start(bf16[16,25,3072]{2,1,0:T(8,128)(2,1)} %reshape.191), calls=%async_computation.2 | async-start | bytes 6291456 | tf_op jit(solution)/shard_map/while/body/eval_jaxpr/all_to_all | solution.py:186
  947.6 143.1 %all-reduce.6.cloned.1.call-start = ((), (), s32[]{:S(2)}) async-start(), calls=%async_computation.5 | async-start | bytes 1572864 | tf_op jit(solution)/shard_map/while/body/eval_jaxpr/psum | solution.py:201
  1031.9 60.4 %copy-start.5 = (f32[3072]{0:T(1024)S(1)}, f32[3072]{0:T(1024)}, u32[]{:S(2)}) copy-start(f32[3072]{0:T(1024)} %get-tuple-element.1102) | copy-start | bytes 36868 | tf_op jit(solution)/shard_map/while
  1031.9 60.4 %copy-start.2 = (bf16[2,64,3072]{2,1,0:T(8,128)(2,1)S(1)}, bf16[2,64,3072]{2,1,0:T(8,128)(2,1)}, u32[]{:S(2)}) copy-start(bf16[2,64,3072]{2,1,0:T(8,128)(2,1)} %get-tuple-element.1122) | copy-start | bytes 2359300 | tf_op jit(solution)/shard_map/while
  1031.9 60.4 %copy-start.3 = (bf16[2,64,3072]{2,1,0:T(8,128)(2,1)S(1)}, bf16[2,64,3072]{2,1,0:T(8,128)(2,1)}, u32[]{:S(2)}) copy-start(bf16[2,64,3072]{2,1,0:T(8,128)(2,1)} %get-tuple-element.1101) | copy-start | bytes 2359300 | tf_op jit(solution)/shard_map/while
  (13 other events, 114.2 us)
Sparse Core Ops, SparseCore 0:
  143.0 58.7 all-reduce.3
  355.8 41.8 all-reduce.3
  537.3 42.2 all-reduce.3
  703.8 39.1 all-reduce.5
  882.6 41.5 all-reduce.5
  1032.1 58.6 all-reduce.5
where the time goes:
time: 1180 us; the launch traced here: 1160 us
  waiting for transfers between devices  654 us (55%)
  blocking collectives  159 us (13%)
  matrix products  109 us (9%)
  local copies, waits for them, and re-layouts  101 us (9%)
  starting transfers between devices  69.5 us (6%)
  other arithmetic  55.4 us (5%)
  between operations  14.8 us (1%)
    all_to_all x3, waiting for transfers between devices, forward_tick(): lax.all_to_all(outgoing, 'dp', split_axis=0, concat_axis=0, tiled=True)  144 us
    all_to_all x3, waiting for transfers between devices, backward_tick(): lax.all_to_all(outgoing, 'dp', split_axis=0, concat_axis=0, tiled=True)  143 us
    psum x3, waiting for transfers between devices, backward_tick(): lax.psum(home_rows(returned, pick_row(selectors, clipped)), 'expert')  133 us
    psum x3, waiting for transfers between devices, forward_tick(): lax.psum(weighted_home(returned, pick_row(selectors, clipped), pick_row(s...  130 us
    all_to_all x3, blocking collectives, backward_tick(): lax.all_to_all(d_part.reshape(owners, capacity, model_width), 'dp', split...  99.4 us
    all_to_all x3, waiting for transfers between devices, forward_tick(): lax.all_to_all(part.reshape(owners, capacity, model_width), 'dp', split_a...  96.7 us
    unnamed x1, blocking collectives  60.1 us
    dot_general x2, matrix products, expert_backward(): jnp.dot(d_pre, up_rows, preferred_element_type=jnp.float32)  30.1 us
  transfers between devices with their start and end apart: 21, of which 21 were waited for; matrix products, arithmetic and copies ran while one was open for 3% of the time, Pallas kernels for 0%

commit v1 on v0

v1 whole, which is shorter than its diff:
```python
import jax
import jax.numpy as jnp
import numpy as np
from jax import lax
from jax.sharding import PartitionSpec as P

EPSILON = 1e-05
SWAP = [(0, 1), (1, 0)]
LANES = 128


def swapped(x):
    return lax.ppermute(x, "section", SWAP)


def normalize(current):
    state_f = current.astype(jnp.float32)
    inverse_rms = lax.rsqrt(jnp.mean(state_f * state_f, axis=-1, keepdims=True) + EPSILON)
    return state_f, inverse_rms


def shards(inputs, cotangent, gain, w_up, w_down, expert_ids, expert_counts, combine_fixed):
    section = lax.axis_index("section")
    owners = lax.axis_size("dp")
    ring = lax.axis_size("expert")
    row_count, width = inputs.shape[1:]
    top = expert_ids.shape[3]
    capacity = min(row_count, row_count * top // owners + 1)
    whole = capacity - 1
    main_rows = owners * whole
    bf16, f32 = jnp.bfloat16, jnp.float32

    up_own, down_own = w_up[0, 0], w_down[0, 0]
    first = section == 0

    def pick(mine, other, layer):
        return jnp.where(section == layer, mine, other)

    ints = jnp.concatenate([expert_ids[0], expert_counts[0][..., None], combine_fixed[0]], axis=-1)
    mine = lax.dynamic_index_in_dim(ints, section, 0, keepdims=False)
    theirs = swapped(lax.dynamic_index_in_dim(ints, 1 - section, 0, keepdims=False))
    gain_other = swapped(gain[0])
    gains = [pick(gain[0], gain_other, layer).astype(f32) for layer in range(2)]
    x0 = lax.dynamic_index_in_dim(inputs, section, 0, keepdims=False)
    upstream = lax.dynamic_index_in_dim(cotangent, section, 0, keepdims=False)
    up_other, down_other = swapped(up_own), swapped(down_own)

    column_owner = np.concatenate([np.repeat(np.arange(owners), whole), np.arange(owners)])
    column_place = np.concatenate([np.tile(np.arange(whole), owners), np.full(owners, whole)])
    spread = jnp.asarray(column_owner[None, :] == np.arange(owners)[:, None], bf16)
    place = jnp.asarray(column_place, f32)[None, :]
    below = jnp.asarray(np.tril(np.ones((row_count, row_count)), -1), bf16)

    def tables(packed):
        ids, counts, fixed = packed[:, :top], packed[:, top], packed[:, top + 1 :]
        live = jnp.arange(top)[None, :] < counts[:, None]
        shares = jnp.where(live, fixed.astype(f32), 0.0)
        shares = shares / jnp.sum(shares, axis=1, keepdims=True)
        named = ids[:, :, None] == jnp.arange(owners)[None, None, :]
        hot = jnp.sum(named.astype(f32), axis=1)
        share = jnp.sum(named.astype(f32) * shares[:, :, None], axis=1)
        before = jnp.dot(below, hot.astype(bf16), preferred_element_type=f32)
        hot_c = jnp.dot(hot.astype(bf16), spread, preferred_element_type=f32)
        before_c = jnp.dot(before.astype(bf16), spread, preferred_element_type=f32)
        share_c = jnp.dot(share.astype(bf16), spread, preferred_element_type=f32)
        chosen = hot_c * (before_c == place).astype(f32)
        return chosen.astype(bf16), (chosen * share_c).astype(bf16)

    plain, weighted = zip(*[tables(pick(mine, theirs, layer)) for layer in range(2)])

    def blocks(rows):
        head = rows[:main_rows].reshape(owners, whole, width)
        tail = rows[main_rows:].reshape(owners, whole, LANES)
        return jnp.concatenate([head, tail], axis=2)

    def unblocks(held):
        head = held[:, :, :width].reshape(main_rows, width)
        tail = held[:, :, width:].reshape(owners, width)
        return jnp.concatenate([head, tail], axis=0)

    def exchange(*rows):
        sent = [blocks(r) for r in rows]
        held = sent[0] if len(sent) == 1 else jnp.concatenate(sent, axis=1)
        back = lax.all_to_all(held, "dp", split_axis=0, concat_axis=0, tiled=True)
        return [unblocks(back[:, i * whole : (i + 1) * whole]) for i in range(len(rows))]

    def gathered(table, rows):
        return lax.dot_general(
            table, rows, (((0,), (0,)), ((), ())), preferred_element_type=f32
        ).astype(bf16)

    def over_groups(part):
        part = part.astype(bf16)
        near = [
            lax.ppermute(part, "expert", [(i, (i + by) % ring) for i in range(ring)])
            for by in (2, 1, 3)
        ]
        part, far, left, right = (v.astype(f32) for v in (part, *near))
        return (part + far) + (left + right)

    def home(table, rows):
        return over_groups(jnp.dot(table, rows, preferred_element_type=f32))

    def with_weights(layer, fn, *args):
        return lax.cond(
            section == layer,
            lambda uo, do, ux, dx, *a: fn(uo, do, *a),
            lambda uo, do, ux, dx, *a: fn(ux, dx, *a),
            up_own,
            down_own,
            up_other,
            down_other,
            *args,
        )

    def forward(up, down, rows):
        pre = lax.dot_general(rows, up, (((1,), (1,)), ((), ())), preferred_element_type=f32)
        activated = jax.nn.silu(pre).astype(bf16)
        return pre, jnp.dot(activated, down, preferred_element_type=f32).astype(bf16)

    def backward(up, down, rows, pre):
        d_act = lax.dot_general(rows, down, (((1,), (1,)), ((), ())), preferred_element_type=f32)
        logistic = jax.nn.sigmoid(pre)
        d_pre = (d_act * logistic * (1.0 + pre * (1.0 - logistic))).astype(bf16)
        return jnp.dot(d_pre, up, preferred_element_type=f32).astype(bf16)

    def forward_backward(up, down, rows, d_rows):
        pre, part = forward(up, down, rows)
        return part, backward(up, down, d_rows, pre)

    def normed_rows(current, layer):
        state_f, inverse_rms = normalize(current)
        return (state_f * inverse_rms * gains[layer]).astype(bf16)

    def finish(current, upstream, d_norm, layer):
        state_f, inverse_rms = normalize(current)
        scaled = state_f * inverse_rms
        d_scaled = d_norm * gains[layer]
        d_input = inverse_rms * (
            d_scaled - scaled * jnp.mean(d_scaled * scaled, axis=-1, keepdims=True)
        )
        return (upstream.astype(f32) + d_input).astype(bf16), jnp.sum(d_norm * scaled, axis=0)

    rows0, d_rows1 = exchange(
        gathered(plain[0], normed_rows(x0, 0)), gathered(weighted[1], upstream)
    )
    pre0, part0 = with_weights(0, forward, rows0)
    (back0,) = exchange(part0)
    x1 = (x0.astype(f32) + home(weighted[0], back0)).astype(bf16)
    (rows1,) = exchange(gathered(plain[1], normed_rows(x1, 1)))
    part1, d_part1 = with_weights(1, forward_backward, rows1, d_rows1)
    d_back1, back1 = exchange(d_part1, part1)
    grad1, gain1 = finish(x1, upstream, home(plain[1], d_back1), 1)
    (d_rows0,) = exchange(gathered(weighted[0], grad1))
    d_part0 = with_weights(0, backward, d_rows0, pre0)
    x2 = (x1.astype(f32) + home(weighted[1], back1)).astype(bf16)
    (d_back0,) = exchange(d_part0)
    grad0, gain0 = finish(x0, grad1, home(plain[0], d_back0), 0)

    kept = jnp.stack([pick(x1, x2, 0), pick(grad0, grad1, 0)])
    given = jnp.stack([pick(x2, x1, 0), pick(grad1, grad0, 0)])
    taken = swapped(given)
    low = jnp.where(first, kept, taken)
    high = jnp.where(first, taken, kept)
    both = jnp.stack([low, high], axis=1)
    gain_kept = pick(gain0, gain1, 0)
    gain_sum = gain_kept + swapped(pick(gain1, gain0, 0))
    slices = lax.all_to_all(
        gain_sum.reshape(owners, width // owners), "dp", split_axis=0, concat_axis=0, tiled=True
    )
    return both[0][None], both[1][None], jnp.sum(slices, axis=0)[None]


def solution(mesh):
    return jax.shard_map(
        shards,
        mesh=mesh,
        in_specs=(
            P(None, "dp", None),
            P(None, "dp", None),
            P("section", None),
            P("section", "dp", "expert", None),
            P("section", "dp", "expert", None),
            P("section", None, "dp", None),
            P("section", None, "dp"),
            P("section", None, "dp", None),
        ),
        out_specs=(
            P("section", None, "dp", None),
            P("section", None, "dp", None),
            P("section", "dp"),
        ),
        check_vma=False,
    )
```

time: 1180 us -> 488 us (0.41)
  waiting for transfers between devices: 654 us -> 213 us
  local copies, waits for them, and re-layouts: 101 us -> 16.3 us
  blocking collectives: 159 us -> 98.5 us
  matrix products: 109 us -> 75.1 us
  other arithmetic: 55.4 us -> 22.5 us
  starting transfers between devices: 69.5 us -> 44.5 us
  between operations: 14.8 us -> 1.89 us
    psum x6 -> x0, waiting for transfers between devices: 262 us -> none  [the longest x3 133 us: backward_tick(): lax.psum(home_rows(returned, pick_row(selectors, clipped)), 'expert')]
    all_to_all x9 -> x4, waiting for transfers between devices: 383 us -> 162 us  [exchange(): back = lax.all_to_all(held, 'dp', split_axis=0, concat_axis=0, tiled=True)]
    unnamed x1 -> x0, blocking collectives: 60.1 us -> none
    reshape x19 -> x0, local copies, waits for them, and re-layouts: 43.7 us -> none  [the longest x3 10.1 us: forward_tick(): part.reshape(owners, capacity, model_width)]
    ppermute x6 -> x18, waiting for transfers between devices: 8.43 us -> 51 us  [the longest x12 49.2 us: over_groups(): lax.ppermute(part, 'expert', [(i, (i + by) % ring) for i in range(ring)])]
    dot_general x20, matrix products: 109 us -> 75.1 us  [the longest x2 30 us: backward(): return jnp.dot(d_pre, up, preferred_element_type=f32).astype(bf16)]
    all_to_all x9 -> x4, starting transfers between devices: 52.5 us -> 19.5 us  [exchange(): back = lax.all_to_all(held, 'dp', split_axis=0, concat_axis=0, tiled=True)]
    dynamic_update_slice x12 -> x0, other arithmetic: 27.5 us -> none  [keep_at(): lax.dynamic_update_index_in_dim(stash, jnp.where(active, value, previous)...]
  transfers between devices with their start and end apart: 21 -> 22, of which waited for: 21 -> 11; matrix products, arithmetic and copies ran while one was open for 3% -> 6% of each run, Pallas kernels for 0% -> 0%
where the time goes in v1:
time: 488 us; the launch traced here: 480 us
  waiting for transfers between devices  213 us (44%)
  blocking collectives  98.5 us (20%)
  matrix products  75.1 us (15%)
  starting transfers between devices  44.5 us (9%)
  other arithmetic  22.5 us (5%)
  local copies, waits for them, and re-layouts  16.3 us (3%)
  loops' own time  8.96 us (2%)
    all_to_all x4, waiting for transfers between devices, exchange(): back = lax.all_to_all(held, 'dp', split_axis=0, concat_axis=0, tiled=True)  162 us
    all_to_all x2, blocking collectives, exchange(): back = lax.all_to_all(held, 'dp', split_axis=0, concat_axis=0, tiled=True)  89 us
    ppermute x12, waiting for transfers between devices, over_groups(): lax.ppermute(part, 'expert', [(i, (i + by) % ring) for i in range(ring)])  49.2 us
    dot_general x2, matrix products, backward(): return jnp.dot(d_pre, up, preferred_element_type=f32).astype(bf16)  30 us
    ppermute x12, starting transfers between devices, over_groups(): lax.ppermute(part, 'expert', [(i, (i + by) % ring) for i in range(ring)])  22.3 us
    all_to_all x4, starting transfers between devices, exchange(): back = lax.all_to_all(held, 'dp', split_axis=0, concat_axis=0, tiled=True)  19.5 us
    dot_general x2, matrix products, forward(): jnp.dot(activated, down, preferred_element_type=f32).astype(bf16)  16 us
    dot_general x2, matrix products, forward(): lax.dot_general(rows, up, (((1,), (1,)), ((), ())), preferred_element_typ...  15.6 us
  transfers between devices with their start and end apart: 22, of which 11 were waited for; matrix products, arithmetic and copies ran while one was open for 6% of the time, Pallas kernels for 0%

profile of v1, /device:TPU:1, one launch (start us, length us, event | category | flops | bytes accessed | tf_op | source)
XLA Modules:
  0.0 480.3 jit_solution(9385304712473183359)
XLA Ops:
  18.4 6.9 %all-to-all-start = ((bf16[16,48,3200]{2,1,0:T(8,128)(2,1)}), bf16[16,48,3200]{2,1,0:T(8,128)(2,1)}, u32[]{:S(2)}, u32[]{:S(2)}) async-start(bf16[16,48,3200]{2,1,0:T(8,128)(2,1)} %maximum_maximum_fusion), calls=%async_computation | async-start | bytes 9830400 | tf_op jit(solution)/shard_map/all_to_all | solution.py:84
  25.3 73.1 %all-to-all-done = bf16[16,48,3200]{2,1,0:T(8,128)(2,1)} async-done(((bf16[16,48,3200]{2,1,0:T(8,128)(2,1)}), bf16[16,48,3200]{2,1,0:T(8,128)(2,1)}, u32[]{:S(2)}, u32[]{:S(2)}) %all-to-all-start) | async-done | bytes 4915232 | tf_op jit(solution)/shard_map/all_to_all | solution.py:84
  99.6 4.4 fusion.101
  104.1 16.1 %conditional.6 = (f32[400,1344]{1,0:T(8,128)}, bf16[400,3072]{1,0:T(8,128)(2,1)S(1)}) conditional(s32[]{:T(128)} %convert_element_type.224, (bf16[400,3072]{1,0:T(8,128)(2,1)S(1)}, bf16[1344,3072]{1,0:T(8,128)(2,1)}, bf16[1344,3072]{1,0:T(8,128)(2,1)}) %tuple.39, (bf16[400,3072]{1,0:T(8,128)(2,1)S(1)}, bf16[1344,3072]{1,0:T(8,128)(2,1)S(1)}, ...), branch_computations={%region_7.8_spmd, %region_8.9_spmd} | conditional | flops 6608716800 | bytes 58761260
  104.2 7.8 %fusion.103 = f32[400,1344]{1,0:T(8,128)} fusion(bf16[400,3072]{1,0:T(8,128)(2,1)S(1)} %get-tuple-element.56, bf16[1344,3072]{1,0:T(8,128)(2,1)} %get-tuple-element.57), kind=kOutput, calls=%fused_computation.194 | convolution fusion | flops 3303014400 | bytes 12865536 | tf_op jit(solution)/shard_map/cond/branch_0_fun/dot_general | solution.py:117
  112.0 8.0 %fusion = bf16[400,3072]{1,0:T(8,128)(2,1)S(1)} fusion(bf16[1344,3072]{1,0:T(8,128)(2,1)} %get-tuple-element.58, f32[400,1344]{1,0:T(8,128)} %fusion.103), kind=kOutput, calls=%fused_computation.1 | convolution fusion | flops 3305702400 | bytes 12865536 | tf_op jit(solution)/shard_map/cond/branch_0_fun/dot_general | solution.py:119
  122.1 5.0 %all-to-all-start.1 = ((bf16[16,24,3200]{2,1,0:T(8,128)(2,1)}), bf16[16,24,3200]{2,1,0:T(8,128)(2,1)S(1)}, u32[]{:S(2)}, u32[]{:S(2)}) async-start(bf16[16,24,3200]{2,1,0:T(8,128)(2,1)} %pad_maximum_fusion.1), calls=%async_computation.1 | async-start | bytes 4915200 | tf_op jit(solution)/shard_map/all_to_all | solution.py:84
  127.3 33.4 %all-to-all-done.1 = bf16[16,24,3200]{2,1,0:T(8,128)(2,1)S(1)} async-done(((bf16[16,24,3200]{2,1,0:T(8,128)(2,1)}), bf16[16,24,3200]{2,1,0:T(8,128)(2,1)S(1)}, u32[]{:S(2)}, u32[]{:S(2)}) %all-to-all-start.1) | async-done | bytes 2457632 | tf_op jit(solution)/shard_map/all_to_all | solution.py:84
  161.6 3.8 collective-permute-start.6
  166.8 14.9 %collective-permute-done.6 = bf16[64,3072]{1,0:T(8,128)(2,1)S(1)} collective-permute-done((bf16[64,3072]{1,0:T(8,128)(2,1)S(1)}, bf16[64,3072]{1,0:T(8,128)(2,1)S(1)}, u32[]{:S(2)}, u32[]{:S(2)}) %collective-permute-start.6) | collective-permute-done | bytes 393248 | tf_op jit(solution)/shard_map/ppermute | solution.py:95
  181.7 3.4 collective-permute-done.5
  188.3 3.7 all-to-all-start.2
  192.0 3.3 pad_maximum_fusion.4
  195.3 32.5 %all-to-all-done.2 = bf16[16,24,3200]{2,1,0:T(8,128)(2,1)S(1)} async-done(((bf16[16,24,3200]{2,1,0:T(8,128)(2,1)}), bf16[16,24,3200]{2,1,0:T(8,128)(2,1)S(1)}, u32[]{:S(2)}, u32[]{:S(2)}) %all-to-all-start.2) | async-done | bytes 2457632 | tf_op jit(solution)/shard_map/all_to_all | solution.py:84
  228.3 39.3 %conditional.7 = (bf16[400,3072]{1,0:T(8,128)(2,1)S(1)}, bf16[400,3072]{1,0:T(8,128)(2,1)S(1)}) conditional(s32[]{:T(128)} %convert_element_type.244, (bf16[400,3072]{1,0:T(8,128)(2,1)S(1)}, bf16[1344,3072]{1,0:T(8,128)(2,1)}, bf16[1344,3072]{1,0:T(8,128)(2,1)}, bf16[400,3072]{1,0:T(8,128)(2,1)}) %tuple.41, (bf16[400,3072]{1,0:T(8,128)(2,1)S(1)}, ...), branch_computations={%region_10.11_spmd, %region_11.12_spmd} | conditional | flops 13219584000 | bytes 49311760
  236.8 7.8 %fusion.107 = f32[400,1344]{1,0:T(8,128)} fusion(bf16[400,3072]{1,0:T(8,128)(2,1)S(1)} %get-tuple-element.66, bf16[1344,3072]{1,0:T(8,128)(2,1)} %get-tuple-element.67), kind=kOutput, calls=%fused_computation.198 | convolution fusion | flops 3303014400 | bytes 12865536 | tf_op jit(solution)/shard_map/cond/branch_1_fun/dot_general | solution.py:117
  244.5 15.0 %fusion.108 = bf16[400,3072]{1,0:T(8,128)(2,1)S(1)} fusion(bf16[1344,3072]{1,0:T(8,128)(2,1)} %get-tuple-element.67, bf16[400,3072]{1,0:T(8,128)(2,1)} %get-tuple-element.69, bf16[1344,3072]{1,0:T(8,128)(2,1)} %get-tuple-element.68, f32[400,1344]{1,0:T(8,128)} %fusion.107), kind=kOutput, calls=%fused_computation.199 | convolution fusion | flops 6610867200 | bytes 23580672 | tf_op jit(solution)/shard_map/cond/branch_1_fun/dot_general | solution.py:125
  259.6 8.0 %fusion.13 = bf16[400,3072]{1,0:T(8,128)(2,1)S(1)} fusion(bf16[1344,3072]{1,0:T(8,128)(2,1)} %get-tuple-element.68, f32[400,1344]{1,0:T(8,128)} %fusion.107), kind=kOutput, calls=%fused_computation.21 | convolution fusion | flops 3305702400 | bytes 12865536 | tf_op jit(solution)/shard_map/cond/branch_1_fun/dot_general | solution.py:119
  271.4 58.3 %all_to_all.39 = bf16[16,48,3200]{2,1,0:T(8,128)(2,1)S(1)} all-to-all(bf16[16,48,3200]{2,1,0:T(8,128)(2,1)S(1)} %maximum_maximum_fusion.1), channel_id=1, replica_groups=mesh['section'=2,'dp'=16,'expert'=4] {'dp'}, dimensions={0} | all-to-all | bytes 9830400 | tf_op jit(solution)/shard_map/all_to_all | solution.py:84
  333.6 9.3 %collective-permute-done.12 = bf16[64,3072]{1,0:T(8,128)(2,1)S(1)} collective-permute-done((bf16[64,3072]{1,0:T(8,128)(2,1)S(1)}, bf16[64,3072]{1,0:T(8,128)(2,1)S(1)}, u32[]{:S(2)}, u32[]{:S(2)}) %collective-permute-start.12) | collective-permute-done | bytes 393248 | tf_op jit(solution)/shard_map/ppermute | solution.py:95
  343.0 5.5 %collective-permute-done.11 = bf16[64,3072]{1,0:T(8,128)(2,1)S(1)} collective-permute-done((bf16[64,3072]{1,0:T(8,128)(2,1)S(1)}, bf16[64,3072]{1,0:T(8,128)(2,1)S(1)}, u32[]{:S(2)}, u32[]{:S(2)}) %collective-permute-start.11) | collective-permute-done | bytes 393248 | tf_op jit(solution)/shard_map/ppermute | solution.py:95
  351.2 30.8 %all_to_all.40 = bf16[16,24,3200]{2,1,0:T(8,128)(2,1)S(1)} all-to-all(bf16[16,24,3200]{2,1,0:T(8,128)(2,1)S(1)} %pad_maximum_fusion.5), channel_id=1, replica_groups=mesh['section'=2,'dp'=16,'expert'=4] {'dp'}, dimensions={0} | all-to-all | bytes 4915200 | tf_op jit(solution)/shard_map/all_to_all | solution.py:84
  383.9 15.3 %conditional.8 = (bf16[400,3072]{1,0:T(8,128)(2,1)S(1)}) conditional(s32[]{:T(128)} %convert_element_type.224, (bf16[400,3072]{1,0:T(8,128)(2,1)}, bf16[1344,3072]{1,0:T(8,128)(2,1)}, f32[400,1344]{1,0:T(8,128)}, bf16[1344,3072]{1,0:T(8,128)(2,1)}) %tuple.43, (bf16[400,3072]{1,0:T(8,128)(2,1)}, bf16[1344,3072]{1,0:T(8,128)(2,1)}, ...), branch_computations={%region_13.14_spmd, %region_14.15_spmd} | conditional | flops 6610867200 | bytes 23580680
  383.9 15.0 %fusion.109 = bf16[400,3072]{1,0:T(8,128)(2,1)S(1)} fusion(bf16[1344,3072]{1,0:T(8,128)(2,1)} %get-tuple-element.73, bf16[400,3072]{1,0:T(8,128)(2,1)} %get-tuple-element.70, bf16[1344,3072]{1,0:T(8,128)(2,1)} %get-tuple-element.71, f32[400,1344]{1,0:T(8,128)} %get-tuple-element.72), kind=kOutput, calls=%fused_computation.200 | convolution fusion | flops 6610867200 | bytes 23580672 | tf_op jit(solution)/shard_map/cond/branch_0_fun/dot_general | solution.py:125
  401.1 3.9 all-to-all-start.5
  410.6 3.5 collective-permute-start.7
  414.0 22.7 %all-to-all-done.5 = bf16[16,24,3200]{2,1,0:T(8,128)(2,1)S(1)} async-done(((bf16[16,24,3200]{2,1,0:T(8,128)(2,1)}), bf16[16,24,3200]{2,1,0:T(8,128)(2,1)S(1)}, u32[]{:S(2)}, u32[]{:S(2)}) %all-to-all-start.5) | async-done | bytes 2457632 | tf_op jit(solution)/shard_map/all_to_all | solution.py:84
  437.7 5.3 %collective-permute-start.15 = (bf16[64,3072]{1,0:T(8,128)(2,1)S(1)}, bf16[64,3072]{1,0:T(8,128)(2,1)S(1)}, u32[]{:S(2)}, u32[]{:S(2)}) collective-permute-start(bf16[64,3072]{1,0:T(8,128)(2,1)S(1)} %convolution_convert_fusion.4), channel_id=1, source_target_pairs={{0,3},{1,0},{2,1},{3,2},{4,7},{5,4},{6,5},{7,6},{8,11},{9,8},{10,9... | collective-permute-start | bytes 1179656 | tf_op jit(solution)/shard_map/ppermute | solution.py:95
  443.0 4.2 collective-permute-start.13
  448.9 10.7 %collective-permute-done.15 = bf16[64,3072]{1,0:T(8,128)(2,1)S(1)} collective-permute-done((bf16[64,3072]{1,0:T(8,128)(2,1)S(1)}, bf16[64,3072]{1,0:T(8,128)(2,1)S(1)}, u32[]{:S(2)}, u32[]{:S(2)}) %collective-permute-start.15) | collective-permute-done | bytes 393248 | tf_op jit(solution)/shard_map/ppermute | solution.py:95
  459.6 5.3 %collective-permute-done.13 = bf16[64,3072]{1,0:T(8,128)(2,1)S(1)} collective-permute-done((bf16[64,3072]{1,0:T(8,128)(2,1)S(1)}, bf16[64,3072]{1,0:T(8,128)(2,1)S(1)}, u32[]{:S(2)}, u32[]{:S(2)}) %collective-permute-start.13) | collective-permute-done | bytes 393248 | tf_op jit(solution)/shard_map/ppermute | solution.py:95
  468.4 9.4 %all_to_all.41 = f32[16,1,192]{2,1,0:T(1,128)S(1)} all-to-all(f32[16,1,192]{2,1,0:T(1,128)S(1)} %all_to_all.30), channel_id=1, replica_groups=mesh['section'=2,'dp'=16,'expert'=4] {'dp'}, dimensions={0} | all-to-all | bytes 24576 | tf_op jit(solution)/shard_map/all_to_all | solution.py:168
  (162 shorter events, 54.5 us)
Async XLA Ops:
  1.4 11.7 %collective-permute-start.1 = (bf16[3072]{0:T(1024)(128)(2,1)S(1)}, bf16[3072]{0:T(1024)(128)(2,1)S(1)}, u32[]{:S(2)}, u32[]{:S(2)}) collective-permute-start(bf16[3072]{0:T(1024)(128)(2,1)S(1)} %reduce.1), channel_id=1, source_target_pairs={{0,64},{64,0},{1,65},{65,1},{2,66},{66,2},{3,67},{67,3},{4,68},{68... | collective-permute-start | bytes 18440 | tf_op jit(solution)/shard_map/ppermute | solution.py:13
  3.6 1.9 collective-permute-start
  3.7 100.4 %collective-permute-start.2 = (bf16[1344,3072]{1,0:T(8,128)(2,1)}, bf16[1344,3072]{1,0:T(8,128)(2,1)}, u32[]{:S(2)}, u32[]{:S(2)}) collective-permute-start(bf16[1344,3072]{1,0:T(8,128)(2,1)} %bitcast.245), channel_id=1, source_target_pairs={{0,64},{64,0},{1,65},{65,1},{2,66},{66,2},{3,67},{67,3},{4,68},{68... | collective-permute-start | bytes 24772616 | tf_op jit(solution)/shard_map/ppermute | solution.py:13
  4.2 99.9 %collective-permute-start.3 = (bf16[1344,3072]{1,0:T(8,128)(2,1)}, bf16[1344,3072]{1,0:T(8,128)(2,1)}, u32[]{:S(2)}, u32[]{:S(2)}) collective-permute-start(bf16[1344,3072]{1,0:T(8,128)(2,1)} %bitcast.251), channel_id=1, source_target_pairs={{0,64},{64,0},{1,65},{65,1},{2,66},{66,2},{3,67},{67,3},{4,68},{68... | collective-permute-start | bytes 24772616 | tf_op jit(solution)/shard_map/ppermute | solution.py:13
  5.5 7.6 %copy-start.13 = (f32[64]{0:T(128)}, f32[64]{0:T(128)S(1)}, u32[]{:S(2)}) copy-start(f32[64]{0:T(128)S(1)} %add_rsqrt_fusion.1) | copy-start | bytes 772
  8.6 3.0 copy-start.7
  18.4 80.0 %all-to-all-start = ((bf16[16,48,3200]{2,1,0:T(8,128)(2,1)}), bf16[16,48,3200]{2,1,0:T(8,128)(2,1)}, u32[]{:S(2)}, u32[]{:S(2)}) async-start(bf16[16,48,3200]{2,1,0:T(8,128)(2,1)} %maximum_maximum_fusion), calls=%async_computation | async-start | bytes 9830400 | tf_op jit(solution)/shard_map/all_to_all | solution.py:84
  98.4 5.7 %slice-start.1 = ((s8[8257536]{0:T(1024)(128)(4,1)}), s8[4194304]{0:T(1024)(128)(4,1)S(1)}, s32[]{:S(2)}) async-start(s8[8257536]{0:T(1024)(128)(4,1)} %bitcast.248), calls=%async_computation.8 | async-start | bytes 8388608
  99.5 4.6 slice-start.2
  122.1 38.6 %all-to-all-start.1 = ((bf16[16,24,3200]{2,1,0:T(8,128)(2,1)}), bf16[16,24,3200]{2,1,0:T(8,128)(2,1)S(1)}, u32[]{:S(2)}, u32[]{:S(2)}) async-start(bf16[16,24,3200]{2,1,0:T(8,128)(2,1)} %pad_maximum_fusion.1), calls=%async_computation.1 | async-start | bytes 4915200 | tf_op jit(solution)/shard_map/all_to_all | solution.py:84
  161.0 24.1 %copy-start.2 = (bf16[2,64,3072]{2,1,0:T(8,128)(2,1)S(1)}, bf16[2,64,3072]{2,1,0:T(8,128)(2,1)}, u32[]{:S(2)}) copy-start(bf16[2,64,3072]{2,1,0:T(8,128)(2,1)} %param.17) | copy-start | bytes 2359300
  161.6 20.1 %collective-permute-start.6 = (bf16[64,3072]{1,0:T(8,128)(2,1)S(1)}, bf16[64,3072]{1,0:T(8,128)(2,1)S(1)}, u32[]{:S(2)}, u32[]{:S(2)}) collective-permute-start(bf16[64,3072]{1,0:T(8,128)(2,1)S(1)} %convolution_convert_fusion.7), channel_id=1, source_target_pairs={{0,3},{1,0},{2,1},{3,2},{4,7},{5,4},{6,5},{7,6},{8,11},{9,8},{10,9... | collective-permute-start | bytes 1179656 | tf_op jit(solution)/shard_map/ppermute | solution.py:95
  165.5 19.7 %collective-permute-start.5 = (bf16[64,3072]{1,0:T(8,128)(2,1)S(1)}, bf16[64,3072]{1,0:T(8,128)(2,1)S(1)}, u32[]{:S(2)}, u32[]{:S(2)}) collective-permute-start(bf16[64,3072]{1,0:T(8,128)(2,1)S(1)} %convolution_convert_fusion.7), channel_id=1, source_target_pairs={{0,1},{1,2},{2,3},{3,0},{4,5},{5,6},{6,7},{7,4},{8,9},{9,10},{10,1... | collective-permute-start | bytes 1179656 | tf_op jit(solution)/shard_map/ppermute | solution.py:95
  165.5 19.7 %collective-permute-start.4 = (bf16[64,3072]{1,0:T(8,128)(2,1)S(1)}, bf16[64,3072]{1,0:T(8,128)(2,1)S(1)}, u32[]{:S(2)}, u32[]{:S(2)}) collective-permute-start(bf16[64,3072]{1,0:T(8,128)(2,1)S(1)} %convolution_convert_fusion.7), channel_id=1, source_target_pairs={{0,2},{1,3},{2,0},{3,1},{4,6},{5,7},{6,4},{7,5},{8,10},{9,11},{10,... | collective-permute-start | bytes 1179656 | tf_op jit(solution)/shard_map/ppermute | solution.py:95
  188.3 39.5 %all-to-all-start.2 = ((bf16[16,24,3200]{2,1,0:T(8,128)(2,1)}), bf16[16,24,3200]{2,1,0:T(8,128)(2,1)S(1)}, u32[]{:S(2)}, u32[]{:S(2)}) async-start(bf16[16,24,3200]{2,1,0:T(8,128)(2,1)} %pad_maximum_fusion.2), calls=%async_computation.2 | async-start | bytes 4915200 | tf_op jit(solution)/shard_map/all_to_all | solution.py:84
  331.5 18.0 %copy-start.6 = (bf16[2,64,3072]{2,1,0:T(8,128)(2,1)S(1)}, bf16[2,64,3072]{2,1,0:T(8,128)(2,1)}, u32[]{:S(2)}) copy-start(bf16[2,64,3072]{2,1,0:T(8,128)(2,1)} %param.18) | copy-start | bytes 2359300
  332.1 10.9 %collective-permute-start.12 = (bf16[64,3072]{1,0:T(8,128)(2,1)S(1)}, bf16[64,3072]{1,0:T(8,128)(2,1)S(1)}, u32[]{:S(2)}, u32[]{:S(2)}) collective-permute-start(bf16[64,3072]{1,0:T(8,128)(2,1)S(1)} %convolution_convert_fusion.5), channel_id=1, source_target_pairs={{0,3},{1,0},{2,1},{3,2},{4,7},{5,4},{6,5},{7,6},{8,11},{9,8},{10,9... | collective-permute-start | bytes 1179656 | tf_op jit(solution)/shard_map/ppermute | solution.py:95
  332.2 16.3 %collective-permute-start.11 = (bf16[64,3072]{1,0:T(8,128)(2,1)S(1)}, bf16[64,3072]{1,0:T(8,128)(2,1)S(1)}, u32[]{:S(2)}, u32[]{:S(2)}) collective-permute-start(bf16[64,3072]{1,0:T(8,128)(2,1)S(1)} %convolution_convert_fusion.5), channel_id=1, source_target_pairs={{0,1},{1,2},{2,3},{3,0},{4,5},{5,6},{6,7},{7,4},{8,9},{9,10},{10,1... | collective-permute-start | bytes 1179656 | tf_op jit(solution)/shard_map/ppermute | solution.py:95
  333.6 14.9 %collective-permute-start.10 = (bf16[64,3072]{1,0:T(8,128)(2,1)S(1)}, bf16[64,3072]{1,0:T(8,128)(2,1)S(1)}, u32[]{:S(2)}, u32[]{:S(2)}) collective-permute-start(bf16[64,3072]{1,0:T(8,128)(2,1)S(1)} %convolution_convert_fusion.5), channel_id=1, source_target_pairs={{0,2},{1,3},{2,0},{3,1},{4,6},{5,7},{6,4},{7,5},{8,10},{9,11},{10,... | collective-permute-start | bytes 1179656 | tf_op jit(solution)/shard_map/ppermute | solution.py:95
  401.1 3.9 copy-start.8
  401.1 35.7 %all-to-all-start.5 = ((bf16[16,24,3200]{2,1,0:T(8,128)(2,1)}), bf16[16,24,3200]{2,1,0:T(8,128)(2,1)S(1)}, u32[]{:S(2)}, u32[]{:S(2)}) async-start(bf16[16,24,3200]{2,1,0:T(8,128)(2,1)} %pad_maximum_fusion.7), calls=%async_computation.5 | async-start | bytes 4915200 | tf_op jit(solution)/shard_map/all_to_all | solution.py:84
  407.9 35.1 %collective-permute-start.9 = (bf16[64,3072]{1,0:T(8,128)(2,1)}, bf16[64,3072]{1,0:T(8,128)(2,1)}, u32[]{:S(2)}, u32[]{:S(2)}) collective-permute-start(bf16[64,3072]{1,0:T(8,128)(2,1)} %convolution_convert_fusion.6), channel_id=1, source_target_pairs={{0,3},{1,0},{2,1},{3,2},{4,7},{5,4},{6,5},{7,6},{8,11},{9,8},{10,9... | collective-permute-start | bytes 1179656 | tf_op jit(solution)/shard_map/ppermute | solution.py:95
  410.5 36.6 %collective-permute-start.8 = (bf16[64,3072]{1,0:T(8,128)(2,1)}, bf16[64,3072]{1,0:T(8,128)(2,1)}, u32[]{:S(2)}, u32[]{:S(2)}) collective-permute-start(bf16[64,3072]{1,0:T(8,128)(2,1)} %convolution_convert_fusion.6), channel_id=1, source_target_pairs={{0,1},{1,2},{2,3},{3,0},{4,5},{5,6},{6,7},{7,4},{8,9},{9,10},{10,1... | collective-permute-start | bytes 1179656 | tf_op jit(solution)/shard_map/ppermute | solution.py:95
  410.6 36.6 %collective-permute-start.7 = (bf16[64,3072]{1,0:T(8,128)(2,1)}, bf16[64,3072]{1,0:T(8,128)(2,1)}, u32[]{:S(2)}, u32[]{:S(2)}) collective-permute-start(bf16[64,3072]{1,0:T(8,128)(2,1)} %convolution_convert_fusion.6), channel_id=1, source_target_pairs={{0,2},{1,3},{2,0},{3,1},{4,6},{5,7},{6,4},{7,5},{8,10},{9,11},{10,... | collective-permute-start | bytes 1179656 | tf_op jit(solution)/shard_map/ppermute | solution.py:95
  437.1 27.8 %copy-start.3 = (bf16[2,64,3072]{2,1,0:T(8,128)(2,1)S(1)}, bf16[2,64,3072]{2,1,0:T(8,128)(2,1)}, u32[]{:S(2)}) copy-start(bf16[2,64,3072]{2,1,0:T(8,128)(2,1)} %param.17) | copy-start | bytes 2359300
  437.1 27.7 %copy-start.11 = (f32[3072]{0:T(1024)S(1)}, f32[3072]{0:T(1024)}, u32[]{:S(2)}) copy-start(f32[3072]{0:T(1024)} %copy-done.10) | copy-start | bytes 36868
  437.1 27.7 %copy-start.14 = (f32[64]{0:T(128)S(1)}, f32[64]{0:T(128)}, u32[]{:S(2)}) copy-start(f32[64]{0:T(128)} %copy-done.13) | copy-start | bytes 772
  437.7 21.9 %collective-permute-start.15 = (bf16[64,3072]{1,0:T(8,128)(2,1)S(1)}, bf16[64,3072]{1,0:T(8,128)(2,1)S(1)}, u32[]{:S(2)}, u32[]{:S(2)}) collective-permute-start(bf16[64,3072]{1,0:T(8,128)(2,1)S(1)} %convolution_convert_fusion.4), channel_id=1, source_target_pairs={{0,3},{1,0},{2,1},{3,2},{4,7},{5,4},{6,5},{7,6},{8,11},{9,8},{10,9... | collective-permute-start | bytes 1179656 | tf_op jit(solution)/shard_map/ppermute | solution.py:95
  443.0 16.6 %collective-permute-start.14 = (bf16[64,3072]{1,0:T(8,128)(2,1)S(1)}, bf16[64,3072]{1,0:T(8,128)(2,1)S(1)}, u32[]{:S(2)}, u32[]{:S(2)}) collective-permute-start(bf16[64,3072]{1,0:T(8,128)(2,1)S(1)} %convolution_convert_fusion.4), channel_id=1, source_target_pairs={{0,1},{1,2},{2,3},{3,0},{4,5},{5,6},{6,7},{7,4},{8,9},{9,10},{10,1... | collective-permute-start | bytes 1179656 | tf_op jit(solution)/shard_map/ppermute | solution.py:95
  443.0 21.8 %collective-permute-start.13 = (bf16[64,3072]{1,0:T(8,128)(2,1)S(1)}, bf16[64,3072]{1,0:T(8,128)(2,1)S(1)}, u32[]{:S(2)}, u32[]{:S(2)}) collective-permute-start(bf16[64,3072]{1,0:T(8,128)(2,1)S(1)} %convolution_convert_fusion.4), channel_id=1, source_target_pairs={{0,2},{1,3},{2,0},{3,1},{4,6},{5,7},{6,4},{7,5},{8,10},{9,11},{10,... | collective-permute-start | bytes 1179656 | tf_op jit(solution)/shard_map/ppermute | solution.py:95
  465.9 12.5 %collective-permute-start.16 = (bf16[2,64,3072]{2,1,0:T(8,128)(2,1)S(1)}, bf16[2,64,3072]{2,1,0:T(8,128)(2,1)S(1)}, u32[]{:S(2)}, u32[]{:S(2)}) collective-permute-start(bf16[2,64,3072]{2,1,0:T(8,128)(2,1)S(1)} %pad_maximum_fusion.10), channel_id=1, source_target_pairs={{0,64},{64,0},{1,65},{65,1},{2,66},{66,2},{3,67},{67,3},{4,68},{68... | collective-permute-start | bytes 2359304 | tf_op jit(solution)/shard_map/ppermute | solution.py:13
  466.4 1.9 collective-permute-start.17
  (8 other events, 12.3 us)

commit v2 on v1

v2 whole, which is shorter than its diff:
```python
import functools

import jax
import jax.numpy as jnp
from jax import lax
from jax.experimental import pallas as pl
from jax.experimental.pallas import tpu as pltpu
from jax.sharding import PartitionSpec as P

EPSILON = 1e-05
SWAP = [(0, 1), (1, 0)]
LANES = 128
HIDDEN_STEP = 512
WIDTH_STEP = 512
VMEM_BYTES = 48 * 1024 * 1024
bf16, f32 = jnp.bfloat16, jnp.float32


def load_rows(held, rows, tails):
    owners, whole, wide = held.shape
    width = wide - LANES
    main = owners * whole
    rows[0:main, :] = held[:, :, 0:width].reshape(main, width)
    tails[...] = held[:, :, width:wide].astype(f32)
    for c in range(width // LANES):
        rows[main : main + owners, c * LANES : (c + 1) * LANES] = tails[:, c, :].astype(bf16)


def store_columns(out, tails, start, value):
    owners, whole, wide = out.shape
    main = owners * whole
    size = value.shape[1]
    out[:, :, start : start + size] = value[:main].astype(bf16).reshape(owners, whole, size)
    for c in range(size // LANES):
        tails[:, start // LANES + c, :] = value[main:, c * LANES : (c + 1) * LANES]


def store_tails(out, tails):
    wide = out.shape[2]
    out[:, :, wide - LANES : wide] = tails[...].astype(bf16)


def by_units(rows, weights):
    return lax.dot_general(rows, weights, (((1,), (1,)), ((), ())), preferred_element_type=f32)


def sigmoid(v):
    return 1.0 / (1.0 + jnp.exp(-v))


def chunks(size, step):
    return [(s, min(step, size - s)) for s in range(0, size, step)]


def expert_kernel(mode, layer, *refs):
    n_in = {"forward": 1, "backward": 3, "both": 2}[mode]
    n_out = 2
    helds, refs = refs[:n_in], refs[n_in:]
    own_hbm, other_hbm, refs = refs[:2], refs[2:4], refs[4:]
    outs, refs = refs[:n_out], refs[n_out:]
    up, down, rows, pre, act, tails, up_sem, down_sem = refs
    hidden, width = up.shape
    units = chunks(hidden, HIDDEN_STEP)
    columns = chunks(width, WIDTH_STEP)
    first, second = (down, up) if mode == "backward" else (up, down)

    def copies(src, dst, sem):
        return [
            pltpu.make_async_copy(src.at[pl.ds(s, n), :], dst.at[pl.ds(s, n), :], sem.at[i])
            for i, (s, n) in enumerate(units)
        ]

    def planned(pair):
        up_copies = copies(pair[0], up, up_sem)
        down_copies = copies(pair[1], down, down_sem)
        return (down_copies + up_copies) if mode == "backward" else (up_copies + down_copies)

    mine = lax.axis_index("section") == layer
    order = planned(own_hbm)

    @pl.when(mine)
    def _():
        for copy in order:
            copy.start()

    @pl.when(jnp.logical_not(mine))
    def _():
        for copy in planned(other_hbm):
            copy.start()

    early, late = order[: len(units)], order[len(units) :]

    load_rows(helds[0], rows, tails)
    for (s, n), copy in zip(units, early):
        copy.wait()
        v = by_units(rows[...], first[s : s + n, :])
        if mode == "backward":
            p = helds[1][:, s : s + n].astype(f32)
            g = sigmoid(p)
            act[:, s : s + n] = (v * g * (1.0 + p * (1.0 - g))).astype(bf16)
        else:
            pre[:, s : s + n] = v
            act[:, s : s + n] = (v * sigmoid(v)).astype(bf16)
    for copy in late:
        copy.wait()
    if mode == "backward":
        load_rows(helds[2], rows, tails)
    for s, n in columns:
        value = jnp.dot(act[...], second[:, s : s + n], preferred_element_type=f32)
        store_columns(outs[0], tails, s, value)
        if mode == "backward":
            terms = value * rows[:, s : s + n].astype(f32)
            outs[1][:, s : s + n] = jnp.sum(terms, axis=0, keepdims=True)
    store_tails(outs[0], tails)
    if mode == "forward":
        outs[1][...] = pre[...]
    if mode == "both":
        load_rows(helds[1], rows, tails)
        for s, n in units:
            v = by_units(rows[...], down[s : s + n, :])
            p = pre[:, s : s + n]
            g = sigmoid(p)
            act[:, s : s + n] = (v * g * (1.0 + p * (1.0 - g))).astype(bf16)
        for s, n in columns:
            store_columns(
                outs[1], tails, s, jnp.dot(act[...], up[:, s : s + n], preferred_element_type=f32)
            )
        store_tails(outs[1], tails)


def expert(mode, layer, weights, *inputs):
    hidden, width = weights[0].shape
    held = inputs[0]
    owners, whole, wide = held.shape
    count = owners * (whole + 1)
    block = jax.ShapeDtypeStruct(held.shape, bf16)
    kept = jax.ShapeDtypeStruct((count, hidden), f32)
    summed = jax.ShapeDtypeStruct((1, width), f32)
    out_shape = {"forward": [block, kept], "backward": [block, summed], "both": [block, block]}
    out_shape = out_shape[mode]
    vmem = pl.BlockSpec(memory_space=pltpu.VMEM)
    anywhere = pl.BlockSpec(memory_space=pl.ANY)
    steps = len(chunks(hidden, HIDDEN_STEP))
    n_mm = 4 if mode == "both" else 2
    return pl.pallas_call(
        functools.partial(expert_kernel, mode, layer),
        out_shape=out_shape,
        in_specs=[vmem] * len(inputs) + [anywhere] * 4,
        out_specs=[vmem] * len(out_shape),
        scratch_shapes=[
            pltpu.VMEM((hidden, width), bf16),
            pltpu.VMEM((hidden, width), bf16),
            pltpu.VMEM((count, width), bf16),
            pltpu.VMEM((count, hidden), f32),
            pltpu.VMEM((count, hidden), bf16),
            pltpu.VMEM((owners, whole, LANES), f32),
            pltpu.SemaphoreType.DMA((steps,)),
            pltpu.SemaphoreType.DMA((steps,)),
        ],
        compiler_params=pltpu.CompilerParams(vmem_limit_bytes=VMEM_BYTES),
        cost_estimate=pl.CostEstimate(
            flops=2 * n_mm * count * hidden * width,
            bytes_accessed=4 * hidden * width + 4 * count * width,
            transcendentals=count * hidden,
        ),
        name="expert_" + mode,
    )(*inputs, *weights)


def tables_kernel(top, whole, packed, plain, weighted):
    row_count, count = plain.shape
    owners = count // (whole + 1)
    main = owners * whole
    own_lane = lax.broadcasted_iota(jnp.int32, (row_count, owners), 1)
    hot = jnp.zeros((row_count, owners), f32)
    share = jnp.zeros((row_count, owners), f32)
    total = jnp.zeros((row_count, 1), f32)
    counts = packed[:, top : top + 1]
    for k in range(top):
        named = packed[:, k : k + 1] == own_lane
        fixed = packed[:, top + 1 + k : top + 2 + k].astype(f32)
        fixed = jnp.where(counts > k, fixed, 0.0)
        hot = hot + jnp.where(named, 1.0, 0.0)
        share = share + jnp.where(named, fixed, 0.0)
        total = total + fixed
    share = share / total
    owner = lax.broadcasted_iota(jnp.int32, (owners, count), 0)
    column = lax.broadcasted_iota(jnp.int32, (owners, count), 1)
    place = column - owner * whole
    inside = (place >= 0) & (place < whole) & (column < main)
    spread = jnp.where(inside | (column - main == owner), 1.0, 0.0)
    place = jnp.sum(jnp.where(inside, place, 0).astype(f32), axis=0, keepdims=True)
    last = lax.broadcasted_iota(jnp.int32, (1, count), 1) >= main
    place = jnp.where(last, float(whole), place)
    spread = spread.astype(bf16)
    row = lax.broadcasted_iota(jnp.int32, (row_count, row_count), 0)
    earlier = lax.broadcasted_iota(jnp.int32, (row_count, row_count), 1) < row
    below = jnp.where(earlier, 1.0, 0.0).astype(bf16)
    before = jnp.dot(below, hot.astype(bf16), preferred_element_type=f32)
    hot_c = jnp.dot(hot.astype(bf16), spread, preferred_element_type=f32)
    before_c = jnp.dot(before.astype(bf16), spread, preferred_element_type=f32)
    share_c = jnp.dot(share.astype(bf16), spread, preferred_element_type=f32)
    chosen = jnp.where(before_c == place, hot_c, 0.0)
    plain[...] = chosen.astype(bf16)
    weighted[...] = (chosen * share_c).astype(bf16)


def pallas(kernel, out_shape, scratch, name, *inputs, awaits=()):
    vmem = pl.BlockSpec(memory_space=pltpu.VMEM)

    def body(*refs):
        awaited, refs = refs[len(inputs) : len(inputs) + len(awaits)], (
            refs[: len(inputs)] + refs[len(inputs) + len(awaits) :]
        )
        if awaited:
            refs, (tile, sem) = refs[:-2], refs[-2:]
        for ref in awaited:
            copy = pltpu.make_async_copy(ref.at[pl.ds(0, 16), pl.ds(0, LANES)], tile, sem)
            copy.start()
            copy.wait()
        kernel(*refs)

    if awaits:
        scratch = [*scratch, pltpu.VMEM((16, LANES), bf16), pltpu.SemaphoreType.DMA(())]

    return pl.pallas_call(
        body,
        out_shape=out_shape,
        in_specs=[vmem] * len(inputs) + [pl.BlockSpec(memory_space=pl.ANY)] * len(awaits),
        out_specs=jax.tree.map(lambda _: vmem, out_shape),
        scratch_shapes=scratch,
        compiler_params=pltpu.CompilerParams(vmem_limit_bytes=VMEM_BYTES),
        name=name,
    )(*inputs, *awaits)


def pack(table, rows, out, tails):
    width = rows.shape[1]
    for s, n in chunks(width, WIDTH_STEP):
        value = lax.dot_general(
            table[...], rows[:, s : s + n], (((0,), (0,)), ((), ())), preferred_element_type=f32
        )
        store_columns(out, tails, s, value)
    store_tails(out, tails)


def normed(state_f):
    mean = jnp.mean(state_f * state_f, axis=-1, keepdims=True)
    inverse_rms = lax.rsqrt(mean + EPSILON)
    return state_f * inverse_rms, inverse_rms


def four(parts):
    own, far, left, right = (p[...].astype(f32) for p in parts)
    return (own + far) + (left + right)


def plain_kernel(rows, table, out, tails):
    pack(table, rows, out, tails)


def norm_kernel(x, gain, table, out, rows, tails):
    rows[...] = (normed(x[...].astype(f32))[0] * gain[...]).astype(bf16)
    pack(table, rows, out, tails)


def sum_norm_kernel(x, p0, p1, p2, p3, gain, table, following, out, rows, tails):
    following[...] = (x[...].astype(f32) + four((p0, p1, p2, p3))).astype(bf16)
    rows[...] = (normed(following[...].astype(f32))[0] * gain[...]).astype(bf16)
    pack(table, rows, out, tails)


def finish(x, upstream, parts, gain, grad, gain_grad=None):
    d_norm = four(parts)
    scaled, inverse_rms = normed(x[...].astype(f32))
    d_scaled = d_norm * gain[...]
    mean = jnp.mean(d_scaled * scaled, axis=-1, keepdims=True)
    d_input = inverse_rms * (d_scaled - scaled * mean)
    grad[...] = (upstream[...].astype(f32) + d_input).astype(bf16)
    if gain_grad is not None:
        gain_grad[...] = jnp.sum(d_norm * scaled, axis=0, keepdims=True)


def finish_kernel(x, upstream, p0, p1, p2, p3, gain, grad):
    finish(x, upstream, (p0, p1, p2, p3), gain, grad)


def finish_pack_kernel(x, upstream, p0, p1, p2, p3, gain, table, grad, gain_grad, out, tails):
    finish(x, upstream, (p0, p1, p2, p3), gain, grad, gain_grad)
    pack(table, grad, out, tails)


def home_kernel(table, held, out, tails):
    owners, whole, wide = held.shape
    width = wide - LANES
    main = owners * whole
    tails[...] = held[:, :, width:wide].astype(f32)
    for s, n in chunks(width, WIDTH_STEP):
        rows = held[:, :, s : s + n].reshape(main, n)
        last = [tails[:, (s // LANES) + c, :] for c in range(n // LANES)]
        last = jnp.concatenate(last, axis=1).astype(bf16)
        value = jnp.dot(table[:, :main], rows, preferred_element_type=f32)
        value = value + jnp.dot(table[:, main:], last, preferred_element_type=f32)
        out[:, s : s + n] = value.astype(bf16)


def swapped(x):
    return lax.ppermute(x, "section", SWAP)


def after(value, first_done):
    return lax.optimization_barrier((value, first_done))[0]


def shards(inputs, cotangent, gain, w_up, w_down, expert_ids, expert_counts, combine_fixed):
    section = lax.axis_index("section")
    owners = lax.axis_size("dp")
    ring = lax.axis_size("expert")
    row_count, width = inputs.shape[1:]
    top = expert_ids.shape[3]
    capacity = min(row_count, row_count * top // owners + 1)
    whole = capacity - 1
    count = owners * capacity
    first = section == 0
    up_own, down_own = w_up[0, 0], w_down[0, 0]

    def like(*shape, dtype=bf16):
        return jax.ShapeDtypeStruct(shape, dtype)

    block = like(owners, whole, width + LANES)
    rows_shape = like(row_count, width)
    gain_shape = like(1, width, dtype=f32)
    table_shape = like(row_count, count)
    tails = pltpu.VMEM((owners, whole, LANES), f32)
    rows = pltpu.VMEM((row_count, width), bf16)

    def pick(mine, other, layer):
        return jnp.where(section == layer, mine, other)

    ints = jnp.concatenate([expert_ids[0], expert_counts[0][..., None], combine_fixed[0]], axis=-1)
    mine = lax.dynamic_index_in_dim(ints, section, 0, keepdims=False)
    theirs = swapped(lax.dynamic_index_in_dim(ints, 1 - section, 0, keepdims=False))
    gain_own = gain.astype(f32)
    gain_other = swapped(gain_own)
    x0 = lax.dynamic_index_in_dim(inputs, section, 0, keepdims=False)
    upstream = lax.dynamic_index_in_dim(cotangent, section, 0, keepdims=False)
    up_other, down_other = swapped(up_own), swapped(down_own)

    def tables(packed):
        kernel = functools.partial(tables_kernel, top, whole)
        return pallas(kernel, [table_shape, table_shape], [], "tables", packed)

    def exchange(held):
        return lax.all_to_all(held, "dp", split_axis=0, concat_axis=0, tiled=True)

    def over_groups(part):
        pairs = [[(i, (i + by) % ring) for i in range(ring)] for by in (2, 1, 3)]
        return (part, *[lax.ppermute(part, "expert", p) for p in pairs])

    def home(table, held):
        return over_groups(pallas(home_kernel, rows_shape, [tails], "home", table, held))

    weights = (up_own, down_own, up_other, down_other)

    def enter(current, gain_row, table, *awaits):
        args = (current, gain_row, table)
        return exchange(pallas(norm_kernel, block, [rows, tails], "enter", *args, awaits=awaits))

    own_tables = tables(mine)
    rows0 = lax.cond(
        first,
        enter,
        lambda *a: jnp.zeros(block.shape, bf16),
        x0,
        gain_own,
        own_tables[0],
    )
    other_tables = tables(theirs)
    rows0 = lax.cond(
        first,
        lambda kept, *a: kept,
        lambda kept, *a: enter(*a),
        rows0,
        x0,
        gain_other,
        other_tables[0],
        up_other,
        down_other,
    )
    gain0, gain1 = (pick(gain_own, gain_other, layer) for layer in range(2))
    plain0, plain1 = (pick(own_tables[0], other_tables[0], layer) for layer in range(2))
    weighted0, weighted1 = (pick(own_tables[1], other_tables[1], layer) for layer in range(2))
    d_held1 = pallas(plain_kernel, block, [tails], "spread", upstream, weighted1)

    part0, pre0 = expert("forward", 0, weights, rows0)
    back0 = exchange(part0)
    d_rows1 = exchange(after(d_held1, back0))
    sums0 = home(weighted0, back0)
    x1, held1 = pallas(
        sum_norm_kernel, [rows_shape, block], [rows, tails], "next", x0, *sums0, gain1, plain1
    )
    rows1 = exchange(after(held1, d_rows1))
    part1, d_part1 = expert("both", 1, weights, rows1, d_rows1)
    d_back1 = exchange(d_part1)
    back1 = exchange(after(part1, d_back1))
    d_sums1 = home(plain1, d_back1)
    grad1, gain_grad1, d_held0 = pallas(
        finish_pack_kernel,
        [rows_shape, gain_shape, block],
        [tails],
        "finish_next",
        x1,
        upstream,
        *d_sums1,
        gain1,
        weighted0,
    )
    d_rows0 = exchange(after(d_held0, back1))
    d_part0, gain_part0 = expert("backward", 0, weights, d_rows0, pre0, rows0)
    x2 = (x1.astype(f32) + four(home(weighted1, back1))).astype(bf16)
    d_back0 = exchange(d_part0)

    gain_part0 = gain_part0 / gain0
    gain_part1 = jnp.where(lax.axis_index("expert") == 0, gain_grad1, 0.0)
    slices = jnp.stack([gain_part0, gain_part1]).reshape(2, owners, width // owners)
    slices = jnp.broadcast_to(slices.transpose(1, 0, 2)[:, None], (owners, ring, 2, width // owners))
    slices = after(slices, d_back0).reshape(owners * ring, 2, width // owners)
    slices = lax.all_to_all(slices, ("dp", "expert"), split_axis=0, concat_axis=0, tiled=True)
    slices = jnp.sum(slices, axis=0)

    grad0 = pallas(finish_kernel, rows_shape, [], "finish", x0, grad1, *home(plain0, d_back0), gain0)

    gain_sum = pick(slices[0], slices[1], 0) + swapped(pick(slices[1], slices[0], 0))
    kept_x, taken_x = pick(x1, x2, 0), swapped(pick(x2, x1, 0))
    kept_g, taken_g = pick(grad0, grad1, 0), swapped(pick(grad1, grad0, 0))

    def both(kept, taken):
        low, high = jnp.where(first, kept, taken), jnp.where(first, taken, kept)
        return jnp.stack([low, high])[None]

    return both(kept_x, taken_x), both(kept_g, taken_g), gain_sum[None]


def solution(mesh):
    return jax.shard_map(
        shards,
        mesh=mesh,
        in_specs=(
            P(None, "dp", None),
            P(None, "dp", None),
            P("section", None),
            P("section", "dp", "expert", None),
            P("section", "dp", "expert", None),
            P("section", None, "dp", None),
            P("section", None, "dp"),
            P("section", None, "dp", None),
        ),
        out_specs=(
            P("section", None, "dp", None),
            P("section", None, "dp", None),
            P("section", "dp"),
        ),
        check_vma=False,
    )
```

time: 488 us -> 371 us (0.76)
  waiting for transfers between devices: 213 us -> 99.2 us
  matrix products: 75.1 us -> 0 us
  Pallas kernels: 0 us -> 70.5 us
  blocking collectives: 98.5 us -> 139 us
  other arithmetic: 22.5 us -> 8.09 us
  loops' own time: 8.96 us -> 0.02 us
  starting transfers between devices: 44.5 us -> 36.2 us
  local copies, waits for them, and re-layouts: 16.3 us -> 11.4 us
    all_to_all x4 -> x3, waiting for transfers between devices: 162 us -> 36.6 us  [exchange(): return lax.all_to_all(held, 'dp', split_axis=0, concat_axis=0, tiled=True)]
    dot_general x20 -> x0, matrix products: 75.1 us -> none  [the longest x2 30 us: backward(): return jnp.dot(d_pre, up, preferred_element_type=f32).astype(bf16)]
    pallas_call x0 -> x14, Pallas kernels: none -> 70.5 us  [the longest x3 55.9 us: expert(): pl.pallas_call(functools.partial(expert_kernel, mode, layer), out_shape=o...]
    all_to_all x3 -> x6, blocking collectives: 98.5 us -> 139 us  [the longest x5 127 us: exchange(): return lax.all_to_all(held, 'dp', split_axis=0, concat_axis=0, tiled=True)]
    ppermute x6 -> x7, waiting for transfers between devices: 1.79 us -> 20.2 us  [swapped(): return lax.ppermute(x, 'section', SWAP)]
    concatenate x10 -> x0, other arithmetic: 13.1 us -> none  [the longest x4 5.26 us: unblocks(): return jnp.concatenate([head, tail], axis=0)]
    slice x23 -> x0, local copies, waits for them, and re-layouts: 11.2 us -> none  [the longest x6 7.39 us: unblocks(): head = held[:, :, :width].reshape(main_rows, width)]
    unnamed x3 -> x0, loops' own time: 8.96 us -> none
  transfers between devices with their start and end apart: 22 -> 22, of which waited for: 11 -> 14; matrix products, arithmetic and copies ran while one was open for 6% -> 2% of each run, Pallas kernels for 0% -> 3%
where the time goes in v2:
time: 371 us; the launch traced here: 366 us
  blocking collectives  139 us (37%)
  waiting for transfers between devices  99.2 us (27%)
  Pallas kernels  70.5 us (19%)
  starting transfers between devices  36.2 us (10%)
  local copies, waits for them, and re-layouts  11.4 us (3%)
  other arithmetic  8.09 us (2%)
    all_to_all x5, blocking collectives, exchange(): return lax.all_to_all(held, 'dp', split_axis=0, concat_axis=0, tiled=True)  127 us
    pallas_call x3, Pallas kernels, expert(): pl.pallas_call(functools.partial(expert_kernel, mode, layer), out_shape=o...  55.9 us
    ppermute x12, waiting for transfers between devices, over_groups(): return (part, *[lax.ppermute(part, 'expert', p) for p in pairs])  42.3 us
    all_to_all x3, waiting for transfers between devices, exchange(): return lax.all_to_all(held, 'dp', split_axis=0, concat_axis=0, tiled=True)  36.6 us
    ppermute x7, waiting for transfers between devices, swapped(): return lax.ppermute(x, 'section', SWAP)  20.2 us
    ppermute x12, starting transfers between devices, over_groups(): return (part, *[lax.ppermute(part, 'expert', p) for p in pairs])  18.3 us
    pallas_call x11, Pallas kernels, pallas(): pl.pallas_call(body, out_shape=out_shape, in_specs=[vmem] * len(inputs) +...  14.6 us
    all_to_all x3, starting transfers between devices, exchange(): return lax.all_to_all(held, 'dp', split_axis=0, concat_axis=0, tiled=True)  13.7 us
  transfers between devices with their start and end apart: 22, of which 14 were waited for; matrix products, arithmetic and copies ran while one was open for 2% of the time, Pallas kernels for 3%

profile of v2, /device:TPU:1, one launch (start us, length us, event | category | flops | bytes accessed | tf_op | source)
XLA Modules:
  0.0 365.8 jit_solution(5557559891448459111)
XLA Ops:
  7.1 7.7 %collective-permute-done.refs_0_ = s32[64,13]{1,0:T(8,128)S(1)} collective-permute-done((s32[64,13]{1,0:T(8,128)S(1)}, s32[64,13]{1,0:T(8,128)S(1)}, u32[]{:S(2)}, u32[]{:S(2)}) %collective-permute-start) | collective-permute-done | bytes 3360 | tf_op jit(solution)/shard_map/ppermute | solution.py:308
  15.3 11.6 %collective-permute-done.3.refs_4_.refs_5_.refs_6_ = bf16[1344,3072]{1,0:T(8,128)(2,1)} collective-permute-done((bf16[1344,3072]{1,0:T(8,128)(2,1)}, bf16[1344,3072]{1,0:T(8,128)(2,1)}, u32[]{:S(2)}, u32[]{:S(2)}) %collective-permute-start.3) | collective-permute-done | bytes 8257568 | tf_op jit(solution)/shard_map/ppermute | solution.py:308
  27.0 28.6 %conditional.3 = (bf16[16,24,3200]{2,1,0:T(8,128)(2,1)}) conditional(s32[]{:T(128)} %convert_element_type.25, (bf16[64,3072]{1,0:T(8,128)(2,1)S(1)}, f32[1,3072]{1,0:T(1,128)S(1)}, bf16[64,400]{1,0:T(8,128)(2,1)S(1)}, bf16[1344,3072]{1,0:T(8,128)(2,1)}, bf16[1344,3072]{1,0:T(8,128)(2,1)}) %tuple.25, bf16[16,24,3200]{2,1,0:T(8,128)(2,1)} %get-tuple-element.91), branch_computations={%region_2.3_spmd, %region_3.4_spmd} | conditional | bytes 4915208 | solution.py:379
  27.0 2.4 enter.3
  29.3 26.3 %all_to_all.49 = bf16[16,24,3200]{2,1,0:T(8,128)(2,1)} all-to-all(bf16[16,24,3200]{2,1,0:T(8,128)(2,1)S(1)} %enter.3), channel_id=1, replica_groups=mesh['section'=2,'dp'=16,'expert'=4] {'dp'}, dimensions={0} | all-to-all | bytes 4915200 | tf_op jit(solution)/shard_map/cond/branch_0_fun/all_to_all | solution.py:354
  55.6 12.8 %expert_forward.1 = (bf16[16,24,3200]{2,1,0:T(8,128)(2,1)S(1)}, f32[400,1344]{1,0:T(8,128)S(1)}) custom-call(bf16[16,24,3200]{2,1,0:T(8,128)(2,1)} %get-tuple-element.92.refs_0_.refs_2_, bf16[1344,3072]{1,0:T(8,128)(2,1)} %bitcast.31, bf16[1344,3072]{1,0:T(8,128)(2,1)} %bitcast.35, bf16[1344,3072]{1,0:T(8,128)(2,1)} %collective-permute-done.2.refs_3_.refs_4_.refs_5_, ...), custom_call_target="tpu_custom_call" | custom-call | flops 6606028800 | bytes 21430272 | tf_op jit(solution)/shard_map/expert_forward/pallas_call | solution.py:145
  71.3 3.9 %all-to-all-start.2 = ((bf16[16,24,3200]{2,1,0:T(8,128)(2,1)}), bf16[16,24,3200]{2,1,0:T(8,128)(2,1)S(1)}, u32[]{:S(2)}, u32[]{:S(2)}) async-start(bf16[16,24,3200]{2,1,0:T(8,128)(2,1)} %copy-done.6), calls=%async_computation.2 | async-start | bytes 4915200 | tf_op jit(solution)/shard_map/all_to_all | solution.py:354
  75.2 2.3 spread.1
  78.3 23.6 %all-to-all-done.2.refs_1_ = bf16[16,24,3200]{2,1,0:T(8,128)(2,1)S(1)} async-done(((bf16[16,24,3200]{2,1,0:T(8,128)(2,1)}), bf16[16,24,3200]{2,1,0:T(8,128)(2,1)S(1)}, u32[]{:S(2)}, u32[]{:S(2)}) %all-to-all-start.2) | async-done | bytes 2457632 | tf_op jit(solution)/shard_map/all_to_all | solution.py:354
  101.9 6.1 %all-to-all-start.3 = ((bf16[16,24,3200]{2,1,0:T(8,128)(2,1)}), bf16[16,24,3200]{2,1,0:T(8,128)(2,1)}, u32[]{:S(2)}, u32[]{:S(2)}) async-start(bf16[16,24,3200]{2,1,0:T(8,128)(2,1)} %spread.1), calls=%async_computation.3 | async-start | bytes 4915200 | tf_op jit(solution)/shard_map/all_to_all | solution.py:354
  108.7 3.9 %collective-permute-start.6 = (bf16[64,3072]{1,0:T(8,128)(2,1)S(1)}, bf16[64,3072]{1,0:T(8,128)(2,1)S(1)}, u32[]{:S(2)}, u32[]{:S(2)}) collective-permute-start(bf16[64,3072]{1,0:T(8,128)(2,1)S(1)} %home.4.refs_1_), channel_id=1, source_target_pairs={{0,3},{1,0},{2,1},{3,2},{4,7},{5,4},{6,5},{7,6},{8,11},{9,8},{10,9... | collective-permute-start | bytes 1179656 | tf_op jit(solution)/shard_map/ppermute | solution.py:358
  113.9 7.6 %collective-permute-done.6.refs_4_ = bf16[64,3072]{1,0:T(8,128)(2,1)S(1)} collective-permute-done((bf16[64,3072]{1,0:T(8,128)(2,1)S(1)}, bf16[64,3072]{1,0:T(8,128)(2,1)S(1)}, u32[]{:S(2)}, u32[]{:S(2)}) %collective-permute-start.6) | collective-permute-done | bytes 393248 | tf_op jit(solution)/shard_map/ppermute | solution.py:358
  121.5 3.5 collective-permute-done.5.refs_3_
  126.4 9.6 %all-to-all-done.3.refs_1_ = bf16[16,24,3200]{2,1,0:T(8,128)(2,1)} async-done(((bf16[16,24,3200]{2,1,0:T(8,128)(2,1)}), bf16[16,24,3200]{2,1,0:T(8,128)(2,1)}, u32[]{:S(2)}, u32[]{:S(2)}) %all-to-all-start.3) | async-done | bytes 2457632 | tf_op jit(solution)/shard_map/all_to_all | solution.py:354
  136.0 22.9 %all_to_all.50.refs_0_ = bf16[16,24,3200]{2,1,0:T(8,128)(2,1)} all-to-all(bf16[16,24,3200]{2,1,0:T(8,128)(2,1)S(1)} %get-tuple-element.62), channel_id=1, replica_groups=mesh['section'=2,'dp'=16,'expert'=4] {'dp'}, dimensions={0} | all-to-all | bytes 4915200 | tf_op jit(solution)/shard_map/all_to_all | solution.py:354
  158.8 30.2 %expert_both.1 = (bf16[16,24,3200]{2,1,0:T(8,128)(2,1)S(1)}, bf16[16,24,3200]{2,1,0:T(8,128)(2,1)S(1)}) custom-call(bf16[16,24,3200]{2,1,0:T(8,128)(2,1)} %all_to_all.50.refs_0_, bf16[16,24,3200]{2,1,0:T(8,128)(2,1)} %all-to-all-done.3.refs_1_, bf16[1344,3072]{1,0:T(8,128)(2,1)} %bitcast.32, bf16[1344,3072]{1,0:T(8,128)(2,1)} %bitcast.36, ...), custom_call_target="tpu_custom_call" | custom-call | flops 13212057600 | bytes 21430272 | tf_op jit(solution)/shard_map/expert_both/pallas_call | solution.py:145
  189.1 28.9 %all_to_all.51.refs_1_ = bf16[16,24,3200]{2,1,0:T(8,128)(2,1)} all-to-all(bf16[16,24,3200]{2,1,0:T(8,128)(2,1)S(1)} %get-tuple-element.64), channel_id=1, replica_groups=mesh['section'=2,'dp'=16,'expert'=4] {'dp'}, dimensions={0} | all-to-all | bytes 4915200 | tf_op jit(solution)/shard_map/all_to_all | solution.py:354
  218.0 3.7 %all-to-all-start.6 = ((bf16[16,24,3200]{2,1,0:T(8,128)(2,1)}), bf16[16,24,3200]{2,1,0:T(8,128)(2,1)S(1)}, u32[]{:S(2)}, u32[]{:S(2)}) async-start(bf16[16,24,3200]{2,1,0:T(8,128)(2,1)} %copy-done.5), calls=%async_computation.6 | async-start | bytes 4915200 | tf_op jit(solution)/shard_map/all_to_all | solution.py:354
  224.1 3.9 %collective-permute-start.13 = (bf16[64,3072]{1,0:T(8,128)(2,1)S(1)}, bf16[64,3072]{1,0:T(8,128)(2,1)S(1)}, u32[]{:S(2)}, u32[]{:S(2)}) collective-permute-start(bf16[64,3072]{1,0:T(8,128)(2,1)S(1)} %home.6.refs_2_), channel_id=1, source_target_pairs={{0,3},{1,0},{2,1},{3,2},{4,7},{5,4},{6,5},{7,6},{8,11},{9,8},{10,9... | collective-permute-start | bytes 1179656 | tf_op jit(solution)/shard_map/ppermute | solution.py:358
  229.3 7.7 %collective-permute-done.13.refs_5_ = bf16[64,3072]{1,0:T(8,128)(2,1)S(1)} collective-permute-done((bf16[64,3072]{1,0:T(8,128)(2,1)S(1)}, bf16[64,3072]{1,0:T(8,128)(2,1)S(1)}, u32[]{:S(2)}, u32[]{:S(2)}) %collective-permute-start.13) | collective-permute-done | bytes 393248 | tf_op jit(solution)/shard_map/ppermute | solution.py:358
  237.0 3.1 collective-permute-done.12.refs_4_
  243.1 3.4 all-to-all-done.6.refs_1_
  246.6 24.6 %all_to_all.52.refs_0_ = bf16[16,24,3200]{2,1,0:T(8,128)(2,1)} all-to-all(bf16[16,24,3200]{2,1,0:T(8,128)(2,1)} %copy-done.7), channel_id=1, replica_groups=mesh['section'=2,'dp'=16,'expert'=4] {'dp'}, dimensions={0} | all-to-all | bytes 4915200 | tf_op jit(solution)/shard_map/all_to_all | solution.py:354
  271.1 12.9 %expert_backward.1 = (bf16[16,24,3200]{2,1,0:T(8,128)(2,1)S(1)}, f32[1,3072]{1,0:T(1,128)S(1)}) custom-call(bf16[16,24,3200]{2,1,0:T(8,128)(2,1)} %all_to_all.52.refs_0_, f32[400,1344]{1,0:T(8,128)S(1)} %copy-done.9, bf16[16,24,3200]{2,1,0:T(8,128)(2,1)S(1)} %copy-done.12, bf16[1344,3072]{1,0:T(8,128)(2,1)} %bitcast.33, bf16[1344,3072]{1,0:T(8,128)(2,1)} %bitcast.37, ...), custom_call_target="tpu_custom_call" | custom-call | flops 6606028800 | bytes 21430272 | tf_op jit(solution)/shard_map/expert_backward/pallas_call | solution.py:145
  284.0 24.1 %all_to_all.53.refs_1_ = bf16[16,24,3200]{2,1,0:T(8,128)(2,1)S(1)} all-to-all(bf16[16,24,3200]{2,1,0:T(8,128)(2,1)S(1)} %get-tuple-element.70), channel_id=1, replica_groups=mesh['section'=2,'dp'=16,'expert'=4] {'dp'}, dimensions={0} | all-to-all | bytes 4915200 | tf_op jit(solution)/shard_map/all_to_all | solution.py:354
  309.6 4.7 %collective-permute-start.16 = (bf16[64,3072]{1,0:T(8,128)(2,1)}, bf16[64,3072]{1,0:T(8,128)(2,1)S(1)}, u32[]{:S(2)}, u32[]{:S(2)}) collective-permute-start(bf16[64,3072]{1,0:T(8,128)(2,1)} %home.7.refs_2_), channel_id=1, source_target_pairs={{0,3},{1,0},{2,1},{3,2},{4,7},{5,4},{6,5},{7,6},{8,11},{9,8},{10,9... | collective-permute-start | bytes 1179656 | tf_op jit(solution)/shard_map/ppermute | solution.py:358
  318.9 11.0 %collective-permute-done.16.refs_5_ = bf16[64,3072]{1,0:T(8,128)(2,1)S(1)} collective-permute-done((bf16[64,3072]{1,0:T(8,128)(2,1)}, bf16[64,3072]{1,0:T(8,128)(2,1)S(1)}, u32[]{:S(2)}, u32[]{:S(2)}) %collective-permute-start.16) | collective-permute-done | bytes 393248 | tf_op jit(solution)/shard_map/ppermute | solution.py:358
  330.9 4.3 %collective-permute-done.15.refs_4_ = bf16[64,3072]{1,0:T(8,128)(2,1)} collective-permute-done((bf16[64,3072]{1,0:T(8,128)(2,1)}, bf16[64,3072]{1,0:T(8,128)(2,1)}, u32[]{:S(2)}, u32[]{:S(2)}) %collective-permute-start.15) | collective-permute-done | bytes 393248 | tf_op jit(solution)/shard_map/ppermute | solution.py:358
  336.2 2.0 finish.1
  340.1 3.3 collective-permute-done.8
  343.4 2.2 broadcast_select_fusion.2
  345.7 12.6 %all_to_all.54 = f32[64,2,192]{2,1,0:T(2,128)S(1)} all-to-all(f32[64,2,192]{2,1,0:T(2,128)S(1)} %bitcast.38), channel_id=1, replica_groups=mesh['section'=2,'dp'=16,'expert'=4] {'dp','expert'}, dimensions={0} | all-to-all | bytes 196608 | tf_op jit(solution)/shard_map/all_to_all | solution.py:428
  (96 shorter events, 39.5 us)
Async XLA Ops:
  0.6 4.3 %copy-start = (bf16[2,64,3072]{2,1,0:T(8,128)(2,1)S(1)}, bf16[2,64,3072]{2,1,0:T(8,128)(2,1)}, u32[]{:S(2)}) copy-start(bf16[2,64,3072]{2,1,0:T(8,128)(2,1)} %param.12) | copy-start | bytes 2359300
  0.6 14.7 %collective-permute-start.2 = (bf16[1344,3072]{1,0:T(8,128)(2,1)}, bf16[1344,3072]{1,0:T(8,128)(2,1)}, u32[]{:S(2)}, u32[]{:S(2)}) collective-permute-start(bf16[1344,3072]{1,0:T(8,128)(2,1)} %bitcast.30), channel_id=1, source_target_pairs={{0,64},{64,0},{1,65},{65,1},{2,66},{66,2},{3,67},{67,3},{4,68},{68... | collective-permute-start | bytes 24772616 | tf_op jit(solution)/shard_map/ppermute | solution.py:308
  2.1 24.8 %collective-permute-start.3 = (bf16[1344,3072]{1,0:T(8,128)(2,1)}, bf16[1344,3072]{1,0:T(8,128)(2,1)}, u32[]{:S(2)}, u32[]{:S(2)}) collective-permute-start(bf16[1344,3072]{1,0:T(8,128)(2,1)} %bitcast.34), channel_id=1, source_target_pairs={{0,64},{64,0},{1,65},{65,1},{2,66},{66,2},{3,67},{67,3},{4,68},{68... | collective-permute-start | bytes 24772616 | tf_op jit(solution)/shard_map/ppermute | solution.py:308
  3.6 11.7 %collective-permute-start.1 = (f32[1,3072]{1,0:T(1,128)}, f32[1,3072]{1,0:T(1,128)S(1)}, u32[]{:S(2)}, u32[]{:S(2)}) collective-permute-start(f32[1,3072]{1,0:T(1,128)} %convert_element_type.26), channel_id=1, source_target_pairs={{0,64},{64,0},{1,65},{65,1},{2,66},{66,2},{3,67},{67,3},{4,68},{68... | collective-permute-start | bytes 36872 | tf_op jit(solution)/shard_map/ppermute | solution.py:308
  4.8 10.0 %collective-permute-start = (s32[64,13]{1,0:T(8,128)S(1)}, s32[64,13]{1,0:T(8,128)S(1)}, u32[]{:S(2)}, u32[]{:S(2)}) collective-permute-start(s32[64,13]{1,0:T(8,128)S(1)} %bitcast.39), channel_id=1, source_target_pairs={{0,64},{64,0},{1,65},{65,1},{2,66},{66,2},{3,67},{67,3},{4,68},{68... | collective-permute-start | bytes 9992 | tf_op jit(solution)/shard_map/ppermute | solution.py:308
  5.0 22.0 %copy-start.13 = (bf16[64,3072]{1,0:T(8,128)(2,1)}, bf16[64,3072]{1,0:T(8,128)(2,1)S(1)}, u32[]{:S(2)}) copy-start(bf16[64,3072]{1,0:T(8,128)(2,1)S(1)} %dynamic-slice_bitcast_fusion.1.refs_0_) | copy-start | bytes 1179652
  71.3 3.9 %copy-start.16 = (bf16[2,64,3072]{2,1,0:T(8,128)(2,1)S(1)}, bf16[2,64,3072]{2,1,0:T(8,128)(2,1)}, u32[]{:S(2)}) copy-start(bf16[2,64,3072]{2,1,0:T(8,128)(2,1)} %param.13) | copy-start | bytes 2359300
  71.3 30.6 %all-to-all-start.2 = ((bf16[16,24,3200]{2,1,0:T(8,128)(2,1)}), bf16[16,24,3200]{2,1,0:T(8,128)(2,1)S(1)}, u32[]{:S(2)}, u32[]{:S(2)}) async-start(bf16[16,24,3200]{2,1,0:T(8,128)(2,1)} %copy-done.6), calls=%async_computation.2 | async-start | bytes 4915200 | tf_op jit(solution)/shard_map/all_to_all | solution.py:354
  101.9 34.1 %all-to-all-start.3 = ((bf16[16,24,3200]{2,1,0:T(8,128)(2,1)}), bf16[16,24,3200]{2,1,0:T(8,128)(2,1)}, u32[]{:S(2)}, u32[]{:S(2)}) async-start(bf16[16,24,3200]{2,1,0:T(8,128)(2,1)} %spread.1), calls=%async_computation.3 | async-start | bytes 4915200 | tf_op jit(solution)/shard_map/all_to_all | solution.py:354
  108.0 5.9 %copy-start.17 = (bf16[1,3072]{1,0:T(2,128)(2,1)S(1)}, bf16[1,3072]{1,0:T(2,128)(2,1)}, u32[]{:S(2)}) copy-start(bf16[1,3072]{1,0:T(2,128)(2,1)} %param.14) | copy-start | bytes 18436
  108.0 17.0 %copy-start.14 = (bf16[64,3072]{1,0:T(8,128)(2,1)S(1)}, bf16[64,3072]{1,0:T(8,128)(2,1)}, u32[]{:S(2)}) copy-start(bf16[64,3072]{1,0:T(8,128)(2,1)} %copy-done.13) | copy-start | bytes 1179652
  108.7 12.8 %collective-permute-start.6 = (bf16[64,3072]{1,0:T(8,128)(2,1)S(1)}, bf16[64,3072]{1,0:T(8,128)(2,1)S(1)}, u32[]{:S(2)}, u32[]{:S(2)}) collective-permute-start(bf16[64,3072]{1,0:T(8,128)(2,1)S(1)} %home.4.refs_1_), channel_id=1, source_target_pairs={{0,3},{1,0},{2,1},{3,2},{4,7},{5,4},{6,5},{7,6},{8,11},{9,8},{10,9... | collective-permute-start | bytes 1179656 | tf_op jit(solution)/shard_map/ppermute | solution.py:358
  112.6 12.5 %collective-permute-start.5 = (bf16[64,3072]{1,0:T(8,128)(2,1)S(1)}, bf16[64,3072]{1,0:T(8,128)(2,1)S(1)}, u32[]{:S(2)}, u32[]{:S(2)}) collective-permute-start(bf16[64,3072]{1,0:T(8,128)(2,1)S(1)} %home.4.refs_1_), channel_id=1, source_target_pairs={{0,1},{1,2},{2,3},{3,0},{4,5},{5,6},{6,7},{7,4},{8,9},{9,10},{10,1... | collective-permute-start | bytes 1179656 | tf_op jit(solution)/shard_map/ppermute | solution.py:358
  112.6 12.5 %collective-permute-start.4 = (bf16[64,3072]{1,0:T(8,128)(2,1)S(1)}, bf16[64,3072]{1,0:T(8,128)(2,1)S(1)}, u32[]{:S(2)}, u32[]{:S(2)}) collective-permute-start(bf16[64,3072]{1,0:T(8,128)(2,1)S(1)} %home.4.refs_1_), channel_id=1, source_target_pairs={{0,2},{1,3},{2,0},{3,1},{4,6},{5,7},{6,4},{7,5},{8,10},{9,11},{10,... | collective-permute-start | bytes 1179656 | tf_op jit(solution)/shard_map/ppermute | solution.py:358
  189.1 28.9 %copy-start.5 = (bf16[16,24,3200]{2,1,0:T(8,128)(2,1)}, bf16[16,24,3200]{2,1,0:T(8,128)(2,1)S(1)}, u32[]{:S(2)}) copy-start(bf16[16,24,3200]{2,1,0:T(8,128)(2,1)S(1)} %get-tuple-element.65) | copy-start | bytes 7372804
  218.0 28.6 %all-to-all-start.6 = ((bf16[16,24,3200]{2,1,0:T(8,128)(2,1)}), bf16[16,24,3200]{2,1,0:T(8,128)(2,1)S(1)}, u32[]{:S(2)}, u32[]{:S(2)}) async-start(bf16[16,24,3200]{2,1,0:T(8,128)(2,1)} %copy-done.5), calls=%async_computation.6 | async-start | bytes 4915200 | tf_op jit(solution)/shard_map/all_to_all | solution.py:354
  223.4 16.6 %copy-start.4 = (bf16[64,3072]{1,0:T(8,128)(2,1)S(1)}, bf16[64,3072]{1,0:T(8,128)(2,1)}, u32[]{:S(2)}) copy-start(bf16[64,3072]{1,0:T(8,128)(2,1)} %copy-done.3) | copy-start | bytes 1179652
  224.1 12.9 %collective-permute-start.13 = (bf16[64,3072]{1,0:T(8,128)(2,1)S(1)}, bf16[64,3072]{1,0:T(8,128)(2,1)S(1)}, u32[]{:S(2)}, u32[]{:S(2)}) collective-permute-start(bf16[64,3072]{1,0:T(8,128)(2,1)S(1)} %home.6.refs_2_), channel_id=1, source_target_pairs={{0,3},{1,0},{2,1},{3,2},{4,7},{5,4},{6,5},{7,6},{8,11},{9,8},{10,9... | collective-permute-start | bytes 1179656 | tf_op jit(solution)/shard_map/ppermute | solution.py:358
  228.0 12.1 %collective-permute-start.12 = (bf16[64,3072]{1,0:T(8,128)(2,1)S(1)}, bf16[64,3072]{1,0:T(8,128)(2,1)S(1)}, u32[]{:S(2)}, u32[]{:S(2)}) collective-permute-start(bf16[64,3072]{1,0:T(8,128)(2,1)S(1)} %home.6.refs_2_), channel_id=1, source_target_pairs={{0,1},{1,2},{2,3},{3,0},{4,5},{5,6},{6,7},{7,4},{8,9},{9,10},{10,1... | collective-permute-start | bytes 1179656 | tf_op jit(solution)/shard_map/ppermute | solution.py:358
  228.0 12.1 %collective-permute-start.11 = (bf16[64,3072]{1,0:T(8,128)(2,1)S(1)}, bf16[64,3072]{1,0:T(8,128)(2,1)S(1)}, u32[]{:S(2)}, u32[]{:S(2)}) collective-permute-start(bf16[64,3072]{1,0:T(8,128)(2,1)S(1)} %home.6.refs_2_), channel_id=1, source_target_pairs={{0,2},{1,3},{2,0},{3,1},{4,6},{5,7},{6,4},{7,5},{8,10},{9,11},{10,... | collective-permute-start | bytes 1179656 | tf_op jit(solution)/shard_map/ppermute | solution.py:358
  246.6 24.6 %copy-start.9 = (f32[400,1344]{1,0:T(8,128)S(1)}, f32[400,1344]{1,0:T(8,128)}, u32[]{:S(2)}) copy-start(f32[400,1344]{1,0:T(8,128)} %copy-done.8) | copy-start | bytes 6451204
  246.6 24.6 %copy-start.12 = (bf16[16,24,3200]{2,1,0:T(8,128)(2,1)S(1)}, bf16[16,24,3200]{2,1,0:T(8,128)(2,1)}, u32[]{:S(2)}) copy-start(bf16[16,24,3200]{2,1,0:T(8,128)(2,1)} %get-tuple-element.92.refs_0_.refs_2_) | copy-start | bytes 7372804
  309.6 20.4 %collective-permute-start.16 = (bf16[64,3072]{1,0:T(8,128)(2,1)}, bf16[64,3072]{1,0:T(8,128)(2,1)S(1)}, u32[]{:S(2)}, u32[]{:S(2)}) collective-permute-start(bf16[64,3072]{1,0:T(8,128)(2,1)} %home.7.refs_2_), channel_id=1, source_target_pairs={{0,3},{1,0},{2,1},{3,2},{4,7},{5,4},{6,5},{7,6},{8,11},{9,8},{10,9... | collective-permute-start | bytes 1179656 | tf_op jit(solution)/shard_map/ppermute | solution.py:358
  314.3 20.9 %collective-permute-start.15 = (bf16[64,3072]{1,0:T(8,128)(2,1)}, bf16[64,3072]{1,0:T(8,128)(2,1)}, u32[]{:S(2)}, u32[]{:S(2)}) collective-permute-start(bf16[64,3072]{1,0:T(8,128)(2,1)} %home.7.refs_2_), channel_id=1, source_target_pairs={{0,1},{1,2},{2,3},{3,0},{4,5},{5,6},{6,7},{7,4},{8,9},{9,10},{10,1... | collective-permute-start | bytes 1179656 | tf_op jit(solution)/shard_map/ppermute | solution.py:358
  314.3 20.9 %collective-permute-start.14 = (bf16[64,3072]{1,0:T(8,128)(2,1)}, bf16[64,3072]{1,0:T(8,128)(2,1)}, u32[]{:S(2)}, u32[]{:S(2)}) collective-permute-start(bf16[64,3072]{1,0:T(8,128)(2,1)} %home.7.refs_2_), channel_id=1, source_target_pairs={{0,2},{1,3},{2,0},{3,1},{4,6},{5,7},{6,4},{7,5},{8,10},{9,11},{10,... | collective-permute-start | bytes 1179656 | tf_op jit(solution)/shard_map/ppermute | solution.py:358
  316.9 23.2 %collective-permute-start.9 = (bf16[64,3072]{1,0:T(8,128)(2,1)}, bf16[64,3072]{1,0:T(8,128)(2,1)S(1)}, u32[]{:S(2)}, u32[]{:S(2)}) collective-permute-start(bf16[64,3072]{1,0:T(8,128)(2,1)} %home.5), channel_id=1, source_target_pairs={{0,3},{1,0},{2,1},{3,2},{4,7},{5,4},{6,5},{7,6},{8,11},{9,8},{10,9... | collective-permute-start | bytes 1179656 | tf_op jit(solution)/shard_map/ppermute | solution.py:358
  318.4 25.0 %collective-permute-start.8 = (bf16[64,3072]{1,0:T(8,128)(2,1)}, bf16[64,3072]{1,0:T(8,128)(2,1)S(1)}, u32[]{:S(2)}, u32[]{:S(2)}) collective-permute-start(bf16[64,3072]{1,0:T(8,128)(2,1)} %home.5), channel_id=1, source_target_pairs={{0,1},{1,2},{2,3},{3,0},{4,5},{5,6},{6,7},{7,4},{8,9},{9,10},{10,1... | collective-permute-start | bytes 1179656 | tf_op jit(solution)/shard_map/ppermute | solution.py:358
  330.7 12.7 %collective-permute-start.7 = (bf16[64,3072]{1,0:T(8,128)(2,1)}, bf16[64,3072]{1,0:T(8,128)(2,1)S(1)}, u32[]{:S(2)}, u32[]{:S(2)}) collective-permute-start(bf16[64,3072]{1,0:T(8,128)(2,1)} %home.5), channel_id=1, source_target_pairs={{0,2},{1,3},{2,0},{3,1},{4,6},{5,7},{6,4},{7,5},{8,10},{9,11},{10,... | collective-permute-start | bytes 1179656 | tf_op jit(solution)/shard_map/ppermute | solution.py:358
  345.6 16.2 %collective-permute-start.10 = (bf16[64,3072]{1,0:T(8,128)(2,1)}, bf16[64,3072]{1,0:T(8,128)(2,1)S(1)}, u32[]{:S(2)}, u32[]{:S(2)}) collective-permute-start(bf16[64,3072]{1,0:T(8,128)(2,1)} %get-tuple-element.76), channel_id=1, source_target_pairs={{0,64},{64,0},{1,65},{65,1},{2,66},{66,2},{3,67},{67,3},{4,68},{68... | collective-permute-start | bytes 1179656 | tf_op jit(solution)/shard_map/ppermute | solution.py:308
  358.4 2.5 collective-permute-start.18
  361.5 3.1 collective-permute-start.17
  363.6 2.0 copy-start.1
  (8 other events, 9.3 us)

commit v3 on v2

v3 whole, which is shorter than its diff:
```python
import functools

import jax
import jax.numpy as jnp
from jax import lax
from jax.experimental import pallas as pl
from jax.experimental.pallas import tpu as pltpu
from jax.sharding import PartitionSpec as P

EPSILON = 1e-05
SWAP = [(0, 1), (1, 0)]
LANES = 128
HIDDEN_STEP = 256
COPY_STEP = 224
WIDTH_STEP = 512
VMEM_BYTES = 48 * 1024 * 1024
bf16, f32 = jnp.bfloat16, jnp.float32


def over_columns(width, body, unrolled=False):
    if unrolled:
        for i in range(width // WIDTH_STEP):
            body(i, i * WIDTH_STEP, WIDTH_STEP)
        return

    @pl.loop(0, width // WIDTH_STEP)
    def _(i):
        body(i, pl.multiple_of(i * WIDTH_STEP, WIDTH_STEP), WIDTH_STEP)


def load_rows(held, rows, tails):
    owners, whole, _ = held.shape
    width = rows.shape[1]
    main = owners * whole

    def load(i, s, n):
        rows[0:main, pl.ds(s, n)] = held[:, :, pl.ds(s, n)].reshape(main, n)

    over_columns(width, load)
    tails[...] = held[:, :, width : width + LANES].astype(f32)
    for c in range(width // LANES):
        rows[main : main + owners, c * LANES : (c + 1) * LANES] = tails[:, c, :].astype(bf16)


def store_columns(out, by_lane, i, start, value):
    owners, whole, _ = out.shape
    main = owners * whole
    size = value.shape[1]
    out[:, :, pl.ds(start, size)] = value[:main].astype(bf16).reshape(owners, whole, size)
    for c in range(size // LANES):
        by_lane[i * (size // LANES) + c] = value[main:, c * LANES : (c + 1) * LANES]


def store_tails(out, by_lane, tails, width):
    for c in range(by_lane.shape[0]):
        tails[:, c, :] = by_lane[c]
    out[:, :, width : width + LANES] = tails[...].astype(bf16)


def store_gain(out, gain_cols, width):
    value = jnp.broadcast_to(gain_cols[...][None], (out.shape[0], *gain_cols.shape))
    out[:, :, width + LANES : width + 2 * LANES] = value.astype(bf16)


def sum_gain(held, width):
    return jnp.sum(held[:, :, width + LANES : width + 2 * LANES].astype(f32), axis=0)


def by_units(rows, weights):
    return lax.dot_general(rows, weights, (((1,), (1,)), ((), ())), preferred_element_type=f32)


def sigmoid(v):
    return 1.0 / (1.0 + jnp.exp(-v))


def expert_kernel(mode, layer, n_in, n_out, n_held, *refs):
    ins, refs = refs[:n_in], refs[n_in:]
    own_hbm, other_hbm, refs = refs[:2], refs[2:4], refs[4:]
    outs, refs = refs[:n_out], refs[n_out:]
    up, down, rows, act, tails, by_lane, up_sem, down_sem, in_sem, out_sem, *refs = refs
    held, refs = refs[:n_held], refs[n_held:]
    hidden, width = up.shape
    loops, columns = hidden // HIDDEN_STEP, width // WIDTH_STEP
    rest = hidden - loops * HIDDEN_STEP
    backward = mode == "backward"

    arrivals = [
        pltpu.make_async_copy(src, dst, in_sem.at[i]) for i, (src, dst) in enumerate(zip(ins, held))
    ]
    for copy in arrivals:
        copy.start()

    def copy_of(k, i, pair):
        part = pl.ds(pl.multiple_of(i * COPY_STEP, COPY_STEP), COPY_STEP)
        dst, sem = ((up, up_sem), (down, down_sem))[k]
        return pltpu.make_async_copy(pair[k].at[part, :], dst.at[part, :], sem.at[i])

    def start(pair):
        for k in (1, 0) if backward else (0, 1):

            @pl.loop(0, hidden // COPY_STEP)
            def _(i):
                copy_of(k, i, pair).start()

    mine = lax.axis_index("section") == layer
    pl.when(mine)(lambda: start(own_hbm))
    pl.when(jnp.logical_not(mine))(lambda: start(other_hbm))

    def hidden_units(weights, body, k=None):
        if k is not None:
            copy_of(k, 0, own_hbm).wait()

        @pl.loop(0, loops)
        def _(i):
            if k is not None:
                copy_of(k, i + 1, own_hbm).wait()
            at = pl.ds(pl.multiple_of(i * HIDDEN_STEP, HIDDEN_STEP), HIDDEN_STEP)
            body(at, by_units(rows[...], weights[at, :]))

        at = pl.ds(loops * HIDDEN_STEP, rest)
        body(at, by_units(rows[...], weights[at, :]))

    def gradient(pre):
        def body(at, v):
            p = pre[:, at].astype(f32)
            g = sigmoid(p)
            act[:, at] = (v * g * (1.0 + p * (1.0 - g))).astype(bf16)

        return body

    def activation(pre):
        def body(at, v):
            pre[:, at] = v.astype(pre.dtype)
            act[:, at] = (v * sigmoid(v)).astype(bf16)

        return body

    def leave(stage, out, number, s, n):
        part = (slice(None), slice(None), pl.ds(s, n))
        return pltpu.make_async_copy(stage.at[part], out.at[part], out_sem.at[number])

    def results(weights, stage, out, number, gain_cols=None):
        def step(i, s, n):
            value = jnp.dot(act[...], weights[:, pl.ds(s, n)], preferred_element_type=f32)
            store_columns(stage, by_lane, i, s, value)
            leave(stage, out, number + i, s, n).start()
            if gain_cols is not None:
                terms = value * rows[:, pl.ds(s, n)].astype(f32)
                summed = jnp.sum(terms, axis=0, keepdims=True)
                for c in range(n // LANES):
                    at = pl.ds(i * (n // LANES) + c, 1)
                    gain_cols[at, :] = summed[:, c * LANES : (c + 1) * LANES]

        over_columns(width, step)
        store_tails(stage, by_lane, tails, width)
        if gain_cols is not None:
            store_gain(stage, gain_cols, width)
        leave(stage, out, number + columns, width, stage.shape[2] - width).start()

    def left(stage, out, number):
        over_columns(width, lambda i, s, n: leave(stage, out, number + i, s, n).wait())
        leave(stage, out, number + columns, width, stage.shape[2] - width).wait()

    def all_here(k):
        @pl.loop(0, hidden // COPY_STEP)
        def _(i):
            copy_of(k, i, own_hbm).wait()

    arrivals[0].wait()
    load_rows(held[0], rows, tails)
    if backward:
        stage, gain_cols, tile = refs
        arrivals[1].wait()
        hidden_units(down, gradient(held[1]), 1)
        outs[1][...] = sum_gain(held[0], width)
        arrivals[2].wait()
        load_rows(held[2], rows, tails)
        copy = pltpu.make_async_copy(ins[3].at[pl.ds(0, 16), pl.ds(0, LANES)], tile, in_sem.at[3])
        copy.start()
        copy.wait()
        all_here(0)
        results(up, stage, outs[0], 0, gain_cols)
        left(stage, outs[0], 0)
        return
    stage, pre, *refs = refs
    hidden_units(up, activation(pre), 0)
    all_here(1)
    if mode == "forward":
        kept = pltpu.make_async_copy(pre, outs[1], in_sem.at[1])
        kept.start()
        results(down, stage, outs[0], 0)
        kept.wait()
    else:
        (d_stage,) = refs
        results(down, stage, outs[0], 0)
        arrivals[1].wait()
        load_rows(held[1], rows, tails)
        hidden_units(down, gradient(pre))
        results(up, d_stage, outs[1], columns + 1)
        left(d_stage, outs[1], columns + 1)
    left(stage, outs[0], 0)


def expert(mode, layer, weights, *inputs):
    hidden, width = weights[0].shape
    owners, whole, wide = inputs[0].shape
    count = owners * (whole + 1)
    copies, columns = hidden // COPY_STEP, width // WIDTH_STEP
    block = jax.ShapeDtypeStruct((owners, whole, wide), bf16)
    pre = jax.ShapeDtypeStruct((count, hidden), bf16)
    cols = jax.ShapeDtypeStruct((width // LANES, LANES), f32)
    out_shape = {"forward": [block, pre], "backward": [block, cols], "both": [block, block]}[mode]
    stage = pltpu.VMEM(block.shape, bf16)
    held = [pltpu.VMEM(x.shape, x.dtype) for x in inputs[:3]]
    own_scratch = {
        "forward": [stage, pltpu.VMEM(pre.shape, bf16)],
        "backward": [stage, pltpu.VMEM(cols.shape, f32), pltpu.VMEM((16, LANES), bf16)],
        "both": [stage, pltpu.VMEM(pre.shape, f32), stage],
    }[mode]
    in_hbm = pl.BlockSpec(memory_space=pltpu.HBM)
    anywhere = pl.BlockSpec(memory_space=pl.ANY)
    vmem = pl.BlockSpec(memory_space=pltpu.VMEM)
    n_mm = 4 if mode == "both" else 2
    return pl.pallas_call(
        functools.partial(expert_kernel, mode, layer, len(inputs), 2, len(held)),
        out_shape=out_shape,
        in_specs=[anywhere] * (len(inputs) + 4),
        out_specs=[in_hbm, vmem if mode == "backward" else in_hbm],
        scratch_shapes=[
            pltpu.VMEM((hidden, width), bf16),
            pltpu.VMEM((hidden, width), bf16),
            pltpu.VMEM((count, width), bf16),
            pltpu.VMEM((count, hidden), bf16),
            pltpu.VMEM((owners, whole, LANES), f32),
            pltpu.VMEM((width // LANES, owners, LANES), f32),
            pltpu.SemaphoreType.DMA((copies,)),
            pltpu.SemaphoreType.DMA((copies,)),
            pltpu.SemaphoreType.DMA((4,)),
            pltpu.SemaphoreType.DMA((2 * columns + 2,)),
            *held,
            *own_scratch,
        ],
        compiler_params=pltpu.CompilerParams(vmem_limit_bytes=VMEM_BYTES),
        cost_estimate=pl.CostEstimate(
            flops=2 * n_mm * count * hidden * width,
            bytes_accessed=4 * hidden * width + 4 * count * width,
            transcendentals=count * hidden,
        ),
        name="expert_" + mode,
    )(*inputs, *weights)


def tables_kernel(top, whole, packed, plain, weighted):
    row_count, count = plain.shape
    owners = count // (whole + 1)
    main = owners * whole
    own_lane = lax.broadcasted_iota(jnp.int32, (row_count, owners), 1)
    hot = jnp.zeros((row_count, owners), f32)
    share = jnp.zeros((row_count, owners), f32)
    total = jnp.zeros((row_count, 1), f32)
    counts = packed[:, top : top + 1]
    for k in range(top):
        named = packed[:, k : k + 1] == own_lane
        fixed = packed[:, top + 1 + k : top + 2 + k].astype(f32)
        fixed = jnp.where(counts > k, fixed, 0.0)
        hot = hot + jnp.where(named, 1.0, 0.0)
        share = share + jnp.where(named, fixed, 0.0)
        total = total + fixed
    share = share / total
    owner = lax.broadcasted_iota(jnp.int32, (owners, count), 0)
    column = lax.broadcasted_iota(jnp.int32, (owners, count), 1)
    place = column - owner * whole
    inside = (place >= 0) & (place < whole) & (column < main)
    spread = jnp.where(inside | (column - main == owner), 1.0, 0.0)
    place = jnp.sum(jnp.where(inside, place, 0).astype(f32), axis=0, keepdims=True)
    last = lax.broadcasted_iota(jnp.int32, (1, count), 1) >= main
    place = jnp.where(last, float(whole), place)
    spread = spread.astype(bf16)
    row = lax.broadcasted_iota(jnp.int32, (row_count, row_count), 0)
    earlier = lax.broadcasted_iota(jnp.int32, (row_count, row_count), 1) < row
    below = jnp.where(earlier, 1.0, 0.0).astype(bf16)
    before = jnp.dot(below, hot.astype(bf16), preferred_element_type=f32)
    hot_c = jnp.dot(hot.astype(bf16), spread, preferred_element_type=f32)
    before_c = jnp.dot(before.astype(bf16), spread, preferred_element_type=f32)
    share_c = jnp.dot(share.astype(bf16), spread, preferred_element_type=f32)
    chosen = jnp.where(before_c == place, hot_c, 0.0)
    plain[...] = chosen.astype(bf16)
    weighted[...] = (chosen * share_c).astype(bf16)


def pallas(kernel, out_shape, scratch, name, *inputs, awaits=()):
    vmem = pl.BlockSpec(memory_space=pltpu.VMEM)

    def body(*refs):
        awaited, refs = refs[len(inputs) : len(inputs) + len(awaits)], (
            refs[: len(inputs)] + refs[len(inputs) + len(awaits) :]
        )
        if awaited:
            refs, (tile, sem) = refs[:-2], refs[-2:]
        for ref in awaited:
            part = (0,) * (len(ref.shape) - 2) + (pl.ds(0, 16), pl.ds(0, LANES))
            copy = pltpu.make_async_copy(ref.at[part], tile, sem)
            copy.start()
            copy.wait()
        kernel(*refs)

    if awaits:
        scratch = [*scratch, pltpu.VMEM((16, LANES), bf16), pltpu.SemaphoreType.DMA(())]

    return pl.pallas_call(
        body,
        out_shape=out_shape,
        in_specs=[vmem] * len(inputs) + [pl.BlockSpec(memory_space=pl.ANY)] * len(awaits),
        out_specs=jax.tree.map(lambda _: vmem, out_shape),
        scratch_shapes=scratch,
        compiler_params=pltpu.CompilerParams(vmem_limit_bytes=VMEM_BYTES),
        name=name,
    )(*inputs, *awaits)


def pack(table, rows, out, by_lane, tails):
    width = rows.shape[1]

    def step(i, s, n):
        value = lax.dot_general(
            table[...], rows[:, pl.ds(s, n)], (((0,), (0,)), ((), ())), preferred_element_type=f32
        )
        store_columns(out, by_lane, i, s, value)

    over_columns(width, step, unrolled=True)
    store_tails(out, by_lane, tails, width)


def normed(state_f):
    mean = jnp.mean(state_f * state_f, axis=-1, keepdims=True)
    inverse_rms = lax.rsqrt(mean + EPSILON)
    return state_f * inverse_rms, inverse_rms


def four(parts):
    own, far, left, right = (p[...].astype(f32) for p in parts)
    return (own + far) + (left + right)


def plain_kernel(rows, table, out, *tails):
    pack(table, rows, out, *tails)


def norm_kernel(x, gain, table, out, rows, *tails):
    rows[...] = (normed(x[...].astype(f32))[0] * gain[...]).astype(bf16)
    pack(table, rows, out, *tails)


def sum_norm_kernel(x, p0, p1, p2, p3, gain, table, following, out, rows, *tails):
    following[...] = (x[...].astype(f32) + four((p0, p1, p2, p3))).astype(bf16)
    rows[...] = (normed(following[...].astype(f32))[0] * gain[...]).astype(bf16)
    pack(table, rows, out, *tails)


def finish(x, upstream, parts, gain, grad):
    d_norm = four(parts)
    scaled, inverse_rms = normed(x[...].astype(f32))
    d_scaled = d_norm * gain[...]
    mean = jnp.mean(d_scaled * scaled, axis=-1, keepdims=True)
    d_input = inverse_rms * (d_scaled - scaled * mean)
    grad[...] = (upstream[...].astype(f32) + d_input).astype(bf16)
    return jnp.sum(d_norm * scaled, axis=0, keepdims=True)


def finish_kernel(x, upstream, p0, p1, p2, p3, gain, grad):
    finish(x, upstream, (p0, p1, p2, p3), gain, grad)


def finish_pack_kernel(x, upstream, p0, p1, p2, p3, gain, table, grad, out, gain_cols, *tails):
    gain_grad = finish(x, upstream, (p0, p1, p2, p3), gain, grad)
    for c in range(gain_cols.shape[0]):
        gain_cols[c : c + 1, :] = gain_grad[:, c * LANES : (c + 1) * LANES]
    pack(table, grad, out, *tails)
    store_gain(out, gain_cols, grad.shape[1])


def home_kernel(table, held, out, *refs):
    *summed, by_lane, tails = refs
    owners, whole, _ = held.shape
    width = out.shape[1]
    main = owners * whole
    tails[...] = held[:, :, width : width + LANES].astype(f32)
    for c in range(width // LANES):
        by_lane[c] = tails[:, c, :]

    def step(i, s, n):
        rows = held[:, :, pl.ds(s, n)].reshape(main, n)
        last = [by_lane[i * (n // LANES) + c] for c in range(n // LANES)]
        last = jnp.concatenate(last, axis=1).astype(bf16)
        value = jnp.dot(table[:, :main], rows, preferred_element_type=f32)
        value = value + jnp.dot(table[:, main:], last, preferred_element_type=f32)
        out[:, pl.ds(s, n)] = value.astype(bf16)

    over_columns(width, step, unrolled=True)
    for ref in summed:
        ref[...] = sum_gain(held, width)


def swapped(x):
    return lax.ppermute(x, "section", SWAP)


def after(value, first_done):
    return lax.optimization_barrier((value, first_done))[0]


def shards(inputs, cotangent, gain, w_up, w_down, expert_ids, expert_counts, combine_fixed):
    section = lax.axis_index("section")
    owners = lax.axis_size("dp")
    ring = lax.axis_size("expert")
    row_count, width = inputs.shape[1:]
    top = expert_ids.shape[3]
    capacity = min(row_count, row_count * top // owners + 1)
    whole = capacity - 1
    count = owners * capacity
    first = section == 0
    up_own, down_own = w_up[0, 0], w_down[0, 0]

    def like(*shape, dtype=bf16):
        return jax.ShapeDtypeStruct(shape, dtype)

    block = like(owners, whole, width + LANES)
    gain_block = like(owners, whole, width + 2 * LANES)
    cols_shape = like(width // LANES, LANES, dtype=f32)
    rows_shape = like(row_count, width)
    table_shape = like(row_count, count)
    tails = [
        pltpu.VMEM((width // LANES, owners, LANES), f32),
        pltpu.VMEM((owners, whole, LANES), f32),
    ]
    rows = pltpu.VMEM((row_count, width), bf16)

    def pick(mine, other, layer):
        return jnp.where(section == layer, mine, other)

    ints = jnp.concatenate([expert_ids[0], expert_counts[0][..., None], combine_fixed[0]], axis=-1)
    mine = lax.dynamic_index_in_dim(ints, section, 0, keepdims=False)
    theirs = swapped(lax.dynamic_index_in_dim(ints, 1 - section, 0, keepdims=False))
    gain_own = gain.astype(f32)
    gain_other = swapped(gain_own)
    x0 = lax.dynamic_index_in_dim(inputs, section, 0, keepdims=False)
    upstream = lax.dynamic_index_in_dim(cotangent, section, 0, keepdims=False)
    up_other, down_other = swapped(up_own), swapped(down_own)

    def tables(packed, *awaits):
        kernel = functools.partial(tables_kernel, top, whole)
        return pallas(kernel, [table_shape, table_shape], [], "tables", packed, awaits=awaits)

    def exchange(held):
        return lax.all_to_all(held, "dp", split_axis=0, concat_axis=0, tiled=True)

    def over_groups(part):
        pairs = [[(i, (i + by) % ring) for i in range(ring)] for by in (2, 1, 3)]
        return (part, *[lax.ppermute(part, "expert", p) for p in pairs])

    def home(table, held):
        return over_groups(pallas(home_kernel, [rows_shape], tails, "home", table, held)[0])

    weights = (up_own, down_own, up_other, down_other)

    def enter(current, gain_row, table, *awaits):
        args = (current, gain_row, table)
        return exchange(pallas(norm_kernel, block, [rows, *tails], "enter", *args, awaits=awaits))

    own_tables = tables(mine)
    rows0 = lax.cond(
        first,
        enter,
        lambda *a: jnp.zeros(block.shape, bf16),
        x0,
        gain_own,
        own_tables[0],
    )
    other_tables = tables(theirs, rows0)
    rows0 = lax.cond(
        first,
        lambda kept, *a: kept,
        lambda kept, *a: enter(*a),
        rows0,
        x0,
        gain_other,
        other_tables[0],
        up_other,
        down_other,
    )
    gain0, gain1 = (pick(gain_own, gain_other, layer) for layer in range(2))
    plain0, plain1 = (pick(own_tables[0], other_tables[0], layer) for layer in range(2))
    weighted0, weighted1 = (pick(own_tables[1], other_tables[1], layer) for layer in range(2))
    d_held1 = pallas(plain_kernel, block, tails, "spread", upstream, weighted1)

    part0, pre0 = expert("forward", 0, weights, rows0)
    back0 = exchange(part0)
    d_rows1 = exchange(after(d_held1, back0))
    sums0 = home(weighted0, back0)
    x1, held1 = pallas(
        sum_norm_kernel, [rows_shape, block], [rows, *tails], "next", x0, *sums0, gain1, plain1
    )
    rows1 = exchange(after(held1, d_rows1))
    part1, d_part1 = expert("both", 1, weights, rows1, d_rows1)
    d_back1 = exchange(d_part1)
    back1 = exchange(after(part1, d_back1))
    d_sums1 = home(plain1, d_back1)
    grad1, d_held0 = pallas(
        finish_pack_kernel,
        [rows_shape, gain_block],
        [pltpu.VMEM(cols_shape.shape, f32), *tails],
        "finish_next",
        x1,
        upstream,
        *d_sums1,
        gain1,
        weighted0,
    )
    d_rows0 = exchange(after(d_held0, back1))
    x2 = (x1.astype(f32) + four(home(weighted1, back1))).astype(bf16)
    d_part0, gain_sum1 = expert("backward", 0, weights, d_rows0, pre0, rows0, x2)
    d_back0 = exchange(d_part0)
    kept_x, taken_x = pick(x1, x2, 0), swapped(pick(x2, x1, 0))
    d_home0, gain_sum0 = pallas(
        home_kernel,
        [rows_shape, cols_shape],
        tails,
        "home_gain",
        plain0,
        d_back0,
        awaits=(taken_x,),
    )
    d_sums0 = over_groups(d_home0)
    gain_sum0 = four(over_groups(gain_sum0)) / gain0.reshape(cols_shape.shape)
    grad0 = pallas(finish_kernel, rows_shape, [], "finish", x0, grad1, *d_sums0, gain0)

    kept_g, taken_g = pick(grad0, grad1, 0), swapped(pick(grad1, grad0, 0))

    def gain_slice(summed):
        summed = summed.reshape(owners, width // owners)
        return lax.dynamic_index_in_dim(summed, lax.axis_index("dp"), 0, keepdims=False)

    slice0, slice1 = gain_slice(gain_sum0), gain_slice(gain_sum1)
    gain_sum = pick(slice0, slice1, 0) + swapped(pick(slice1, slice0, 0))

    def both(kept, taken):
        low, high = jnp.where(first, kept, taken), jnp.where(first, taken, kept)
        return jnp.stack([low, high])[None]

    return both(kept_x, taken_x), both(kept_g, taken_g), gain_sum[None]


def solution(mesh):
    return jax.shard_map(
        shards,
        mesh=mesh,
        in_specs=(
            P(None, "dp", None),
            P(None, "dp", None),
            P("section", None),
            P("section", "dp", "expert", None),
            P("section", "dp", "expert", None),
            P("section", None, "dp", None),
            P("section", None, "dp"),
            P("section", None, "dp", None),
        ),
        out_specs=(
            P("section", None, "dp", None),
            P("section", None, "dp", None),
            P("section", "dp"),
        ),
        check_vma=False,
    )
```

time: 371 us -> 346 us (0.933); the launches traced: 366 us -> 345 us
  blocking collectives: 139 us -> 80.1 us
  waiting for transfers between devices: 99.2 us -> 123 us
  starting transfers between devices: 36.2 us -> 50.5 us
    all_to_all x5 -> x3, blocking collectives: 127 us -> 80.1 us  [exchange(): return lax.all_to_all(held, 'dp', split_axis=0, concat_axis=0, tiled=True)]
    all_to_all x3 -> x5, waiting for transfers between devices: 36.6 us -> 60.2 us  [exchange(): return lax.all_to_all(held, 'dp', split_axis=0, concat_axis=0, tiled=True)]
    all_to_all x1 -> x0, blocking collectives: 12.6 us -> none  [shards(): lax.all_to_all(slices, ('dp', 'expert'), split_axis=0, concat_axis=0, til...]
    all_to_all x3 -> x5, starting transfers between devices: 13.7 us -> 23.2 us  [exchange(): return lax.all_to_all(held, 'dp', split_axis=0, concat_axis=0, tiled=True)]
    ppermute x12 -> x15, starting transfers between devices: 18.3 us -> 24.2 us  [over_groups(): return (part, *[lax.ppermute(part, 'expert', p) for p in pairs])]
    unnamed x36 -> x38, local copies, waits for them, and re-layouts: 9.35 us -> 12.4 us
    ppermute x12 -> x15, waiting for transfers between devices: 42.3 us -> 42.1 us  [over_groups(): return (part, *[lax.ppermute(part, 'expert', p) for p in pairs])]
  transfers between devices with their start and end apart: 22 -> 27, of which waited for: 14 -> 18; matrix products, arithmetic and copies ran while one was open for 2% -> 3% of each run, Pallas kernels for 3% -> 3%
where the time goes in v3:
time: 346 us; the launch traced here: 345 us
  waiting for transfers between devices  123 us (36%)
  blocking collectives  80.1 us (23%)
  Pallas kernels  67.4 us (19%)
  starting transfers between devices  50.5 us (15%)
  local copies, waits for them, and re-layouts  14.7 us (4%)
  other arithmetic  7.72 us (2%)
    all_to_all x3, blocking collectives, exchange(): return lax.all_to_all(held, 'dp', split_axis=0, concat_axis=0, tiled=True)  80.1 us
    all_to_all x5, waiting for transfers between devices, exchange(): return lax.all_to_all(held, 'dp', split_axis=0, concat_axis=0, tiled=True)  60.2 us
    pallas_call x3, Pallas kernels, expert(): pl.pallas_call(functools.partial(expert_kernel, mode, layer, len(inputs),...  52.5 us
    ppermute x15, waiting for transfers between devices, over_groups(): return (part, *[lax.ppermute(part, 'expert', p) for p in pairs])  42.1 us
    ppermute x15, starting transfers between devices, over_groups(): return (part, *[lax.ppermute(part, 'expert', p) for p in pairs])  24.2 us
    all_to_all x5, starting transfers between devices, exchange(): return lax.all_to_all(held, 'dp', split_axis=0, concat_axis=0, tiled=True)  23.2 us
    ppermute x7, waiting for transfers between devices, swapped(): return lax.ppermute(x, 'section', SWAP)  20.9 us
    pallas_call x11, Pallas kernels, pallas(): pl.pallas_call(body, out_shape=out_shape, in_specs=[vmem] * len(inputs) +...  14.9 us
  transfers between devices with their start and end apart: 27, of which 18 were waited for; matrix products, arithmetic and copies ran while one was open for 3% of the time, Pallas kernels for 3%

profile of v3, /device:TPU:1, one launch (start us, length us, event | category | flops | bytes accessed | tf_op | source)
XLA Modules:
  0.0 344.7 jit_solution(10391184817704300150)
XLA Ops:
  7.1 7.8 %collective-permute-done.refs_0_ = s32[64,13]{1,0:T(8,128)S(1)} collective-permute-done((s32[64,13]{1,0:T(8,128)S(1)}, s32[64,13]{1,0:T(8,128)S(1)}, u32[]{:S(2)}, u32[]{:S(2)}) %collective-permute-start) | collective-permute-done | bytes 3360 | tf_op jit(solution)/shard_map/ppermute | solution.py:406
  15.9 11.0 %collective-permute-done.3.refs_4_.refs_5_.refs_7_ = bf16[1344,3072]{1,0:T(8,128)(2,1)} collective-permute-done((bf16[1344,3072]{1,0:T(8,128)(2,1)}, bf16[1344,3072]{1,0:T(8,128)(2,1)}, u32[]{:S(2)}, u32[]{:S(2)}) %collective-permute-start.3) | collective-permute-done | bytes 8257568 | tf_op jit(solution)/shard_map/ppermute | solution.py:406
  27.0 29.4 %conditional.3 = (bf16[16,24,3200]{2,1,0:T(8,128)(2,1)S(1)}) conditional(s32[]{:T(128)} %convert_element_type.25, (bf16[64,3072]{1,0:T(8,128)(2,1)S(1)}, f32[1,3072]{1,0:T(1,128)S(1)}, bf16[64,400]{1,0:T(8,128)(2,1)}, bf16[1344,3072]{1,0:T(8,128)(2,1)}, bf16[1344,3072]{1,0:T(8,128)(2,1)}) %tuple.44, ...), branch_computations={%region_2.3_spmd, %region_3.4_spmd} | conditional | bytes 4915208 | solution.py:481
  27.0 3.2 enter.3
  30.2 26.2 %all_to_all.44 = bf16[16,24,3200]{2,1,0:T(8,128)(2,1)S(1)} all-to-all(bf16[16,24,3200]{2,1,0:T(8,128)(2,1)S(1)} %enter.3), channel_id=1, replica_groups=mesh['section'=2,'dp'=16,'expert'=4] {'dp'}, dimensions={0} | all-to-all | bytes 4915200 | tf_op jit(solution)/shard_map/cond/branch_0_fun/all_to_all | solution.py:456
  56.3 13.4 %expert_forward.1 = (bf16[16,24,3200]{2,1,0:T(8,128)(2,1)S(1)}, bf16[400,1344]{1,0:T(8,128)(2,1)S(1)}) custom-call(bf16[16,24,3200]{2,1,0:T(8,128)(2,1)S(1)} %get-tuple-element.91.refs_0_.refs_2_, bf16[1344,3072]{1,0:T(8,128)(2,1)} %bitcast.30, bf16[1344,3072]{1,0:T(8,128)(2,1)} %bitcast.34, ...), custom_call_target="tpu_custom_call" | custom-call | flops 6606028800 | bytes 21430272 | tf_op jit(solution)/shard_map/expert_forward/pallas_call | solution.py:225
  72.2 3.7 %all-to-all-start.2 = ((bf16[16,24,3200]{2,1,0:T(8,128)(2,1)}), bf16[16,24,3200]{2,1,0:T(8,128)(2,1)S(1)}, u32[]{:S(2)}, u32[]{:S(2)}) async-start(bf16[16,24,3200]{2,1,0:T(8,128)(2,1)} %copy-done.8), calls=%async_computation.2 | async-start | bytes 4915200 | tf_op jit(solution)/shard_map/all_to_all | solution.py:456
  77.0 2.4 spread.1
  79.4 21.7 %all-to-all-done.2.refs_1_ = bf16[16,24,3200]{2,1,0:T(8,128)(2,1)S(1)} async-done(((bf16[16,24,3200]{2,1,0:T(8,128)(2,1)}), bf16[16,24,3200]{2,1,0:T(8,128)(2,1)S(1)}, u32[]{:S(2)}, u32[]{:S(2)}) %all-to-all-start.2) | async-done | bytes 2457632 | tf_op jit(solution)/shard_map/all_to_all | solution.py:456
  101.0 6.2 %all-to-all-start.3 = ((bf16[16,24,3200]{2,1,0:T(8,128)(2,1)}), bf16[16,24,3200]{2,1,0:T(8,128)(2,1)}, u32[]{:S(2)}, u32[]{:S(2)}) async-start(bf16[16,24,3200]{2,1,0:T(8,128)(2,1)} %spread.1), calls=%async_computation.3 | async-start | bytes 4915200 | tf_op jit(solution)/shard_map/all_to_all | solution.py:456
  108.9 3.8 %collective-permute-start.6 = (bf16[64,3072]{1,0:T(8,128)(2,1)S(1)}, bf16[64,3072]{1,0:T(8,128)(2,1)S(1)}, u32[]{:S(2)}, u32[]{:S(2)}) collective-permute-start(bf16[64,3072]{1,0:T(8,128)(2,1)S(1)} %home.3.refs_1_), channel_id=1, source_target_pairs={{0,3},{1,0},{2,1},{3,2},{4,7},{5,4},{6,5},{7,6},{8,11},{9,8},{10,9... | collective-permute-start | bytes 1179656 | tf_op jit(solution)/shard_map/ppermute | solution.py:460
  114.0 7.6 %collective-permute-done.6.refs_4_ = bf16[64,3072]{1,0:T(8,128)(2,1)S(1)} collective-permute-done((bf16[64,3072]{1,0:T(8,128)(2,1)S(1)}, bf16[64,3072]{1,0:T(8,128)(2,1)S(1)}, u32[]{:S(2)}, u32[]{:S(2)}) %collective-permute-start.6) | collective-permute-done | bytes 393248 | tf_op jit(solution)/shard_map/ppermute | solution.py:460
  121.6 3.5 %collective-permute-done.5.refs_3_ = bf16[64,3072]{1,0:T(8,128)(2,1)S(1)} collective-permute-done((bf16[64,3072]{1,0:T(8,128)(2,1)S(1)}, bf16[64,3072]{1,0:T(8,128)(2,1)S(1)}, u32[]{:S(2)}, u32[]{:S(2)}) %collective-permute-start.5) | collective-permute-done | bytes 393248 | tf_op jit(solution)/shard_map/ppermute | solution.py:460
  126.5 6.6 %all-to-all-done.3.refs_1_ = bf16[16,24,3200]{2,1,0:T(8,128)(2,1)} async-done(((bf16[16,24,3200]{2,1,0:T(8,128)(2,1)}), bf16[16,24,3200]{2,1,0:T(8,128)(2,1)}, u32[]{:S(2)}, u32[]{:S(2)}) %all-to-all-start.3) | async-done | bytes 2457632 | tf_op jit(solution)/shard_map/all_to_all | solution.py:456
  133.1 25.0 %all_to_all.45.refs_0_ = bf16[16,24,3200]{2,1,0:T(8,128)(2,1)} all-to-all(bf16[16,24,3200]{2,1,0:T(8,128)(2,1)S(1)} %get-tuple-element.62), channel_id=1, replica_groups=mesh['section'=2,'dp'=16,'expert'=4] {'dp'}, dimensions={0} | all-to-all | bytes 4915200 | tf_op jit(solution)/shard_map/all_to_all | solution.py:456
  158.1 24.3 %expert_both.1 = (bf16[16,24,3200]{2,1,0:T(8,128)(2,1)S(1)}, bf16[16,24,3200]{2,1,0:T(8,128)(2,1)S(1)}) custom-call(bf16[16,24,3200]{2,1,0:T(8,128)(2,1)} %all_to_all.45.refs_0_, bf16[16,24,3200]{2,1,0:T(8,128)(2,1)} %all-to-all-done.3.refs_1_, bf16[1344,3072]{1,0:T(8,128)(2,1)} %bitcast.31, bf16[1344,3072]{1,0:T(8,128)(2,1)} %bitcast.35, ...), custom_call_target="tpu_custom_call" | custom-call | flops 13212057600 | bytes 21430272 | tf_op jit(solution)/shard_map/expert_both/pallas_call | solution.py:225
  182.4 28.9 %all_to_all.46.refs_1_ = bf16[16,24,3200]{2,1,0:T(8,128)(2,1)} all-to-all(bf16[16,24,3200]{2,1,0:T(8,128)(2,1)S(1)} %get-tuple-element.64), channel_id=1, replica_groups=mesh['section'=2,'dp'=16,'expert'=4] {'dp'}, dimensions={0} | all-to-all | bytes 4915200 | tf_op jit(solution)/shard_map/all_to_all | solution.py:456
  211.3 3.7 %all-to-all-start.6 = ((bf16[16,24,3200]{2,1,0:T(8,128)(2,1)}), bf16[16,24,3200]{2,1,0:T(8,128)(2,1)S(1)}, u32[]{:S(2)}, u32[]{:S(2)}) async-start(bf16[16,24,3200]{2,1,0:T(8,128)(2,1)} %copy-done.7), calls=%async_computation.6 | async-start | bytes 4915200 | tf_op jit(solution)/shard_map/all_to_all | solution.py:456
  217.4 3.8 %collective-permute-start.13 = (bf16[64,3072]{1,0:T(8,128)(2,1)S(1)}, bf16[64,3072]{1,0:T(8,128)(2,1)S(1)}, u32[]{:S(2)}, u32[]{:S(2)}) collective-permute-start(bf16[64,3072]{1,0:T(8,128)(2,1)S(1)} %home.5.refs_2_), channel_id=1, source_target_pairs={{0,3},{1,0},{2,1},{3,2},{4,7},{5,4},{6,5},{7,6},{8,11},{9,8},{10,9... | collective-permute-start | bytes 1179656 | tf_op jit(solution)/shard_map/ppermute | solution.py:460
  222.5 7.6 %collective-permute-done.13.refs_5_ = bf16[64,3072]{1,0:T(8,128)(2,1)S(1)} collective-permute-done((bf16[64,3072]{1,0:T(8,128)(2,1)S(1)}, bf16[64,3072]{1,0:T(8,128)(2,1)S(1)}, u32[]{:S(2)}, u32[]{:S(2)}) %collective-permute-start.13) | collective-permute-done | bytes 393248 | tf_op jit(solution)/shard_map/ppermute | solution.py:460
  230.1 3.1 collective-permute-done.12.refs_4_
  237.1 2.6 all-to-all-done.6.refs_1_
  239.7 5.8 %all-to-all-start.7 = ((bf16[16,24,3328]{2,1,0:T(8,128)(2,1)}), bf16[16,24,3328]{2,1,0:T(8,128)(2,1)}, u32[]{:S(2)}, u32[]{:S(2)}) async-start(bf16[16,24,3328]{2,1,0:T(8,128)(2,1)} %copy-done.5), calls=%async_computation.7 | async-start | bytes 5111808 | tf_op jit(solution)/shard_map/all_to_all | solution.py:456
  246.2 3.8 %collective-permute-start.9 = (bf16[64,3072]{1,0:T(8,128)(2,1)S(1)}, bf16[64,3072]{1,0:T(8,128)(2,1)S(1)}, u32[]{:S(2)}, u32[]{:S(2)}) collective-permute-start(bf16[64,3072]{1,0:T(8,128)(2,1)S(1)} %home.4), channel_id=1, source_target_pairs={{0,3},{1,0},{2,1},{3,2},{4,7},{5,4},{6,5},{7,6},{8,11},{9,8},{10,9... | collective-permute-start | bytes 1179656 | tf_op jit(solution)/shard_map/ppermute | solution.py:460
  251.3 7.6 %collective-permute-done.9 = bf16[64,3072]{1,0:T(8,128)(2,1)S(1)} collective-permute-done((bf16[64,3072]{1,0:T(8,128)(2,1)S(1)}, bf16[64,3072]{1,0:T(8,128)(2,1)S(1)}, u32[]{:S(2)}, u32[]{:S(2)}) %collective-permute-start.9) | collective-permute-done | bytes 393248 | tf_op jit(solution)/shard_map/ppermute | solution.py:460
  259.0 3.1 collective-permute-done.8
  263.1 5.4 %all-to-all-done.7.refs_0_ = bf16[16,24,3328]{2,1,0:T(8,128)(2,1)} async-done(((bf16[16,24,3328]{2,1,0:T(8,128)(2,1)}), bf16[16,24,3328]{2,1,0:T(8,128)(2,1)}, u32[]{:S(2)}, u32[]{:S(2)}) %all-to-all-start.7) | async-done | bytes 2555936 | tf_op jit(solution)/shard_map/all_to_all | solution.py:456
  268.6 14.9 %expert_backward.1 = (bf16[16,24,3328]{2,1,0:T(8,128)(2,1)S(1)}, f32[24,128]{1,0:T(8,128)S(1)}) custom-call(bf16[16,24,3328]{2,1,0:T(8,128)(2,1)} %all-to-all-done.7.refs_0_, bf16[400,1344]{1,0:T(8,128)(2,1)S(1)} %copy-done.12, bf16[16,24,3200]{2,1,0:T(8,128)(2,1)} %copy-done.15, bf16[64,3072]{1,0:T(8,128)(2,1)S(1)} %get-tuple-element.75.refs_3_, ...), custom_call_target="tpu_custom_call" | custom-call | flops 6606028800 | bytes 21430272 | tf_op jit(solution)/shard_map/expert_backward/pallas_call | solution.py:225
  284.9 3.7 %all-to-all-start.8 = ((bf16[16,24,3328]{2,1,0:T(8,128)(2,1)}), bf16[16,24,3328]{2,1,0:T(8,128)(2,1)S(1)}, u32[]{:S(2)}, u32[]{:S(2)}) async-start(bf16[16,24,3328]{2,1,0:T(8,128)(2,1)} %copy-done.6), calls=%async_computation.8 | async-start | bytes 5111808 | tf_op jit(solution)/shard_map/all_to_all | solution.py:456
  291.6 24.0 %all-to-all-done.8.refs_1_ = bf16[16,24,3328]{2,1,0:T(8,128)(2,1)S(1)} async-done(((bf16[16,24,3328]{2,1,0:T(8,128)(2,1)}), bf16[16,24,3328]{2,1,0:T(8,128)(2,1)S(1)}, u32[]{:S(2)}, u32[]{:S(2)}) %all-to-all-start.8) | async-done | bytes 2555936 | tf_op jit(solution)/shard_map/all_to_all | solution.py:456
  318.0 3.8 %collective-permute-start.20 = (f32[24,128]{1,0:T(8,128)S(1)}, f32[24,128]{1,0:T(8,128)S(1)}, u32[]{:S(2)}, u32[]{:S(2)}) collective-permute-start(f32[24,128]{1,0:T(8,128)S(1)} %get-tuple-element.72), channel_id=1, source_target_pairs={{0,3},{1,0},{2,1},{3,2},{4,7},{5,4},{6,5},{7,6},{8,11},{9,8},{10,9... | collective-permute-start | bytes 36872 | tf_op jit(solution)/shard_map/ppermute | solution.py:460
  331.0 6.5 %collective-permute-done.15.refs_4_ = bf16[64,3072]{1,0:T(8,128)(2,1)S(1)} collective-permute-done((bf16[64,3072]{1,0:T(8,128)(2,1)}, bf16[64,3072]{1,0:T(8,128)(2,1)S(1)}, u32[]{:S(2)}, u32[]{:S(2)}) %collective-permute-start.15) | collective-permute-done | bytes 393248 | tf_op jit(solution)/shard_map/ppermute | solution.py:460
  (101 shorter events, 49.0 us)
Async XLA Ops:
  0.6 15.3 %collective-permute-start.2 = (bf16[1344,3072]{1,0:T(8,128)(2,1)}, bf16[1344,3072]{1,0:T(8,128)(2,1)}, u32[]{:S(2)}, u32[]{:S(2)}) collective-permute-start(bf16[1344,3072]{1,0:T(8,128)(2,1)} %bitcast.29), channel_id=1, source_target_pairs={{0,64},{64,0},{1,65},{65,1},{2,66},{66,2},{3,67},{67,3},{4,68},{68... | collective-permute-start | bytes 24772616 | tf_op jit(solution)/shard_map/ppermute | solution.py:406
  2.1 24.8 %collective-permute-start.3 = (bf16[1344,3072]{1,0:T(8,128)(2,1)}, bf16[1344,3072]{1,0:T(8,128)(2,1)}, u32[]{:S(2)}, u32[]{:S(2)}) collective-permute-start(bf16[1344,3072]{1,0:T(8,128)(2,1)} %bitcast.33), channel_id=1, source_target_pairs={{0,64},{64,0},{1,65},{65,1},{2,66},{66,2},{3,67},{67,3},{4,68},{68... | collective-permute-start | bytes 24772616 | tf_op jit(solution)/shard_map/ppermute | solution.py:406
  3.6 12.4 %collective-permute-start.1 = (f32[1,3072]{1,0:T(1,128)}, f32[1,3072]{1,0:T(1,128)S(1)}, u32[]{:S(2)}, u32[]{:S(2)}) collective-permute-start(f32[1,3072]{1,0:T(1,128)} %convert_element_type.26), channel_id=1, source_target_pairs={{0,64},{64,0},{1,65},{65,1},{2,66},{66,2},{3,67},{67,3},{4,68},{68... | collective-permute-start | bytes 36872 | tf_op jit(solution)/shard_map/ppermute | solution.py:406
  4.8 10.0 %collective-permute-start = (s32[64,13]{1,0:T(8,128)S(1)}, s32[64,13]{1,0:T(8,128)S(1)}, u32[]{:S(2)}, u32[]{:S(2)}) collective-permute-start(s32[64,13]{1,0:T(8,128)S(1)} %bitcast.37), channel_id=1, source_target_pairs={{0,64},{64,0},{1,65},{65,1},{2,66},{66,2},{3,67},{67,3},{4,68},{68... | collective-permute-start | bytes 9992 | tf_op jit(solution)/shard_map/ppermute | solution.py:406
  7.1 19.9 %copy-start.16 = (bf16[64,3072]{1,0:T(8,128)(2,1)S(1)}, bf16[64,3072]{1,0:T(8,128)(2,1)}, u32[]{:S(2)}) copy-start(bf16[64,3072]{1,0:T(8,128)(2,1)} %dynamic-slice_bitcast_fusion.1.refs_0_) | copy-start | bytes 1179652
  56.3 13.4 %copy-start.15 = (bf16[16,24,3200]{2,1,0:T(8,128)(2,1)}, bf16[16,24,3200]{2,1,0:T(8,128)(2,1)S(1)}, u32[]{:S(2)}) copy-start(bf16[16,24,3200]{2,1,0:T(8,128)(2,1)S(1)} %get-tuple-element.91.refs_0_.refs_2_) | copy-start | bytes 7372804
  72.2 28.8 %all-to-all-start.2 = ((bf16[16,24,3200]{2,1,0:T(8,128)(2,1)}), bf16[16,24,3200]{2,1,0:T(8,128)(2,1)S(1)}, u32[]{:S(2)}, u32[]{:S(2)}) async-start(bf16[16,24,3200]{2,1,0:T(8,128)(2,1)} %copy-done.8), calls=%async_computation.2 | async-start | bytes 4915200 | tf_op jit(solution)/shard_map/all_to_all | solution.py:456
  101.0 32.0 %all-to-all-start.3 = ((bf16[16,24,3200]{2,1,0:T(8,128)(2,1)}), bf16[16,24,3200]{2,1,0:T(8,128)(2,1)}, u32[]{:S(2)}, u32[]{:S(2)}) async-start(bf16[16,24,3200]{2,1,0:T(8,128)(2,1)} %spread.1), calls=%async_computation.3 | async-start | bytes 4915200 | tf_op jit(solution)/shard_map/all_to_all | solution.py:456
  107.2 17.9 %copy-start.17 = (bf16[64,3072]{1,0:T(8,128)(2,1)S(1)}, bf16[64,3072]{1,0:T(8,128)(2,1)}, u32[]{:S(2)}) copy-start(bf16[64,3072]{1,0:T(8,128)(2,1)} %dynamic-slice_bitcast_fusion.1.refs_0_) | copy-start | bytes 1179652
  108.9 12.8 %collective-permute-start.6 = (bf16[64,3072]{1,0:T(8,128)(2,1)S(1)}, bf16[64,3072]{1,0:T(8,128)(2,1)S(1)}, u32[]{:S(2)}, u32[]{:S(2)}) collective-permute-start(bf16[64,3072]{1,0:T(8,128)(2,1)S(1)} %home.3.refs_1_), channel_id=1, source_target_pairs={{0,3},{1,0},{2,1},{3,2},{4,7},{5,4},{6,5},{7,6},{8,11},{9,8},{10,9... | collective-permute-start | bytes 1179656 | tf_op jit(solution)/shard_map/ppermute | solution.py:460
  112.7 12.5 %collective-permute-start.5 = (bf16[64,3072]{1,0:T(8,128)(2,1)S(1)}, bf16[64,3072]{1,0:T(8,128)(2,1)S(1)}, u32[]{:S(2)}, u32[]{:S(2)}) collective-permute-start(bf16[64,3072]{1,0:T(8,128)(2,1)S(1)} %home.3.refs_1_), channel_id=1, source_target_pairs={{0,1},{1,2},{2,3},{3,0},{4,5},{5,6},{6,7},{7,4},{8,9},{9,10},{10,1... | collective-permute-start | bytes 1179656 | tf_op jit(solution)/shard_map/ppermute | solution.py:460
  112.7 12.5 %collective-permute-start.4 = (bf16[64,3072]{1,0:T(8,128)(2,1)S(1)}, bf16[64,3072]{1,0:T(8,128)(2,1)S(1)}, u32[]{:S(2)}, u32[]{:S(2)}) collective-permute-start(bf16[64,3072]{1,0:T(8,128)(2,1)S(1)} %home.3.refs_1_), channel_id=1, source_target_pairs={{0,2},{1,3},{2,0},{3,1},{4,6},{5,7},{6,4},{7,5},{8,10},{9,11},{10,... | collective-permute-start | bytes 1179656 | tf_op jit(solution)/shard_map/ppermute | solution.py:460
  182.3 28.9 %copy-start.7 = (bf16[16,24,3200]{2,1,0:T(8,128)(2,1)}, bf16[16,24,3200]{2,1,0:T(8,128)(2,1)S(1)}, u32[]{:S(2)}) copy-start(bf16[16,24,3200]{2,1,0:T(8,128)(2,1)S(1)} %get-tuple-element.65) | copy-start | bytes 7372804
  211.3 28.4 %all-to-all-start.6 = ((bf16[16,24,3200]{2,1,0:T(8,128)(2,1)}), bf16[16,24,3200]{2,1,0:T(8,128)(2,1)S(1)}, u32[]{:S(2)}, u32[]{:S(2)}) async-start(bf16[16,24,3200]{2,1,0:T(8,128)(2,1)} %copy-done.7), calls=%async_computation.6 | async-start | bytes 4915200 | tf_op jit(solution)/shard_map/all_to_all | solution.py:456
  217.4 12.8 %collective-permute-start.13 = (bf16[64,3072]{1,0:T(8,128)(2,1)S(1)}, bf16[64,3072]{1,0:T(8,128)(2,1)S(1)}, u32[]{:S(2)}, u32[]{:S(2)}) collective-permute-start(bf16[64,3072]{1,0:T(8,128)(2,1)S(1)} %home.5.refs_2_), channel_id=1, source_target_pairs={{0,3},{1,0},{2,1},{3,2},{4,7},{5,4},{6,5},{7,6},{8,11},{9,8},{10,9... | collective-permute-start | bytes 1179656 | tf_op jit(solution)/shard_map/ppermute | solution.py:460
  221.2 12.1 %collective-permute-start.12 = (bf16[64,3072]{1,0:T(8,128)(2,1)S(1)}, bf16[64,3072]{1,0:T(8,128)(2,1)S(1)}, u32[]{:S(2)}, u32[]{:S(2)}) collective-permute-start(bf16[64,3072]{1,0:T(8,128)(2,1)S(1)} %home.5.refs_2_), channel_id=1, source_target_pairs={{0,1},{1,2},{2,3},{3,0},{4,5},{5,6},{6,7},{7,4},{8,9},{9,10},{10,1... | collective-permute-start | bytes 1179656 | tf_op jit(solution)/shard_map/ppermute | solution.py:460
  221.2 12.1 %collective-permute-start.11 = (bf16[64,3072]{1,0:T(8,128)(2,1)S(1)}, bf16[64,3072]{1,0:T(8,128)(2,1)S(1)}, u32[]{:S(2)}, u32[]{:S(2)}) collective-permute-start(bf16[64,3072]{1,0:T(8,128)(2,1)S(1)} %home.5.refs_2_), channel_id=1, source_target_pairs={{0,2},{1,3},{2,0},{3,1},{4,6},{5,7},{6,4},{7,5},{8,10},{9,11},{10,... | collective-permute-start | bytes 1179656 | tf_op jit(solution)/shard_map/ppermute | solution.py:460
  239.7 28.9 %all-to-all-start.7 = ((bf16[16,24,3328]{2,1,0:T(8,128)(2,1)}), bf16[16,24,3328]{2,1,0:T(8,128)(2,1)}, u32[]{:S(2)}, u32[]{:S(2)}) async-start(bf16[16,24,3328]{2,1,0:T(8,128)(2,1)} %copy-done.5), calls=%async_computation.7 | async-start | bytes 5111808 | tf_op jit(solution)/shard_map/all_to_all | solution.py:456
  246.2 22.4 %copy-start.12 = (bf16[400,1344]{1,0:T(8,128)(2,1)S(1)}, bf16[400,1344]{1,0:T(8,128)(2,1)}, u32[]{:S(2)}) copy-start(bf16[400,1344]{1,0:T(8,128)(2,1)} %copy-done.11) | copy-start | bytes 3225604
  246.2 12.8 %collective-permute-start.9 = (bf16[64,3072]{1,0:T(8,128)(2,1)S(1)}, bf16[64,3072]{1,0:T(8,128)(2,1)S(1)}, u32[]{:S(2)}, u32[]{:S(2)}) collective-permute-start(bf16[64,3072]{1,0:T(8,128)(2,1)S(1)} %home.4), channel_id=1, source_target_pairs={{0,3},{1,0},{2,1},{3,2},{4,7},{5,4},{6,5},{7,6},{8,11},{9,8},{10,9... | collective-permute-start | bytes 1179656 | tf_op jit(solution)/shard_map/ppermute | solution.py:460
  250.0 12.1 %collective-permute-start.8 = (bf16[64,3072]{1,0:T(8,128)(2,1)S(1)}, bf16[64,3072]{1,0:T(8,128)(2,1)S(1)}, u32[]{:S(2)}, u32[]{:S(2)}) collective-permute-start(bf16[64,3072]{1,0:T(8,128)(2,1)S(1)} %home.4), channel_id=1, source_target_pairs={{0,1},{1,2},{2,3},{3,0},{4,5},{5,6},{6,7},{7,4},{8,9},{9,10},{10,1... | collective-permute-start | bytes 1179656 | tf_op jit(solution)/shard_map/ppermute | solution.py:460
  250.0 12.1 %collective-permute-start.7 = (bf16[64,3072]{1,0:T(8,128)(2,1)S(1)}, bf16[64,3072]{1,0:T(8,128)(2,1)S(1)}, u32[]{:S(2)}, u32[]{:S(2)}) collective-permute-start(bf16[64,3072]{1,0:T(8,128)(2,1)S(1)} %home.4), channel_id=1, source_target_pairs={{0,2},{1,3},{2,0},{3,1},{4,6},{5,7},{6,4},{7,5},{8,10},{9,11},{10,... | collective-permute-start | bytes 1179656 | tf_op jit(solution)/shard_map/ppermute | solution.py:460
  284.9 30.7 %all-to-all-start.8 = ((bf16[16,24,3328]{2,1,0:T(8,128)(2,1)}), bf16[16,24,3328]{2,1,0:T(8,128)(2,1)S(1)}, u32[]{:S(2)}, u32[]{:S(2)}) async-start(bf16[16,24,3328]{2,1,0:T(8,128)(2,1)} %copy-done.6), calls=%async_computation.8 | async-start | bytes 5111808 | tf_op jit(solution)/shard_map/all_to_all | solution.py:456
  288.6 2.2 collective-permute-start.10
  318.0 7.0 %collective-permute-start.20 = (f32[24,128]{1,0:T(8,128)S(1)}, f32[24,128]{1,0:T(8,128)S(1)}, u32[]{:S(2)}, u32[]{:S(2)}) collective-permute-start(f32[24,128]{1,0:T(8,128)S(1)} %get-tuple-element.72), channel_id=1, source_target_pairs={{0,3},{1,0},{2,1},{3,2},{4,7},{5,4},{6,5},{7,6},{8,11},{9,8},{10,9... | collective-permute-start | bytes 36872 | tf_op jit(solution)/shard_map/ppermute | solution.py:460
  321.8 7.1 %collective-permute-start.19 = (f32[24,128]{1,0:T(8,128)S(1)}, f32[24,128]{1,0:T(8,128)S(1)}, u32[]{:S(2)}, u32[]{:S(2)}) collective-permute-start(f32[24,128]{1,0:T(8,128)S(1)} %get-tuple-element.72), channel_id=1, source_target_pairs={{0,1},{1,2},{2,3},{3,0},{4,5},{5,6},{6,7},{7,4},{8,9},{9,10},{10,1... | collective-permute-start | bytes 36872 | tf_op jit(solution)/shard_map/ppermute | solution.py:460
  321.8 7.1 %collective-permute-start.18 = (f32[24,128]{1,0:T(8,128)S(1)}, f32[24,128]{1,0:T(8,128)S(1)}, u32[]{:S(2)}, u32[]{:S(2)}) collective-permute-start(f32[24,128]{1,0:T(8,128)S(1)} %get-tuple-element.72), channel_id=1, source_target_pairs={{0,2},{1,3},{2,0},{3,1},{4,6},{5,7},{6,4},{7,5},{8,10},{9,11},{10,... | collective-permute-start | bytes 36872 | tf_op jit(solution)/shard_map/ppermute | solution.py:460
  323.1 7.9 %collective-permute-start.16 = (bf16[64,3072]{1,0:T(8,128)(2,1)}, bf16[64,3072]{1,0:T(8,128)(2,1)S(1)}, u32[]{:S(2)}, u32[]{:S(2)}) collective-permute-start(bf16[64,3072]{1,0:T(8,128)(2,1)} %copy-done.13), channel_id=1, source_target_pairs={{0,3},{1,0},{2,1},{3,2},{4,7},{5,4},{6,5},{7,6},{8,11},{9,8},{10,9... | collective-permute-start | bytes 1179656 | tf_op jit(solution)/shard_map/ppermute | solution.py:460
  324.5 13.1 %collective-permute-start.15 = (bf16[64,3072]{1,0:T(8,128)(2,1)}, bf16[64,3072]{1,0:T(8,128)(2,1)S(1)}, u32[]{:S(2)}, u32[]{:S(2)}) collective-permute-start(bf16[64,3072]{1,0:T(8,128)(2,1)} %copy-done.13), channel_id=1, source_target_pairs={{0,1},{1,2},{2,3},{3,0},{4,5},{5,6},{6,7},{7,4},{8,9},{9,10},{10,1... | collective-permute-start | bytes 1179656 | tf_op jit(solution)/shard_map/ppermute | solution.py:460
  325.1 12.5 %collective-permute-start.14 = (bf16[64,3072]{1,0:T(8,128)(2,1)}, bf16[64,3072]{1,0:T(8,128)(2,1)S(1)}, u32[]{:S(2)}, u32[]{:S(2)}) collective-permute-start(bf16[64,3072]{1,0:T(8,128)(2,1)} %copy-done.13), channel_id=1, source_target_pairs={{0,2},{1,3},{2,0},{3,1},{4,6},{5,7},{6,4},{7,5},{8,10},{9,11},{10,... | collective-permute-start | bytes 1179656 | tf_op jit(solution)/shard_map/ppermute | solution.py:460
  341.3 2.4 collective-permute-start.17
  341.4 1.7 collective-permute-start.21
  (14 other events, 26.2 us)

commit v4 on v3

--- a/solution.py
+++ b/solution.py
@@ -319,6 +319,25 @@
     )(*inputs, *awaits)
 
 
+def in_turn(value, awaited):
+    def kernel(_, ref, out, tile, sem):
+        part = (0,) * (len(ref.shape) - 2) + (pl.ds(0, 16), pl.ds(0, LANES))
+        copy = pltpu.make_async_copy(ref.at[part], tile, sem)
+        copy.start()
+        copy.wait()
+
+    anywhere = pl.BlockSpec(memory_space=pl.ANY)
+    return pl.pallas_call(
+        kernel,
+        out_shape=jax.ShapeDtypeStruct(value.shape, value.dtype),
+        in_specs=[anywhere] * 2,
+        out_specs=anywhere,
+        scratch_shapes=[pltpu.VMEM((16, LANES), bf16), pltpu.SemaphoreType.DMA(())],
+        input_output_aliases={0: 0},
+        name="in_turn",
+    )(value, awaited)
+
+
 def pack(table, rows, out, by_lane, tails):
     width = rows.shape[1]
 
@@ -492,11 +511,11 @@
     gain0, gain1 = (pick(gain_own, gain_other, layer) for layer in range(2))
     plain0, plain1 = (pick(own_tables[0], other_tables[0], layer) for layer in range(2))
     weighted0, weighted1 = (pick(own_tables[1], other_tables[1], layer) for layer in range(2))
-    d_held1 = pallas(plain_kernel, block, tails, "spread", upstream, weighted1)
+    d_held1 = pallas(plain_kernel, block, tails, "spread", upstream, weighted1, awaits=(rows0,))
+    d_rows1 = exchange(d_held1)
 
     part0, pre0 = expert("forward", 0, weights, rows0)
-    back0 = exchange(part0)
-    d_rows1 = exchange(after(d_held1, back0))
+    back0 = exchange(in_turn(part0, d_rows1))
     sums0 = home(weighted0, back0)
     x1, held1 = pallas(
         sum_norm_kernel, [rows_shape, block], [rows, *tails], "next", x0, *sums0, gain1, plain1
@@ -504,7 +523,6 @@
     rows1 = exchange(after(held1, d_rows1))
     part1, d_part1 = expert("both", 1, weights, rows1, d_rows1)
     d_back1 = exchange(d_part1)
-    back1 = exchange(after(part1, d_back1))
     d_sums1 = home(plain1, d_back1)
     grad1, d_held0 = pallas(
         finish_pack_kernel,
@@ -517,10 +535,11 @@
         gain1,
         weighted0,
     )
-    d_rows0 = exchange(after(d_held0, back1))
+    d_rows0 = exchange(d_held0)
+    back1 = exchange(in_turn(part1, d_rows0))
+    d_part0, gain_sum1 = expert("backward", 0, weights, d_rows0, pre0, rows0, grad1)
+    d_back0 = exchange(in_turn(d_part0, back1))
     x2 = (x1.astype(f32) + four(home(weighted1, back1))).astype(bf16)
-    d_part0, gain_sum1 = expert("backward", 0, weights, d_rows0, pre0, rows0, x2)
-    d_back0 = exchange(d_part0)
     kept_x, taken_x = pick(x1, x2, 0), swapped(pick(x2, x1, 0))
     d_home0, gain_sum0 = pallas(
         home_kernel,

time: 346 us -> 343 us (level)
  blocking collectives: 80.1 us -> 104 us
  waiting for transfers between devices: 123 us -> 110 us
  starting transfers between devices: 50.5 us -> 41.5 us
  local copies, waits for them, and re-layouts: 14.7 us -> 9.07 us
    all_to_all x3 -> x4, blocking collectives: 80.1 us -> 104 us  [exchange(): return lax.all_to_all(held, 'dp', split_axis=0, concat_axis=0, tiled=True)]
    all_to_all x5 -> x4, waiting for transfers between devices: 60.2 us -> 46.9 us  [exchange(): return lax.all_to_all(held, 'dp', split_axis=0, concat_axis=0, tiled=True)]
    ppermute x15, starting transfers between devices: 24.2 us -> 18.1 us  [over_groups(): return (part, *[lax.ppermute(part, 'expert', p) for p in pairs])]
    unnamed x38 -> x46, local copies, waits for them, and re-layouts: 12.4 us -> 6.76 us
    all_to_all x5 -> x4, starting transfers between devices: 23.2 us -> 20.6 us  [exchange(): return lax.all_to_all(held, 'dp', split_axis=0, concat_axis=0, tiled=True)]
  transfers between devices with their start and end apart: 27 -> 26, of which waited for: 18 -> 17; matrix products, arithmetic and copies ran while one was open for 3% -> 3% of each run, Pallas kernels for 3% -> 9%
where the time goes in v4:
time: 343 us; the launch traced here: 342 us
  waiting for transfers between devices  110 us (32%)
  blocking collectives  104 us (30%)
  Pallas kernels  68.6 us (20%)
  starting transfers between devices  41.5 us (12%)
  local copies, waits for them, and re-layouts  9.07 us (3%)
  other arithmetic  7.74 us (2%)
    all_to_all x4, blocking collectives, exchange(): return lax.all_to_all(held, 'dp', split_axis=0, concat_axis=0, tiled=True)  104 us
    pallas_call x3, Pallas kernels, expert(): pl.pallas_call(functools.partial(expert_kernel, mode, layer, len(inputs),...  52 us
    all_to_all x4, waiting for transfers between devices, exchange(): return lax.all_to_all(held, 'dp', split_axis=0, concat_axis=0, tiled=True)  46.9 us
    ppermute x15, waiting for transfers between devices, over_groups(): return (part, *[lax.ppermute(part, 'expert', p) for p in pairs])  42.3 us
    ppermute x7, waiting for transfers between devices, swapped(): return lax.ppermute(x, 'section', SWAP)  20.9 us
    all_to_all x4, starting transfers between devices, exchange(): return lax.all_to_all(held, 'dp', split_axis=0, concat_axis=0, tiled=True)  20.6 us
    ppermute x15, starting transfers between devices, over_groups(): return (part, *[lax.ppermute(part, 'expert', p) for p in pairs])  18.1 us
    pallas_call x11, Pallas kernels, pallas(): pl.pallas_call(body, out_shape=out_shape, in_specs=[vmem] * len(inputs) +...  14.6 us
  transfers between devices with their start and end apart: 26, of which 17 were waited for; matrix products, arithmetic and copies ran while one was open for 3% of the time, Pallas kernels for 9%

profile of v4, /device:TPU:1, one launch (start us, length us, event | category | flops | bytes accessed | tf_op | source)
XLA Modules:
  0.0 341.8 jit_solution(1391367567701579317)
XLA Ops:
  7.5 7.3 %collective-permute-done.refs_0_ = s32[64,13]{1,0:T(8,128)S(1)} collective-permute-done((s32[64,13]{1,0:T(8,128)S(1)}, s32[64,13]{1,0:T(8,128)S(1)}, u32[]{:S(2)}, u32[]{:S(2)}) %collective-permute-start) | collective-permute-done | bytes 3360 | tf_op jit(solution)/shard_map/ppermute | solution.py:425
  15.4 11.6 %collective-permute-done.3.refs_4_.refs_5_.refs_7_ = bf16[1344,3072]{1,0:T(8,128)(2,1)} collective-permute-done((bf16[1344,3072]{1,0:T(8,128)(2,1)}, bf16[1344,3072]{1,0:T(8,128)(2,1)}, u32[]{:S(2)}, u32[]{:S(2)}) %collective-permute-start.3) | collective-permute-done | bytes 8257568 | tf_op jit(solution)/shard_map/ppermute | solution.py:425
  27.0 34.6 %conditional.3 = (bf16[16,24,3200]{2,1,0:T(8,128)(2,1)S(1)}) conditional(s32[]{:T(128)} %convert_element_type.25, (bf16[64,3072]{1,0:T(8,128)(2,1)S(1)}, f32[1,3072]{1,0:T(1,128)S(1)}, bf16[64,400]{1,0:T(8,128)(2,1)S(1)}, bf16[1344,3072]{1,0:T(8,128)(2,1)}, bf16[1344,3072]{1,0:T(8,128)(2,1)}) %tuple.38, ...), branch_computations={%region_2.3_spmd, %region_3.4_spmd} | conditional | bytes 4915208 | solution.py:500
  27.0 2.4 enter.3
  29.3 32.3 %all_to_all.44 = bf16[16,24,3200]{2,1,0:T(8,128)(2,1)S(1)} all-to-all(bf16[16,24,3200]{2,1,0:T(8,128)(2,1)S(1)} %enter.3), channel_id=1, replica_groups=mesh['section'=2,'dp'=16,'expert'=4] {'dp'}, dimensions={0} | all-to-all | bytes 4915200 | tf_op jit(solution)/shard_map/cond/branch_0_fun/all_to_all | solution.py:475
  61.6 2.3 spread.1
  63.9 4.5 %all-to-all-start.2 = ((bf16[16,24,3200]{2,1,0:T(8,128)(2,1)}), bf16[16,24,3200]{2,1,0:T(8,128)(2,1)}, u32[]{:S(2)}, u32[]{:S(2)}) async-start(bf16[16,24,3200]{2,1,0:T(8,128)(2,1)} %spread.1), calls=%async_computation.2 | async-start | bytes 4915200 | tf_op jit(solution)/shard_map/all_to_all | solution.py:475
  68.4 12.8 %expert_forward.1 = (bf16[16,24,3200]{2,1,0:T(8,128)(2,1)S(1)}, bf16[400,1344]{1,0:T(8,128)(2,1)S(1)}) custom-call(bf16[16,24,3200]{2,1,0:T(8,128)(2,1)S(1)} %get-tuple-element.85.refs_0_.refs_2_, bf16[1344,3072]{1,0:T(8,128)(2,1)} %bitcast.30, bf16[1344,3072]{1,0:T(8,128)(2,1)} %bitcast.34, ...), custom_call_target="tpu_custom_call" | custom-call | flops 6606028800 | bytes 21430272 | tf_op jit(solution)/shard_map/expert_forward/pallas_call | solution.py:225
  83.7 11.3 %all-to-all-done.2.ref.refs_1_ = bf16[16,24,3200]{2,1,0:T(8,128)(2,1)} async-done(((bf16[16,24,3200]{2,1,0:T(8,128)(2,1)}), bf16[16,24,3200]{2,1,0:T(8,128)(2,1)}, u32[]{:S(2)}, u32[]{:S(2)}) %all-to-all-start.2) | async-done | bytes 2457632 | tf_op jit(solution)/shard_map/all_to_all | solution.py:475
  95.7 6.0 %all-to-all-start.3 = ((bf16[16,24,3200]{2,1,0:T(8,128)(2,1)}), bf16[16,24,3200]{2,1,0:T(8,128)(2,1)S(1)}, u32[]{:S(2)}, u32[]{:S(2)}) async-start(bf16[16,24,3200]{2,1,0:T(8,128)(2,1)} %in_turn.3), calls=%async_computation.3 | async-start | bytes 4915200 | tf_op jit(solution)/shard_map/all_to_all | solution.py:475
  101.8 22.2 %all-to-all-done.3.refs_1_ = bf16[16,24,3200]{2,1,0:T(8,128)(2,1)S(1)} async-done(((bf16[16,24,3200]{2,1,0:T(8,128)(2,1)}), bf16[16,24,3200]{2,1,0:T(8,128)(2,1)S(1)}, u32[]{:S(2)}, u32[]{:S(2)}) %all-to-all-start.3) | async-done | bytes 2457632 | tf_op jit(solution)/shard_map/all_to_all | solution.py:475
  124.7 3.8 %collective-permute-start.6 = (bf16[64,3072]{1,0:T(8,128)(2,1)S(1)}, bf16[64,3072]{1,0:T(8,128)(2,1)S(1)}, u32[]{:S(2)}, u32[]{:S(2)}) collective-permute-start(bf16[64,3072]{1,0:T(8,128)(2,1)S(1)} %home.3.refs_1_), channel_id=1, source_target_pairs={{0,3},{1,0},{2,1},{3,2},{4,7},{5,4},{6,5},{7,6},{8,11},{9,8},{10,9... | collective-permute-start | bytes 1179656 | tf_op jit(solution)/shard_map/ppermute | solution.py:479
  129.9 7.6 %collective-permute-done.6.refs_4_ = bf16[64,3072]{1,0:T(8,128)(2,1)S(1)} collective-permute-done((bf16[64,3072]{1,0:T(8,128)(2,1)S(1)}, bf16[64,3072]{1,0:T(8,128)(2,1)S(1)}, u32[]{:S(2)}, u32[]{:S(2)}) %collective-permute-start.6) | collective-permute-done | bytes 393248 | tf_op jit(solution)/shard_map/ppermute | solution.py:479
  137.5 3.5 %collective-permute-done.5.refs_3_ = bf16[64,3072]{1,0:T(8,128)(2,1)S(1)} collective-permute-done((bf16[64,3072]{1,0:T(8,128)(2,1)S(1)}, bf16[64,3072]{1,0:T(8,128)(2,1)S(1)}, u32[]{:S(2)}, u32[]{:S(2)}) %collective-permute-start.5) | collective-permute-done | bytes 393248 | tf_op jit(solution)/shard_map/ppermute | solution.py:479
  141.0 2.3 next.1
  143.3 22.9 %all_to_all.45.refs_0_ = bf16[16,24,3200]{2,1,0:T(8,128)(2,1)} all-to-all(bf16[16,24,3200]{2,1,0:T(8,128)(2,1)S(1)} %get-tuple-element.58), channel_id=1, replica_groups=mesh['section'=2,'dp'=16,'expert'=4] {'dp'}, dimensions={0} | all-to-all | bytes 4915200 | tf_op jit(solution)/shard_map/all_to_all | solution.py:475
  166.2 24.3 %expert_both.1 = (bf16[16,24,3200]{2,1,0:T(8,128)(2,1)S(1)}, bf16[16,24,3200]{2,1,0:T(8,128)(2,1)S(1)}) custom-call(bf16[16,24,3200]{2,1,0:T(8,128)(2,1)} %all_to_all.45.refs_0_, bf16[16,24,3200]{2,1,0:T(8,128)(2,1)} %all-to-all-done.2.ref.refs_1_, bf16[1344,3072]{1,0:T(8,128)(2,1)} %bitcast.31, bf16[1344,3072]{1,0:T(8,128)(2,1)} %bitcast.35, ...), custom_call_target="tpu_custom_call" | custom-call | flops 13212057600 | bytes 21430272 | tf_op jit(solution)/shard_map/expert_both/pallas_call | solution.py:225
  190.5 22.1 %all_to_all.46.refs_1_ = bf16[16,24,3200]{2,1,0:T(8,128)(2,1)S(1)} all-to-all(bf16[16,24,3200]{2,1,0:T(8,128)(2,1)S(1)} %get-tuple-element.60), channel_id=1, replica_groups=mesh['section'=2,'dp'=16,'expert'=4] {'dp'}, dimensions={0} | all-to-all | bytes 4915200 | tf_op jit(solution)/shard_map/all_to_all | solution.py:475
  215.1 5.0 %collective-permute-done.9.refs_5_ = bf16[64,3072]{1,0:T(8,128)(2,1)S(1)} collective-permute-done((bf16[64,3072]{1,0:T(8,128)(2,1)S(1)}, bf16[64,3072]{1,0:T(8,128)(2,1)S(1)}, u32[]{:S(2)}, u32[]{:S(2)}) %collective-permute-start.9) | collective-permute-done | bytes 393248 | tf_op jit(solution)/shard_map/ppermute | solution.py:479
  220.1 5.8 %collective-permute-done.8.refs_4_ = bf16[64,3072]{1,0:T(8,128)(2,1)S(1)} collective-permute-done((bf16[64,3072]{1,0:T(8,128)(2,1)S(1)}, bf16[64,3072]{1,0:T(8,128)(2,1)S(1)}, u32[]{:S(2)}, u32[]{:S(2)}) %collective-permute-start.8) | collective-permute-done | bytes 393248 | tf_op jit(solution)/shard_map/ppermute | solution.py:479
  227.5 26.4 %all_to_all.47.ref.refs_0_ = bf16[16,24,3328]{2,1,0:T(8,128)(2,1)} all-to-all(bf16[16,24,3328]{2,1,0:T(8,128)(2,1)S(1)} %get-tuple-element.61), channel_id=1, replica_groups=mesh['section'=2,'dp'=16,'expert'=4] {'dp'}, dimensions={0} | all-to-all | bytes 5111808 | tf_op jit(solution)/shard_map/all_to_all | solution.py:475
  254.6 5.5 %all-to-all-start.7 = ((bf16[16,24,3200]{2,1,0:T(8,128)(2,1)}), bf16[16,24,3200]{2,1,0:T(8,128)(2,1)S(1)}, u32[]{:S(2)}, u32[]{:S(2)}) async-start(bf16[16,24,3200]{2,1,0:T(8,128)(2,1)} %in_turn.4), calls=%async_computation.7 | async-start | bytes 4915200 | tf_op jit(solution)/shard_map/all_to_all | solution.py:475
  261.4 14.9 %expert_backward.1 = (bf16[16,24,3328]{2,1,0:T(8,128)(2,1)S(1)}, f32[24,128]{1,0:T(8,128)S(1)}) custom-call(bf16[16,24,3328]{2,1,0:T(8,128)(2,1)} %all_to_all.47.ref.refs_0_, bf16[400,1344]{1,0:T(8,128)(2,1)S(1)} %copy-done.16, bf16[16,24,3200]{2,1,0:T(8,128)(2,1)} %copy-done.17, bf16[64,3072]{1,0:T(8,128)(2,1)S(1)} %copy-done.8, ...), custom_call_target="tpu_custom_call" | custom-call | flops 6606028800 | bytes 21430272 | tf_op jit(solution)/shard_map/expert_backward/pallas_call | solution.py:225
  277.7 6.6 %all-to-all-done.7.refs_1_.ref = bf16[16,24,3200]{2,1,0:T(8,128)(2,1)S(1)} async-done(((bf16[16,24,3200]{2,1,0:T(8,128)(2,1)}), bf16[16,24,3200]{2,1,0:T(8,128)(2,1)S(1)}, u32[]{:S(2)}, u32[]{:S(2)}) %all-to-all-start.7) | async-done | bytes 2457632 | tf_op jit(solution)/shard_map/all_to_all | solution.py:475
  286.5 4.6 %all-to-all-start.8 = ((bf16[16,24,3328]{2,1,0:T(8,128)(2,1)}), bf16[16,24,3328]{2,1,0:T(8,128)(2,1)}, u32[]{:S(2)}, u32[]{:S(2)}) async-start(bf16[16,24,3328]{2,1,0:T(8,128)(2,1)} %in_turn.5), calls=%async_computation.8 | async-start | bytes 5111808 | tf_op jit(solution)/shard_map/all_to_all | solution.py:475
  293.4 3.4 collective-permute-start.10
  298.6 2.7 collective-permute-done.11
  301.2 4.9 %collective-permute-done.10 = bf16[64,3072]{1,0:T(8,128)(2,1)S(1)} collective-permute-done((bf16[64,3072]{1,0:T(8,128)(2,1)S(1)}, bf16[64,3072]{1,0:T(8,128)(2,1)S(1)}, u32[]{:S(2)}, u32[]{:S(2)}) %collective-permute-start.10) | collective-permute-done | bytes 393248 | tf_op jit(solution)/shard_map/ppermute | solution.py:479
  308.9 6.8 %all-to-all-done.8.refs_1_ = bf16[16,24,3328]{2,1,0:T(8,128)(2,1)} async-done(((bf16[16,24,3328]{2,1,0:T(8,128)(2,1)}), bf16[16,24,3328]{2,1,0:T(8,128)(2,1)}, u32[]{:S(2)}, u32[]{:S(2)}) %all-to-all-start.8) | async-done | bytes 2555936 | tf_op jit(solution)/shard_map/all_to_all | solution.py:475
  315.8 2.5 home_gain.1
  326.6 7.6 %collective-permute-done.16.refs_5_ = bf16[64,3072]{1,0:T(8,128)(2,1)S(1)} collective-permute-done((bf16[64,3072]{1,0:T(8,128)(2,1)S(1)}, bf16[64,3072]{1,0:T(8,128)(2,1)S(1)}, u32[]{:S(2)}, u32[]{:S(2)}) %collective-permute-start.16) | collective-permute-done | bytes 393248 | tf_op jit(solution)/shard_map/ppermute | solution.py:479
  334.2 3.4 collective-permute-done.15.refs_4_
  (111 shorter events, 41.5 us)
Async XLA Ops:
  0.6 14.7 %collective-permute-start.2 = (bf16[1344,3072]{1,0:T(8,128)(2,1)}, bf16[1344,3072]{1,0:T(8,128)(2,1)}, u32[]{:S(2)}, u32[]{:S(2)}) collective-permute-start(bf16[1344,3072]{1,0:T(8,128)(2,1)} %bitcast.29), channel_id=1, source_target_pairs={{0,64},{64,0},{1,65},{65,1},{2,66},{66,2},{3,67},{67,3},{4,68},{68... | collective-permute-start | bytes 24772616 | tf_op jit(solution)/shard_map/ppermute | solution.py:425
  2.1 24.8 %collective-permute-start.3 = (bf16[1344,3072]{1,0:T(8,128)(2,1)}, bf16[1344,3072]{1,0:T(8,128)(2,1)}, u32[]{:S(2)}, u32[]{:S(2)}) collective-permute-start(bf16[1344,3072]{1,0:T(8,128)(2,1)} %bitcast.33), channel_id=1, source_target_pairs={{0,64},{64,0},{1,65},{65,1},{2,66},{66,2},{3,67},{67,3},{4,68},{68... | collective-permute-start | bytes 24772616 | tf_op jit(solution)/shard_map/ppermute | solution.py:425
  3.6 11.8 %collective-permute-start.1 = (f32[1,3072]{1,0:T(1,128)}, f32[1,3072]{1,0:T(1,128)S(1)}, u32[]{:S(2)}, u32[]{:S(2)}) collective-permute-start(f32[1,3072]{1,0:T(1,128)} %convert_element_type.26), channel_id=1, source_target_pairs={{0,64},{64,0},{1,65},{65,1},{2,66},{66,2},{3,67},{67,3},{4,68},{68... | collective-permute-start | bytes 36872 | tf_op jit(solution)/shard_map/ppermute | solution.py:425
  4.8 10.0 %collective-permute-start = (s32[64,13]{1,0:T(8,128)S(1)}, s32[64,13]{1,0:T(8,128)S(1)}, u32[]{:S(2)}, u32[]{:S(2)}) collective-permute-start(s32[64,13]{1,0:T(8,128)S(1)} %bitcast.37), channel_id=1, source_target_pairs={{0,64},{64,0},{1,65},{65,1},{2,66},{66,2},{3,67},{67,3},{4,68},{68... | collective-permute-start | bytes 9992 | tf_op jit(solution)/shard_map/ppermute | solution.py:425
  6.8 54.9 %copy-start.13 = (bf16[64,3072]{1,0:T(8,128)(2,1)}, bf16[64,3072]{1,0:T(8,128)(2,1)S(1)}, u32[]{:S(2)}) copy-start(bf16[64,3072]{1,0:T(8,128)(2,1)S(1)} %dynamic-slice_bitcast_fusion.refs_0_.refs_1_) | copy-start | bytes 1179652
  63.9 31.1 %all-to-all-start.2 = ((bf16[16,24,3200]{2,1,0:T(8,128)(2,1)}), bf16[16,24,3200]{2,1,0:T(8,128)(2,1)}, u32[]{:S(2)}, u32[]{:S(2)}) async-start(bf16[16,24,3200]{2,1,0:T(8,128)(2,1)} %spread.1), calls=%async_computation.2 | async-start | bytes 4915200 | tf_op jit(solution)/shard_map/all_to_all | solution.py:475
  95.7 28.3 %all-to-all-start.3 = ((bf16[16,24,3200]{2,1,0:T(8,128)(2,1)}), bf16[16,24,3200]{2,1,0:T(8,128)(2,1)S(1)}, u32[]{:S(2)}, u32[]{:S(2)}) async-start(bf16[16,24,3200]{2,1,0:T(8,128)(2,1)} %in_turn.3), calls=%async_computation.3 | async-start | bytes 4915200 | tf_op jit(solution)/shard_map/all_to_all | solution.py:475
  101.8 28.1 %copy-start.22 = (bf16[1,3072]{1,0:T(2,128)(2,1)S(1)}, bf16[1,3072]{1,0:T(2,128)(2,1)}, u32[]{:S(2)}) copy-start(bf16[1,3072]{1,0:T(2,128)(2,1)} %param.14) | copy-start | bytes 18436
  124.7 12.8 %collective-permute-start.6 = (bf16[64,3072]{1,0:T(8,128)(2,1)S(1)}, bf16[64,3072]{1,0:T(8,128)(2,1)S(1)}, u32[]{:S(2)}, u32[]{:S(2)}) collective-permute-start(bf16[64,3072]{1,0:T(8,128)(2,1)S(1)} %home.3.refs_1_), channel_id=1, source_target_pairs={{0,3},{1,0},{2,1},{3,2},{4,7},{5,4},{6,5},{7,6},{8,11},{9,8},{10,9... | collective-permute-start | bytes 1179656 | tf_op jit(solution)/shard_map/ppermute | solution.py:479
  128.5 12.5 %collective-permute-start.5 = (bf16[64,3072]{1,0:T(8,128)(2,1)S(1)}, bf16[64,3072]{1,0:T(8,128)(2,1)S(1)}, u32[]{:S(2)}, u32[]{:S(2)}) collective-permute-start(bf16[64,3072]{1,0:T(8,128)(2,1)S(1)} %home.3.refs_1_), channel_id=1, source_target_pairs={{0,1},{1,2},{2,3},{3,0},{4,5},{5,6},{6,7},{7,4},{8,9},{9,10},{10,1... | collective-permute-start | bytes 1179656 | tf_op jit(solution)/shard_map/ppermute | solution.py:479
  128.5 12.5 %collective-permute-start.4 = (bf16[64,3072]{1,0:T(8,128)(2,1)S(1)}, bf16[64,3072]{1,0:T(8,128)(2,1)S(1)}, u32[]{:S(2)}, u32[]{:S(2)}) collective-permute-start(bf16[64,3072]{1,0:T(8,128)(2,1)S(1)} %home.3.refs_1_), channel_id=1, source_target_pairs={{0,2},{1,3},{2,0},{3,1},{4,6},{5,7},{6,4},{7,5},{8,10},{9,11},{10,... | collective-permute-start | bytes 1179656 | tf_op jit(solution)/shard_map/ppermute | solution.py:479
  143.3 82.6 %copy-start.10 = (bf16[64,3072]{1,0:T(8,128)(2,1)}, bf16[64,3072]{1,0:T(8,128)(2,1)S(1)}, u32[]{:S(2)}) copy-start(bf16[64,3072]{1,0:T(8,128)(2,1)S(1)} %get-tuple-element.56.refs_0_) | copy-start | bytes 1179652
  190.5 22.2 %copy-start.5 = (bf16[16,24,3200]{2,1,0:T(8,128)(2,1)}, bf16[16,24,3200]{2,1,0:T(8,128)(2,1)S(1)}, u32[]{:S(2)}) copy-start(bf16[16,24,3200]{2,1,0:T(8,128)(2,1)S(1)} %get-tuple-element.59._) | copy-start | bytes 7372804
  213.3 6.8 %collective-permute-start.9 = (bf16[64,3072]{1,0:T(8,128)(2,1)S(1)}, bf16[64,3072]{1,0:T(8,128)(2,1)S(1)}, u32[]{:S(2)}, u32[]{:S(2)}) collective-permute-start(bf16[64,3072]{1,0:T(8,128)(2,1)S(1)} %home.4.refs_2_), channel_id=1, source_target_pairs={{0,3},{1,0},{2,1},{3,2},{4,7},{5,4},{6,5},{7,6},{8,11},{9,8},{10,9... | collective-permute-start | bytes 1179656 | tf_op jit(solution)/shard_map/ppermute | solution.py:479
  213.4 12.5 %collective-permute-start.8 = (bf16[64,3072]{1,0:T(8,128)(2,1)S(1)}, bf16[64,3072]{1,0:T(8,128)(2,1)S(1)}, u32[]{:S(2)}, u32[]{:S(2)}) collective-permute-start(bf16[64,3072]{1,0:T(8,128)(2,1)S(1)} %home.4.refs_2_), channel_id=1, source_target_pairs={{0,1},{1,2},{2,3},{3,0},{4,5},{5,6},{6,7},{7,4},{8,9},{9,10},{10,1... | collective-permute-start | bytes 1179656 | tf_op jit(solution)/shard_map/ppermute | solution.py:479
  214.8 11.1 %collective-permute-start.7 = (bf16[64,3072]{1,0:T(8,128)(2,1)S(1)}, bf16[64,3072]{1,0:T(8,128)(2,1)S(1)}, u32[]{:S(2)}, u32[]{:S(2)}) collective-permute-start(bf16[64,3072]{1,0:T(8,128)(2,1)S(1)} %home.4.refs_2_), channel_id=1, source_target_pairs={{0,2},{1,3},{2,0},{3,1},{4,6},{5,7},{6,4},{7,5},{8,10},{9,11},{10,... | collective-permute-start | bytes 1179656 | tf_op jit(solution)/shard_map/ppermute | solution.py:479
  227.5 26.5 %copy-start.7 = (bf16[64,3072]{1,0:T(8,128)(2,1)}, bf16[64,3072]{1,0:T(8,128)(2,1)S(1)}, u32[]{:S(2)}) copy-start(bf16[64,3072]{1,0:T(8,128)(2,1)S(1)} %get-tuple-element.62.refs_3_.refs_1_) | copy-start | bytes 1179652
  254.6 29.7 %all-to-all-start.7 = ((bf16[16,24,3200]{2,1,0:T(8,128)(2,1)}), bf16[16,24,3200]{2,1,0:T(8,128)(2,1)S(1)}, u32[]{:S(2)}, u32[]{:S(2)}) async-start(bf16[16,24,3200]{2,1,0:T(8,128)(2,1)} %in_turn.4), calls=%async_computation.7 | async-start | bytes 4915200 | tf_op jit(solution)/shard_map/all_to_all | solution.py:475
  286.5 29.2 %all-to-all-start.8 = ((bf16[16,24,3328]{2,1,0:T(8,128)(2,1)}), bf16[16,24,3328]{2,1,0:T(8,128)(2,1)}, u32[]{:S(2)}, u32[]{:S(2)}) async-start(bf16[16,24,3328]{2,1,0:T(8,128)(2,1)} %in_turn.5), calls=%async_computation.8 | async-start | bytes 5111808 | tf_op jit(solution)/shard_map/all_to_all | solution.py:475
  291.8 32.7 %copy-start.12 = (bf16[64,3072]{1,0:T(8,128)(2,1)S(1)}, bf16[64,3072]{1,0:T(8,128)(2,1)}, u32[]{:S(2)}) copy-start(bf16[64,3072]{1,0:T(8,128)(2,1)} %copy-done.10) | copy-start | bytes 1179652
  291.9 6.7 %collective-permute-start.12 = (bf16[64,3072]{1,0:T(8,128)(2,1)S(1)}, bf16[64,3072]{1,0:T(8,128)(2,1)S(1)}, u32[]{:S(2)}, u32[]{:S(2)}) collective-permute-start(bf16[64,3072]{1,0:T(8,128)(2,1)S(1)} %home.5), channel_id=1, source_target_pairs={{0,3},{1,0},{2,1},{3,2},{4,7},{5,4},{6,5},{7,6},{8,11},{9,8},{10,9... | collective-permute-start | bytes 1179656 | tf_op jit(solution)/shard_map/ppermute | solution.py:479
  293.0 8.2 %collective-permute-start.11 = (bf16[64,3072]{1,0:T(8,128)(2,1)S(1)}, bf16[64,3072]{1,0:T(8,128)(2,1)S(1)}, u32[]{:S(2)}, u32[]{:S(2)}) collective-permute-start(bf16[64,3072]{1,0:T(8,128)(2,1)S(1)} %home.5), channel_id=1, source_target_pairs={{0,1},{1,2},{2,3},{3,0},{4,5},{5,6},{6,7},{7,4},{8,9},{9,10},{10,1... | collective-permute-start | bytes 1179656 | tf_op jit(solution)/shard_map/ppermute | solution.py:479
  293.4 12.8 %collective-permute-start.10 = (bf16[64,3072]{1,0:T(8,128)(2,1)S(1)}, bf16[64,3072]{1,0:T(8,128)(2,1)S(1)}, u32[]{:S(2)}, u32[]{:S(2)}) collective-permute-start(bf16[64,3072]{1,0:T(8,128)(2,1)S(1)} %home.5), channel_id=1, source_target_pairs={{0,2},{1,3},{2,0},{3,1},{4,6},{5,7},{6,4},{7,5},{8,10},{9,11},{10,... | collective-permute-start | bytes 1179656 | tf_op jit(solution)/shard_map/ppermute | solution.py:479
  307.2 1.7 collective-permute-start.13
  318.2 4.8 %collective-permute-start.20 = (f32[24,128]{1,0:T(8,128)S(1)}, f32[24,128]{1,0:T(8,128)S(1)}, u32[]{:S(2)}, u32[]{:S(2)}) collective-permute-start(f32[24,128]{1,0:T(8,128)S(1)} %get-tuple-element.66), channel_id=1, source_target_pairs={{0,3},{1,0},{2,1},{3,2},{4,7},{5,4},{6,5},{7,6},{8,11},{9,8},{10,9... | collective-permute-start | bytes 36872 | tf_op jit(solution)/shard_map/ppermute | solution.py:479
  319.5 7.0 %collective-permute-start.19 = (f32[24,128]{1,0:T(8,128)S(1)}, f32[24,128]{1,0:T(8,128)S(1)}, u32[]{:S(2)}, u32[]{:S(2)}) collective-permute-start(f32[24,128]{1,0:T(8,128)S(1)} %get-tuple-element.66), channel_id=1, source_target_pairs={{0,1},{1,2},{2,3},{3,0},{4,5},{5,6},{6,7},{7,4},{8,9},{9,10},{10,1... | collective-permute-start | bytes 36872 | tf_op jit(solution)/shard_map/ppermute | solution.py:479
  319.8 6.7 %collective-permute-start.18 = (f32[24,128]{1,0:T(8,128)S(1)}, f32[24,128]{1,0:T(8,128)S(1)}, u32[]{:S(2)}, u32[]{:S(2)}) collective-permute-start(f32[24,128]{1,0:T(8,128)S(1)} %get-tuple-element.66), channel_id=1, source_target_pairs={{0,2},{1,3},{2,0},{3,1},{4,6},{5,7},{6,4},{7,5},{8,10},{9,11},{10,... | collective-permute-start | bytes 36872 | tf_op jit(solution)/shard_map/ppermute | solution.py:479
  321.6 12.6 %collective-permute-start.16 = (bf16[64,3072]{1,0:T(8,128)(2,1)S(1)}, bf16[64,3072]{1,0:T(8,128)(2,1)S(1)}, u32[]{:S(2)}, u32[]{:S(2)}) collective-permute-start(bf16[64,3072]{1,0:T(8,128)(2,1)S(1)} %get-tuple-element.65.refs_2_), channel_id=1, source_target_pairs={{0,3},{1,0},{2,1},{3,2},{4,7},{5,4},{6,5},{7,6},{8,11},{9,8},{10,9... | collective-permute-start | bytes 1179656 | tf_op jit(solution)/shard_map/ppermute | solution.py:479
  322.3 15.4 %collective-permute-start.15 = (bf16[64,3072]{1,0:T(8,128)(2,1)S(1)}, bf16[64,3072]{1,0:T(8,128)(2,1)S(1)}, u32[]{:S(2)}, u32[]{:S(2)}) collective-permute-start(bf16[64,3072]{1,0:T(8,128)(2,1)S(1)} %get-tuple-element.65.refs_2_), channel_id=1, source_target_pairs={{0,1},{1,2},{2,3},{3,0},{4,5},{5,6},{6,7},{7,4},{8,9},{9,10},{10,1... | collective-permute-start | bytes 1179656 | tf_op jit(solution)/shard_map/ppermute | solution.py:479
  323.1 14.6 %collective-permute-start.14 = (bf16[64,3072]{1,0:T(8,128)(2,1)S(1)}, bf16[64,3072]{1,0:T(8,128)(2,1)S(1)}, u32[]{:S(2)}, u32[]{:S(2)}) collective-permute-start(bf16[64,3072]{1,0:T(8,128)(2,1)S(1)} %get-tuple-element.65.refs_2_), channel_id=1, source_target_pairs={{0,2},{1,3},{2,0},{3,1},{4,6},{5,7},{6,4},{7,5},{8,10},{9,11},{10,... | collective-permute-start | bytes 1179656 | tf_op jit(solution)/shard_map/ppermute | solution.py:479
  338.4 2.4 collective-permute-start.17
  338.5 1.7 collective-permute-start.21
  (17 other events, 147.2 us)
